TPU v7x, 32 devices: a whole 2x2x4 slice. The times are simulated.
32 devices in a mesh: dp: 8 (over z, x), tensor: 4 (over y, core).
Axes of the slice: x: 2, y: 2, z: 4, core: 2. Of those that a mesh axis runs over, the one named last changes fastest.
Arguments:
- layer_input: bfloat16 [32768, 512], P(('dp', 'tensor')), may hold values from -6 to 6
- lengths: int32 [8, 32, 2], P('dp'), may hold values from 0 to 126, as said below
- ln1_gain: float32 [512], replicated, may hold values from 0.5 to 1.5
- ln1_bias: float32 [512], replicated, may hold values from -3 to 3
- w_query: bfloat16 [512, 512], P(None, 'tensor'), may hold values from -0.25 to 0.25
- b_query: bfloat16 [512], P('tensor'), may hold values from -3 to 3
- w_key: bfloat16 [512, 512], P(None, 'tensor'), may hold values from -0.25 to 0.25
- w_value: bfloat16 [512, 512], P(None, 'tensor'), may hold values from -0.25 to 0.25
- b_value: bfloat16 [512], P('tensor'), may hold values from -3 to 3
- w_out: bfloat16 [512, 512], P('tensor'), may hold values from -0.75 to 0.75
- b_out: bfloat16 [512], replicated, may hold values from -3 to 3
- ln2_gain: float32 [512], replicated, may hold values from 0.5 to 1.5
- ln2_bias: float32 [512], replicated, may hold values from -3 to 3
- w_up: bfloat16 [512, 2048], P(None, 'tensor'), may hold values from -0.25 to 0.25
- b_up: bfloat16 [2048], P('tensor'), may hold values from -3 to 3
- w_down: bfloat16 [2048, 512], P('tensor'), may hold values from -0.125 to 0.125
- b_down: bfloat16 [512], replicated, may hold values from -3 to 3
- cotangent: bfloat16 [32768, 512], P(('dp', 'tensor')), may hold values from -6 to 6
Outputs:
- block_output: bfloat16 [32768, 512], P(('dp', 'tensor'))
- input_grad: bfloat16 [32768, 512], P(('dp', 'tensor'))
- grad_ln1_gain: float32 [512], replicated
- grad_ln1_bias: float32 [512], replicated
- grad_w_query: float32 [512, 512], P(None, 'tensor')
- grad_b_query: float32 [512], P('tensor')
- grad_w_key: float32 [512, 512], P(None, 'tensor')
- grad_w_value: float32 [512, 512], P(None, 'tensor')
- grad_b_value: float32 [512], P('tensor')
- grad_w_out: float32 [512, 512], P('tensor')
- grad_b_out: float32 [512], replicated
- grad_ln2_gain: float32 [512], replicated
- grad_ln2_bias: float32 [512], replicated
- grad_w_up: float32 [512, 2048], P(None, 'tensor')
- grad_b_up: float32 [2048], P('tensor')
- grad_w_down: float32 [2048, 512], P('tensor')
- grad_b_down: float32 [512], replicated
Inputs may be any that keep to these rules, and one draw needn't show every extreme that they name: `lengths`: in each group the occupied slots come first, between 28 and 31 of them; the other slots hold 0 in both entries. In a group of 126-token sequences each occupied slot holds (126, 0); in a group of 48-token sequences each occupied slot holds (48, 48). Some group holds 126-token sequences and some other group 48-token ones.
All inputs are finite; a program needn't handle non-finite values.
Results may differ from a plain program's by a relative error of at most 0.018.
Values may be sent and summed in bfloat16 or wider, within the bound.
No kernel may reach another device: no remote copies, remote signals or barrier semaphores. Data moves between devices by JAX's collectives and lax.ppermute only.
A program may use at most 128 MiB of HBM per device.

v0:
```python
import math

import jax
import jax.numpy as jnp
from jax import lax
from jax.sharding import PartitionSpec as P

HD = 64
SLOT = 128
FRAME = 6


norm_eps = 1e-05


def layer_norm(values, gain, bias):
    row_mean = jnp.mean(values, -1, keepdims=True)
    centred = values - row_mean
    variance = jnp.mean(centred * centred, -1, keepdims=True)
    return centred * lax.rsqrt(variance + norm_eps) * gain + bias


def matmul(left, right):
    return jnp.dot(left, right, preferred_element_type=jnp.float32)


def matmul_tn(left, right):
    return lax.dot_general(
        left, right, (((0,), (0,)), ((), ())), preferred_element_type=jnp.float32
    )


def matmul_nt(left, right):
    return lax.dot_general(
        left, right, (((1,), (1,)), ((), ())), preferred_element_type=jnp.float32
    )


def column_sum(values):
    return jnp.sum(values.astype(jnp.float32), 0)


def gelu_exact(values):
    return jax.nn.gelu(values, approximate=False)


def keep_grads(*grads):
    return grads


def slot_masks(slot_lengths):
    places = jnp.arange(SLOT, dtype=jnp.int32)
    half_slot = SLOT // 2
    first_len = slot_lengths[:, 0:1]
    second_len = slot_lengths[:, 1:2]
    in_second = (second_len > 0) & (places[None, :] >= half_slot)
    local_pos = places[None, :] - jnp.where(in_second, half_slot, 0).astype(jnp.int32)
    is_valid = jnp.where(in_second, local_pos < second_len, places[None, :] < first_len)
    frames = local_pos // FRAME
    causal = frames[:, None, :] <= frames[:, :, None]
    same_seq = in_second[:, :, None] == in_second[:, None, :]
    allowed = is_valid[:, None, :] & is_valid[:, :, None] & causal & same_seq
    return (allowed[:, None], is_valid[:, None, :, None])


def attend_block(inputs):
    queries, key_rows, values, slot_lengths = inputs
    score_scale = HD ** (-0.5)
    scores = (
        jnp.einsum("bqhd,bkhd->bhqk", queries, key_rows, preferred_element_type=jnp.float32)
        * score_scale
    )
    allowed, valid_query = slot_masks(slot_lengths)
    row_top = jnp.max(jnp.where(allowed, scores, -1e30), -1, keepdims=True)
    row_top = jnp.where(valid_query, row_top, 0.0)
    expo_terms = jnp.where(allowed, jnp.exp(scores - row_top), 0.0)
    denom_sum = jnp.sum(expo_terms, -1, keepdims=True) + jnp.where(valid_query, 0.0, 1.0)
    softmax_w = (expo_terms / denom_sum).astype(jnp.bfloat16)
    attended = jnp.einsum("bhqk,bkhd->bqhd", softmax_w, values, preferred_element_type=jnp.float32)
    return (attended.astype(jnp.bfloat16), row_top + jnp.log(denom_sum))


def attend_back(inputs):
    queries, key_rows, values, slot_lengths, log_norm, grad_attended = inputs
    score_scale = HD ** (-0.5)
    scores = (
        jnp.einsum("bqhd,bkhd->bhqk", queries, key_rows, preferred_element_type=jnp.float32)
        * score_scale
    )
    allowed, valid_query = slot_masks(slot_lengths)
    softmax_w = jnp.where(allowed, jnp.exp(scores - log_norm), 0.0)
    grad_softmax = jnp.einsum(
        "bqhd,bkhd->bhqk", grad_attended, values, preferred_element_type=jnp.float32
    )
    centre_term = jnp.sum(softmax_w * grad_softmax, -1, keepdims=True)
    grad_scores = (softmax_w * (grad_softmax - centre_term)).astype(jnp.bfloat16)
    grad_queries = (
        jnp.einsum("bhqk,bkhd->bqhd", grad_scores, key_rows, preferred_element_type=jnp.float32)
        * score_scale
    )
    grad_keys = (
        jnp.einsum("bhqk,bqhd->bkhd", grad_scores, queries, preferred_element_type=jnp.float32)
        * score_scale
    )
    grad_values = jnp.einsum(
        "bhqk,bqhd->bkhd",
        softmax_w.astype(jnp.bfloat16),
        grad_attended,
        preferred_element_type=jnp.float32,
    )
    return (
        grad_queries.astype(jnp.bfloat16),
        grad_keys.astype(jnp.bfloat16),
        grad_values.astype(jnp.bfloat16),
    )


def run_layer(rows_in, slot_lengths, param_set, grad_out, movers, hooks):
    (
        ln1_gain,
        ln1_bias,
        w_query,
        b_query,
        w_key,
        w_value,
        b_value,
        w_out,
        b_out,
        ln2_gain,
        ln2_bias,
        w_up,
        b_up,
        w_down,
        b_down,
    ) = param_set
    (
        gather_attn,
        sum_attn,
        gather_mlp,
        sum_mlp,
        gather_grad_mlp,
        sum_grad_mlp,
        gather_grad_attn,
        sum_grad_attn,
    ) = movers
    hook_mlp, hook_attn = hooks
    slot_count = slot_lengths.shape[0]
    per_block = math.gcd(slot_count, 4)
    head_count = w_query.shape[1] // HD
    block_shape = (slot_count // per_block, per_block, SLOT, head_count, HD)
    length_blocks = slot_lengths.reshape(slot_count // per_block, per_block, 2)
    normed_one, norm_one_back = jax.vjp(layer_norm, rows_in, ln1_gain, ln1_bias)
    normed_all = gather_attn(normed_one.astype(jnp.bfloat16))
    all_rows = normed_all.shape[0]
    query_blocks = (matmul(normed_all, w_query) + b_query).astype(jnp.bfloat16).reshape(block_shape)
    key_blocks = matmul(normed_all, w_key).astype(jnp.bfloat16).reshape(block_shape)
    value_blocks = (matmul(normed_all, w_value) + b_value).astype(jnp.bfloat16).reshape(block_shape)
    attended, log_norm = lax.map(
        attend_block, (query_blocks, key_blocks, value_blocks, length_blocks)
    )
    attended = attended.reshape(all_rows, head_count * HD)
    hidden_in = rows_in + (sum_attn(matmul(attended, w_out)) + b_out)
    normed_two, norm_two_back = jax.vjp(layer_norm, hidden_in, ln2_gain, ln2_bias)
    normed_both = gather_mlp(normed_two.astype(jnp.bfloat16))
    up_rows = matmul(normed_both, w_up) + b_up
    activated, gelu_back = jax.vjp(gelu_exact, up_rows)
    act_low = activated.astype(jnp.bfloat16)
    block_out = hidden_in + (sum_mlp(matmul(act_low, w_down)) + b_down)
    grad_rows_all = gather_grad_mlp(grad_out)
    grad_w_down = matmul_tn(act_low, grad_rows_all)
    grad_up = gelu_back(matmul_nt(grad_rows_all, w_down))[0].astype(jnp.bfloat16)
    grad_w_up = matmul_tn(normed_both, grad_up)
    grad_b_up = column_sum(grad_up)
    grad_w_up, grad_b_up, grad_w_down = hook_mlp(grad_w_up, grad_b_up, grad_w_down)
    grad_normed_two = sum_grad_mlp(matmul_nt(grad_up, w_up))
    grad_hidden_ln, grad_ln2_gain, grad_ln2_bias = norm_two_back(grad_normed_two)
    grad_hidden = grad_out.astype(jnp.float32) + grad_hidden_ln
    grad_b_down = column_sum(grad_out)
    grad_attn_low = grad_hidden.astype(jnp.bfloat16)
    grad_b_out = column_sum(grad_attn_low)
    grad_attn_all = gather_grad_attn(grad_attn_low)
    grad_w_out = matmul_tn(attended, grad_attn_all)
    grad_attended = matmul_nt(grad_attn_all, w_out).astype(jnp.bfloat16)
    grad_queries, grad_keys, grad_values = lax.map(
        attend_back,
        (
            query_blocks,
            key_blocks,
            value_blocks,
            length_blocks,
            log_norm,
            grad_attended.reshape(block_shape),
        ),
    )
    grad_queries = grad_queries.reshape(all_rows, head_count * HD)
    grad_keys = grad_keys.reshape(all_rows, head_count * HD)
    grad_values = grad_values.reshape(all_rows, head_count * HD)
    grad_w_query = matmul_tn(normed_all, grad_queries)
    grad_b_query = column_sum(grad_queries)
    grad_w_key = matmul_tn(normed_all, grad_keys)
    grad_w_value = matmul_tn(normed_all, grad_values)
    grad_b_value = column_sum(grad_values)
    attn_grads = hook_attn(
        grad_w_query, grad_b_query, grad_w_key, grad_w_value, grad_b_value, grad_w_out
    )
    grad_normed_one = sum_grad_attn(
        matmul_nt(grad_queries, w_query)
        + matmul_nt(grad_keys, w_key)
        + matmul_nt(grad_values, w_value)
    )
    grad_rows_ln, grad_ln1_gain, grad_ln1_bias = norm_one_back(grad_normed_one)
    grad_in = (grad_hidden + grad_rows_ln).astype(jnp.bfloat16)
    shared = (grad_ln1_gain, grad_ln1_bias, grad_b_out, grad_ln2_gain, grad_ln2_bias, grad_b_down)
    return (
        block_out.astype(jnp.bfloat16),
        grad_in,
        (grad_w_up, grad_b_up, grad_w_down),
        attn_grads,
        shared,
    )


def per_device(
    layer_input,
    lengths,
    ln1_gain,
    ln1_bias,
    w_query,
    b_query,
    w_key,
    w_value,
    b_value,
    w_out,
    b_out,
    ln2_gain,
    ln2_bias,
    w_up,
    b_up,
    w_down,
    b_down,
    cotangent,
):
    rows_in = layer_input.astype(jnp.float32)
    slot_lengths = lengths.reshape(-1, 2)

    def gather_attn(rows_low):
        return lax.all_gather(rows_low, "tensor", axis=0, tiled=True)

    def sum_attn(partial_rows):
        return lax.psum_scatter(
            partial_rows.astype(jnp.bfloat16), "tensor", scatter_dimension=0, tiled=True
        ).astype(jnp.float32)

    def gather_mlp(rows_low):
        return lax.all_gather(rows_low, "tensor", axis=0, tiled=True)

    def sum_mlp(partial_rows):
        return lax.psum_scatter(
            partial_rows.astype(jnp.bfloat16), "tensor", scatter_dimension=0, tiled=True
        ).astype(jnp.float32)

    def gather_grad_mlp(rows_low):
        return lax.all_gather(rows_low, "tensor", axis=0, tiled=True)

    def sum_grad_mlp(partial_rows):
        return lax.psum_scatter(
            partial_rows.astype(jnp.bfloat16), "tensor", scatter_dimension=0, tiled=True
        ).astype(jnp.float32)

    def gather_grad_attn(rows_low):
        return lax.all_gather(rows_low, "tensor", axis=0, tiled=True)

    def sum_grad_attn(partial_rows):
        return lax.psum_scatter(
            partial_rows.astype(jnp.bfloat16), "tensor", scatter_dimension=0, tiled=True
        ).astype(jnp.float32)

    movers = (
        gather_attn,
        sum_attn,
        gather_mlp,
        sum_mlp,
        gather_grad_mlp,
        sum_grad_mlp,
        gather_grad_attn,
        sum_grad_attn,
    )
    param_set = (
        ln1_gain,
        ln1_bias,
        w_query,
        b_query,
        w_key,
        w_value,
        b_value,
        w_out,
        b_out,
        ln2_gain,
        ln2_bias,
        w_up,
        b_up,
        w_down,
        b_down,
    )
    block_out, grad_in, mlp_grads, attn_grads, shared = run_layer(
        rows_in, slot_lengths, param_set, cotangent, movers, (keep_grads, keep_grads)
    )
    grad_w_up, grad_b_up, grad_w_down = mlp_grads
    grad_w_query, grad_b_query, grad_w_key, grad_w_value, grad_b_value, grad_w_out = attn_grads
    (
        grad_w_up,
        grad_b_up,
        grad_w_down,
        grad_w_query,
        grad_b_query,
        grad_w_key,
        grad_w_value,
        grad_b_value,
        grad_w_out,
    ) = lax.psum(
        (
            grad_w_up,
            grad_b_up,
            grad_w_down,
            grad_w_query,
            grad_b_query,
            grad_w_key,
            grad_w_value,
            grad_b_value,
            grad_w_out,
        ),
        "dp",
    )
    grad_ln1_gain, grad_ln1_bias, grad_b_out, grad_ln2_gain, grad_ln2_bias, grad_b_down = shared
    grad_ln1_gain, grad_ln1_bias, grad_b_out, grad_ln2_gain, grad_ln2_bias, grad_b_down = lax.psum(
        (grad_ln1_gain, grad_ln1_bias, grad_b_out, grad_ln2_gain, grad_ln2_bias, grad_b_down),
        ("dp", "tensor"),
    )
    return (
        block_out,
        grad_in,
        grad_ln1_gain,
        grad_ln1_bias,
        grad_w_query,
        grad_b_query,
        grad_w_key,
        grad_w_value,
        grad_b_value,
        grad_w_out,
        grad_b_out,
        grad_ln2_gain,
        grad_ln2_bias,
        grad_w_up,
        grad_b_up,
        grad_w_down,
        grad_b_down,
    )


def solution(mesh):
    return jax.shard_map(
        per_device,
        mesh=mesh,
        in_specs=(
            P(("dp", "tensor"), None),
            P("dp", None, None),
            P(),
            P(),
            P(None, "tensor"),
            P("tensor"),
            P(None, "tensor"),
            P(None, "tensor"),
            P("tensor"),
            P("tensor", None),
            P(),
            P(),
            P(),
            P(None, "tensor"),
            P("tensor"),
            P("tensor", None),
            P(),
            P(("dp", "tensor"), None),
        ),
        out_specs=(
            P(("dp", "tensor"), None),
            P(("dp", "tensor"), None),
            P(),
            P(),
            P(None, "tensor"),
            P("tensor"),
            P(None, "tensor"),
            P(None, "tensor"),
            P("tensor"),
            P("tensor", None),
            P(),
            P(),
            P(),
            P(None, "tensor"),
            P("tensor"),
            P("tensor", None),
            P(),
        ),
        check_vma=False,
    )
```

profile of v0, /device:TPU:0, one launch (start us, length us, event | category | flops | bytes accessed | tf_op | source)
XLA Modules:
  0.0 695.8 jit_solution(15430279360527942443)
XLA Ops:
  13.5 37.1 %all-gather.5.cloned.1.call-done = bf16[4096,512]{1,0:T(8,128)(2,1)} async-done(((bf16[1024,512]{1,0:T(8,128)(2,1)}), bf16[4096,512]{1,0:T(8,128)(2,1)}) %all-gather.5.cloned.1.call-update) | async-done | bytes 4194320 | tf_op jit(solution)/shard_map/all_gather | solution.py:247
  50.6 3.4 fusion.60
  55.9 5.8 copy.55
  67.1 4.6 copy.57
  77.0 5.8 copy.58
  84.0 30.1 %while.30 = (s32[]{:T(128)}, bf16[8,4,128,2,64]{2,1,0,4,3:T(4,128)(2,1)}, f32[8,4,2,128,1]{3,2,1,4,0:T(2,128)S(1)}, bf16[8,4,128,2,64]{2,4,3,1,0:T(8,128)(2,1)},...) while((s32[]{:T(128)}, ...), condition=%wide.region_5.6_spmd, body=%wide.region_2.5_spmd.sunk | while | flops 35270276 | bytes 2686997 | solution.py:158
  121.3 44.0 %reduce-scatter.5.cloned.1.call-done = bf16[1024,512]{1,0:T(8,128)(2,1)} async-done(((bf16[4096,512]{1,0:T(8,128)(2,1)}), bf16[1024,512]{1,0:T(8,128)(2,1)}) %reduce-scatter.5.cloned.1.call-update) | async-done | bytes 1048592 | tf_op jit(solution)/shard_map/reduce_scatter | solution.py:250
  171.4 33.8 %all-gather.7.cloned.1.call-done = bf16[4096,512]{1,0:T(8,128)(2,1)} async-done(((bf16[1024,512]{1,0:T(8,128)(2,1)}), bf16[4096,512]{1,0:T(8,128)(2,1)}) %all-gather.7.cloned.1.call-update) | async-done | bytes 4194320 | tf_op jit(solution)/shard_map/all_gather | solution.py:255
  205.2 7.8 %fusion.87 = f32[4096,512]{1,0:T(8,128)} fusion(bf16[4096,512]{1,0:T(8,128)(2,1)} %all-gather.7.cloned.1.call-done, bf16[512,512]{1,0:T(8,128)(2,1)S(1)} %copy-done.27), kind=kOutput, calls=%fused_computation.175 | convolution fusion | flops 2147483648 | bytes 13107200 | tf_op jit(solution)/shard_map/dot_general | solution.py:24
  213.0 28.3 %all-gather.9.cloned.1.call-done = bf16[4096,512]{1,0:T(8,128)(2,1)} async-done(((bf16[1024,512]{1,0:T(8,128)(2,1)}), bf16[4096,512]{1,0:T(8,128)(2,1)}) %all-gather.9.cloned.1.call-update) | async-done | bytes 4194320 | tf_op jit(solution)/shard_map/all_gather | solution.py:263
  241.2 24.7 %convert_reduce_fusion = (f32[512]{0:T(512)S(1)}, bf16[4096,512]{1,0:T(8,128)(2,1)S(1)}, f32[4096,512]{1,0:T(8,128)}) fusion(f32[4096,512]{1,0:T(8,128)} %fusion.87, f32[512]{0:T(512)S(1)} %convert_element_type.158, bf16[4096,512]{1,0:T(8,128)(2,1)} %all-gather.9.cloned.1.call-done, bf16[512,512]{1,0:T(8,128)(2,1)S(1)} %copy-done), kind=kOutput, calls=%fused_computation.99 | convolution fusion | flops 2304769536 | bytes 25694208 | tf_op jit(solution)/shard_map/dot_general | solution.py:34
  267.8 4.6 convolution_convert_fusion.3
  272.8 8.6 %multiply_convert_fusion.1 = bf16[4096,512]{1,0:T(8,128)(2,1)S(1)} fusion(f32[4096,512]{1,0:T(8,128)} %get-tuple-element.338, f32[4096,512]{1,0:T(8,128)} %fusion.87, f32[512]{0:T(512)S(1)} %convert_element_type.158), kind=kLoop, calls=%fused_computation.102 | loop fusion | flops 8388608 | bytes 20973568 | tf_op jit(solution)/shard_map/convert_element_type | solution.py:167
  283.3 4.3 convolution_convert_fusion.4
  288.3 28.8 %reduce-scatter.9.cloned.1.call-done = bf16[1024,512]{1,0:T(8,128)(2,1)} async-done(((bf16[4096,512]{1,0:T(8,128)(2,1)}), bf16[1024,512]{1,0:T(8,128)(2,1)}) %reduce-scatter.9.cloned.1.call-update) | async-done | bytes 1048592 | tf_op jit(solution)/shard_map/reduce_scatter | solution.py:266
  319.5 44.6 %reduce-scatter.7.cloned.1.call-done = bf16[1024,512]{1,0:T(8,128)(2,1)} async-done(((bf16[4096,512]{1,0:T(8,128)(2,1)}), bf16[1024,512]{1,0:T(8,128)(2,1)}) %reduce-scatter.7.cloned.1.call-update) | async-done | bytes 1048592 | tf_op jit(solution)/shard_map/reduce_scatter | solution.py:258
  364.1 3.5 fusion.86
  370.8 34.1 %all-gather.11.cloned.1.call-done = bf16[4096,512]{1,0:T(8,128)(2,1)} async-done(((bf16[1024,512]{1,0:T(8,128)(2,1)}), bf16[4096,512]{1,0:T(8,128)(2,1)}) %all-gather.11.cloned.1.call-update) | async-done | bytes 4194320 | tf_op jit(solution)/shard_map/all_gather | solution.py:271
  410.2 4.6 copy.64
  416.0 61.5 %while.31 = (s32[]{:T(128)}, bf16[8,4,128,2,64]{2,4,3,1,0:T(8,128)(2,1)}, bf16[8,4,128,2,64]{2,1,0,4,3:T(4,128)(2,1)}, bf16[8,4,128,2,64]{2,4,3,1,0:T(8,128)(2,1...) while((s32[]{:T(128)}, ...), condition=%wide.region_15.16_spmd, body=%wide.region_13.15_spmd.sunk | while | flops 85728384 | bytes 5668909 | solution.py:184
  496.8 6.9 fusion.94
  518.2 22.0 %all-reduce.1 = (f32[128]{0:T(128)}, f32[128]{0:T(128)}, f32[512]{0:T(512)}) all-reduce(f32[128]{0:T(128)S(1)} %reduce_sum.226, f32[128]{0:T(128)S(1)} %reduce_sum.228, f32[512]{0:T(512)S(1)} %get-tuple-element.336), channel_id=1, replica_groups=mesh['dp'=8,'tensor'=4] {'dp'}, use_global_device_ids=true, to_apply=%region_25.26 | all-reduce | flops 768 | bytes 6144 | tf_op jit(solution)/shard_map/psum | solution.py:320
  548.0 42.8 %all-reduce = (f32[512]{0:T(512)}, f32[512]{0:T(512)}, f32[512]{0:T(512)}, f32[512]{0:T(512)}, f32[512]{0:T(512)}, /*index=5*/f32[512]{0:T(512)}) all-reduce(f32[512]{0:T(512)S(1)} %get-tuple-element.277, f32[512]{0:T(512)S(1)} %get-tuple-element.280, ...), channel_id=1, replica_groups=mesh['dp'=8,'tensor'=4] {'dp','tensor'}, use_global_device_ids=true, to_apply=%region_20.21 | all-reduce | flops 3072 | bytes 24576 | tf_op jit(solution)/shard_map/psum | solution.py:335
  590.8 88.3 %all-reduce.5.cloned.1.call-done = (f32[512,128]{1,0:T(8,128)}, f32[512,128]{1,0:T(8,128)}, f32[512,128]{1,0:T(8,128)}, f32[128,512]{1,0:T(8,128)}, f32[512,512]{1,0:T(8,128)}, /*index=5*/f32[512,512]{1,0:T(8,128)}) async-done(((f32[512,128]{1,0:T(8,128)}, f32[512,128]{1,0:T(8,128)}, f32[512,128]{1,0:T(8,128)}, f32[128,512]{1,0:T(8,128)}, f32[512,512]{1,0:T(8,128)}, /*index=5*/f32[512,512]{1,0:T(8,128)}), ...) | async-done | bytes 3145744 | tf_op jit(solution)/shard_map/psum | solution.py:320
  (399 shorter events, 191.9 us)
Async XLA Ops:
  7.2 234.0 %copy-start = (bf16[512,512]{1,0:T(8,128)(2,1)S(1)}, bf16[512,512]{1,0:T(8,128)(2,1)}, u32[]{:S(2)}) copy-start(bf16[512,512]{1,0:T(8,128)(2,1)} %param.37) | copy-start | bytes 1572868
  7.2 43.3 %copy-start.26 = (bf16[512,128]{1,0:T(8,128)(2,1)S(1)}, bf16[512,128]{1,0:T(8,128)(2,1)}, u32[]{:S(2)}) copy-start(bf16[512,128]{1,0:T(8,128)(2,1)} %param.29) | copy-start | bytes 393220
  7.2 43.3 %all-gather.5.cloned.1.call-start = ((), (), s32[]{:S(2)}) async-start(), calls=%async_computation.4 | async-start | bytes 5242880 | tf_op jit(solution)/shard_map/all_gather | solution.py:247
  13.2 152.0 %reduce-scatter.5.cloned.1.call-start = ((), (), s32[]{:S(2)}) async-start(), calls=%async_computation.5 | async-start | bytes 5242880 | tf_op jit(solution)/shard_map/reduce_scatter | solution.py:250
  54.0 7.7 %copy-start.24 = (bf16[512,128]{1,0:T(8,128)(2,1)S(1)}, bf16[512,128]{1,0:T(8,128)(2,1)}, u32[]{:S(2)}) copy-start(bf16[512,128]{1,0:T(8,128)(2,1)} %param.26) | copy-start | bytes 393220
  84.0 33.3 %copy-start.23 = (bf16[128,512]{1,0:T(8,128)(2,1)S(1)}, bf16[128,512]{1,0:T(8,128)(2,1)}, u32[]{:S(2)}) copy-start(bf16[128,512]{1,0:T(8,128)(2,1)} %param.31) | copy-start | bytes 393220
  120.6 44.7 %copy-start.2 = (bf16[1024,512]{1,0:T(8,128)(2,1)S(1)}, bf16[1024,512]{1,0:T(8,128)(2,1)}, u32[]{:S(2)}) copy-start(bf16[1024,512]{1,0:T(8,128)(2,1)} %param.22) | copy-start | bytes 3145732
  120.6 48.4 %copy-start.35 = (f32[512]{0:T(512)S(1)}, f32[512]{0:T(512)}, u32[]{:S(2)}) copy-start(f32[512]{0:T(512)} %param.33) | copy-start | bytes 6148
  120.6 48.4 %copy-start.36 = (f32[512]{0:T(512)S(1)}, f32[512]{0:T(512)}, u32[]{:S(2)}) copy-start(f32[512]{0:T(512)} %param.34) | copy-start | bytes 6148
  120.6 84.6 %all-gather.7.cloned.1.call-start = ((), (), s32[]{:S(2)}) async-start(), calls=%async_computation.6 | async-start | bytes 5242880 | tf_op jit(solution)/shard_map/all_gather | solution.py:255
  167.0 38.2 %copy-start.27 = (bf16[512,512]{1,0:T(8,128)(2,1)S(1)}, bf16[512,512]{1,0:T(8,128)(2,1)}, u32[]{:S(2)}) copy-start(bf16[512,512]{1,0:T(8,128)(2,1)} %param.35) | copy-start | bytes 1572868
  170.6 70.6 %all-gather.9.cloned.1.call-start = ((), (), s32[]{:S(2)}) async-start(), calls=%async_computation.8 | async-start | bytes 5242880 | tf_op jit(solution)/shard_map/all_gather | solution.py:263
  171.1 146.0 %reduce-scatter.9.cloned.1.call-start = ((), (), s32[]{:S(2)}) async-start(), calls=%async_computation.9 | async-start | bytes 5242880 | tf_op jit(solution)/shard_map/reduce_scatter | solution.py:266
  272.5 91.6 %reduce-scatter.7.cloned.1.call-start = ((), (), s32[]{:S(2)}) async-start(), calls=%async_computation.7 | async-start | bytes 5242880 | tf_op jit(solution)/shard_map/reduce_scatter | solution.py:258
  287.6 29.5 %copy-start.6 = (bf16[1024,512]{1,0:T(8,128)(2,1)S(1)}, bf16[1024,512]{1,0:T(8,128)(2,1)}, u32[]{:S(2)}) copy-start(bf16[1024,512]{1,0:T(8,128)(2,1)} %reduce-scatter.5.cloned.1.call-done) | copy-start | bytes 3145732
  287.6 117.3 %all-gather.11.cloned.1.call-start = ((), (), s32[]{:S(2)}) async-start(), calls=%async_computation.10 | async-start | bytes 5242880 | tf_op jit(solution)/shard_map/all_gather | solution.py:271
  370.3 170.9 %reduce-scatter.11.cloned.1.call-start = ((), (), s32[]{:S(2)}) async-start(), calls=%async_computation.11 | async-start | bytes 5242880 | tf_op jit(solution)/shard_map/reduce_scatter | solution.py:274
  496.5 182.5 %all-reduce.5.cloned.1.call-start = ((), (), s32[]{:S(2)}) async-start(), calls=%async_computation.12 | async-start | bytes 6291456 | tf_op jit(solution)/shard_map/psum | solution.py:320
  514.0 27.3 %copy-start.29 = (f32[1024]{0:T(1024)S(1)}, f32[1024]{0:T(1024)}, u32[]{:S(2)}) copy-start(f32[1024]{0:T(1024)} %copy-done.28) | copy-start | bytes 12292
  514.0 27.3 %copy-start.34 = (f32[512]{0:T(512)S(1)}, f32[512]{0:T(512)}, u32[]{:S(2)}) copy-start(f32[512]{0:T(512)} %param.24) | copy-start | bytes 6148
  516.0 27.5 %copy-start.33 = (f32[1024]{0:T(1024)S(1)}, f32[1024]{0:T(1024)}, u32[]{:S(2)}) copy-start(f32[1024]{0:T(1024)} %copy-done.32) | copy-start | bytes 12292
  516.0 27.5 %copy-start.31 = (f32[1024]{0:T(1024)S(1)}, f32[1024]{0:T(1024)}, u32[]{:S(2)}) copy-start(f32[1024]{0:T(1024)} %copy-done.30) | copy-start | bytes 12292
  516.0 30.0 %copy-start.17 = (bf16[1024,512]{1,0:T(8,128)(2,1)S(1)}, bf16[1024,512]{1,0:T(8,128)(2,1)}, u32[]{:S(2)}) copy-start(bf16[1024,512]{1,0:T(8,128)(2,1)} %param.39) | copy-start | bytes 3145732
  679.1 9.0 %copy-start.22 = (f32[512,512]{1,0:T(8,128)S(1)}, f32[512,512]{1,0:T(8,128)}, u32[]{:S(2)}) copy-start(f32[512,512]{1,0:T(8,128)} %get-tuple-element.558) | copy-start | bytes 3145732
  (28 other events, 105.9 us)
Sparse Core Ops, SparseCore 0:
  13.4 37.1 all-gather.4
  120.7 44.4 reduce-scatter.4
  170.7 34.4 all-gather.6
  206.7 34.4 all-gather.8
  272.6 44.5 reduce-scatter.8
  319.5 44.5 reduce-scatter.6
  370.4 34.4 all-gather.10
  496.7 44.5 reduce-scatter.10
  546.6 132.3 all-reduce.4
where the time goes:
time: 706 us; the launch traced here: 696 us
  waiting for transfers between devices  341 us (48%)
  matrix products  152 us (22%)
  local copies, waits for them, and re-layouts  77.9 us (11%)
  blocking collectives  64.8 us (9%)
  other arithmetic  43.5 us (6%)
  between operations  14.6 us (2%)
    psum x1, waiting for transfers between devices, per_device(): lax.psum((grad_w_up, grad_b_up, grad_w_down, grad_w_query, grad_b_query,...  88.3 us
    reduce_scatter x1, waiting for transfers between devices, sum_mlp(): lax.psum_scatter(partial_rows.astype(jnp.bfloat16), 'tensor', scatter_dim...  44.6 us
    reduce_scatter x1, waiting for transfers between devices, sum_attn(): lax.psum_scatter(partial_rows.astype(jnp.bfloat16), 'tensor', scatter_dim...  44 us
    psum x1, blocking collectives, per_device(): lax.psum((grad_ln1_gain, grad_ln1_bias, grad_b_out, grad_ln2_gain, grad_l...  42.8 us
    dot_general x6, matrix products, matmul_nt(): lax.dot_general(left, right, (((1,), (1,)), ((), ())), preferred_element_...  38.6 us
    all_gather x1, waiting for transfers between devices, gather_attn(): return lax.all_gather(rows_low, 'tensor', axis=0, tiled=True)  37.1 us
    all_gather x1, waiting for transfers between devices, gather_grad_attn(): return lax.all_gather(rows_low, 'tensor', axis=0, tiled=True)  34.1 us
    all_gather x1, waiting for transfers between devices, gather_mlp(): return lax.all_gather(rows_low, 'tensor', axis=0, tiled=True)  33.8 us
  transfers between devices with their start and end apart: 9, of which 9 were waited for; matrix products, arithmetic and copies ran while one was open for 7% of the time, Pallas kernels for 0%

commit v1 on v0

v1 whole, which is shorter than its diff:
```python
import functools

import jax
import jax.numpy as jnp
from jax import lax
from jax.experimental import pallas as pl
from jax.experimental.pallas import tpu as pltpu
from jax.sharding import PartitionSpec as P

BF, F32 = jnp.bfloat16, jnp.float32
D = 512
HD = 64
SLOT = 128
BR = 256
BIAS = 16
EPS = 1e-5
SLOT_UNROLL = 2
SMEM = functools.partial(pl.BlockSpec, memory_space=pltpu.SMEM)
VMEM = functools.partial(pl.BlockSpec, memory_space=pltpu.VMEM)


def dot(a, b):
    return lax.dot_general(a, b, (((1,), (0,)), ((), ())), preferred_element_type=F32)


def dot_nt(a, b):
    return lax.dot_general(a, b, (((1,), (1,)), ((), ())), preferred_element_type=F32)


def params(mib, **kw):
    return pltpu.CompilerParams(vmem_limit_bytes=mib << 20, **kw)


def cost(flops, nbytes, trans=0):
    return pl.CostEstimate(flops=int(flops), bytes_accessed=int(nbytes), transcendentals=int(trans))


def sds(shape, dtype=BF):
    return jax.ShapeDtypeStruct(shape, dtype)


def whole(shape):
    return pl.BlockSpec(shape, lambda *i: (0,) * len(shape))


def normalise(v):
    mean = jnp.mean(v, -1, keepdims=True)
    centred = v - mean
    rstd = lax.rsqrt(jnp.mean(centred * centred, -1, keepdims=True) + EPS)
    return centred * rstd, rstd


def head_stack(v):
    first = lax.broadcasted_iota(jnp.int32, v.shape, 1) < HD
    zero = jnp.zeros_like(v)
    return jnp.concatenate([jnp.where(first, v, zero), jnp.where(first, zero, v)], 0)


def untranspose(v):
    return jnp.concatenate([v[:, :SLOT].T, v[:, SLOT:].T], 1)


def slot_bias(len1, len2):
    def places(shape, dim):
        p = lax.broadcasted_iota(jnp.int32, shape, dim) & (SLOT - 1)
        second = (p >= SLOT // 2) & (len2 > 0)
        local = jnp.where(second, p - SLOT // 2, p)
        valid = local < jnp.where(second, len2, len1)
        base = jnp.where(second, 1000, 0)
        return valid, base, base + ((local * 43) >> 8)

    valid_k, _, frame_k = places((SLOT, 1), 0)
    valid_q, base_q, frame_q = places((1, 2 * SLOT), 1)
    frame_k = jnp.where(valid_k, frame_k, 1 << 20)
    frame_q = jnp.where(valid_q, frame_q, -1)
    allowed = (frame_k <= frame_q) & (frame_k >= base_q)
    return jnp.where(allowed, 0.0, -1e30).astype(F32)


def pack_kernel(wq, wk, wv, wo, bq, bv, bup, out):
    for i, ref in enumerate((wq, wk, wv)):
        out[0:D, i * 128 : (i + 1) * 128] = ref[...]
    for b in range(4):
        out[b * 128 : (b + 1) * 128, 384:512] = wo[:, b * 128 : (b + 1) * 128]
    zero = jnp.zeros((1, 128), F32)
    first = jnp.concatenate([bq[...].astype(F32), zero, bv[...].astype(F32), zero], 1)
    row = lax.broadcasted_iota(jnp.int32, (BIAS, D), 0)
    block = jnp.where(row == 0, first, jnp.where(row == 1, bup[...].astype(F32), 0.0))
    out[D : D + BIAS, :] = block.astype(BF)


def prep_kernel(x, gain, bias, bout, cot, n1_o, n1t_o, cott_o, base_o):
    def tile(m, _):
        here = pl.ds(pl.multiple_of(m * BR, BR), BR)
        xf = x[here, :].astype(F32)
        xhat, _ = normalise(xf)
        n1 = (xhat * gain[...] + bias[...]).astype(BF)
        n1_o[here, :] = n1
        n1t_o[:, here] = n1.T
        cott_o[:, here] = cot[here, :].T
        base_o[here, :] = xf + bout[...].astype(F32)
        return 0

    lax.fori_loop(0, x.shape[0] // BR, tile, 0)


def attn_fwd_kernel(last, *refs):
    if last:
        (scal, lens, n1, base, wa, wb, gain, bias, q_o, k_o, v_o, att_o, pt_o, hid_o, n2_o, n2t_o) = refs
    else:
        (scal, lens, n1, base, wa, wb, q_o, k_o, v_o, att_o, pt_o, hid_o) = refs
    slots = n1.shape[0] // SLOT

    for c, w in enumerate((wa, wb)):
        brow = w[D : D + BIAS, :].astype(F32)[0:1]
        cols = slice(c * 128, (c + 1) * 128)
        qkv = dot(n1[...], w[0:D, 0:384])
        q_o[:, cols] = (qkv[:, 0:128] + brow[:, 0:128]).astype(BF) * jnp.asarray(0.125, BF)
        k_o[:, cols] = qkv[:, 128:256].astype(BF)
        v_o[:, cols] = (qkv[:, 256:384] + brow[:, 256:384]).astype(BF)

    def slot(s, _):
        rows = pl.ds(pl.multiple_of(s * SLOT, SLOT), SLOT)
        place = scal[3] + s
        mask = slot_bias(lens[2 * place], lens[2 * place + 1])
        for c in range(2):
            cols = slice(c * 128, (c + 1) * 128)
            st = dot_nt(k_o[rows, cols], head_stack(q_o[rows, cols])) + mask
            top = jnp.maximum(jnp.max(st, 0, keepdims=True), -1e29)
            e = jnp.exp(st - top)
            den = jnp.sum(e, 0, keepdims=True)
            pt = (e * (1.0 / jnp.where(den == 0.0, 1.0, den))).astype(BF)
            pt_o[rows, c * 256 : (c + 1) * 256] = pt
            att_o[rows, cols] = dot(untranspose(pt), head_stack(v_o[rows, cols])).astype(BF)
        return 0

    lax.fori_loop(0, slots, slot, 0, unroll=SLOT_UNROLL)
    hid = base[...]
    for c, w in enumerate((wa, wb)):
        wo = jnp.concatenate([w[b * 128 : (b + 1) * 128, 384:512] for b in range(4)], 1)
        hid += dot(att_o[:, c * 128 : (c + 1) * 128], wo)
    hid_o[...] = hid
    if last:

        def tile(m, _):
            here = pl.ds(pl.multiple_of(m * BR, BR), BR)
            xhat, _ = normalise(hid_o[here, :])
            n2 = (xhat * gain[...] + bias[...]).astype(BF)
            n2_o[here, :] = n2
            n2t_o[:, here] = n2.T
            return 0

        lax.fori_loop(0, n1.shape[0] // BR, tile, 0)


def gelu_pair(u):
    phi = 0.5 + 0.5 * lax.erf(u * 0.7071067811865476)
    return u * phi, phi + u * (jnp.exp(-0.5 * (u * u)) * 0.3989422804014327)


def mlp_kernel(first, *refs):
    if first:
        (n2, n2t, cot, cott, ba, bb, ua, ub, da, db, gua, gub, gda, gdb, out, dn2, act_s, gup_s) = refs
    else:
        (n2, n2t, cot, cott, ba, bb, ua, ub, da, db, out_i, dn2_i, gua, gub, gda, gdb, out, dn2, act_s, gup_s) = refs
    bias = [b[D : D + BIAS, :].astype(F32)[1:2] for b in (ba, bb)]

    def tile(m, sums):
        here = pl.ds(pl.multiple_of(m * BR, BR), BR)
        n, c = n2[here, :], cot[here, :]
        new, acts, gups = [], [], []
        for j, (u, d) in enumerate(((ua, da), (ub, db))):
            up = dot(n, u[...]) + bias[j]
            dact = dot_nt(c, d[...])
            act, slope = gelu_pair(up)
            gup = (slope * dact).astype(BF)
            act = act.astype(BF)
            act_s[here, j * D : (j + 1) * D] = act
            gup_s[here, j * D : (j + 1) * D] = gup
            new.append(sums[j] + jnp.sum(gup.astype(F32), 0, keepdims=True))
            acts.append(act)
            gups.append(gup)
        o = dot(acts[0], da[...]) + dot(acts[1], db[...])
        e = dot_nt(gups[0], ua[...]) + dot_nt(gups[1], ub[...])
        out[here, :] = o if first else out_i[here, :] + o
        dn2[here, :] = e if first else dn2_i[here, :] + e
        return tuple(new)

    zero = jnp.zeros((1, D), F32)
    sums = lax.fori_loop(0, n2.shape[0] // BR, tile, (zero, zero), unroll=True)
    row = lax.broadcasted_iota(jnp.int32, (BIAS, D), 0)
    for j, (gu_o, gd_o) in enumerate(((gua, gda), (gub, gdb))):
        cols = slice(j * D, (j + 1) * D)
        gu_o[0:D, :] = dot(n2t[...], gup_s[:, cols]).astype(BF)
        gd_o[0:D, :] = dot(cott[...], act_s[:, cols]).astype(BF)
        high = sums[j].astype(BF).astype(F32)
        gu_o[D : D + BIAS, :] = jnp.where(row == 0, high, jnp.where(row == 8, sums[j] - high, 0.0)).astype(BF)


def attn_bwd_kernel(*refs):
    (x, hid, mlp, dn2, cot, g1, g2, bdown) = refs[:8]
    (q0, k0, v0, att0, pt0, q1, k1, v1, att1, pt1) = refs[8:18]
    w = refs[18:22]
    n1t = refs[22]
    block_o, gin_o = refs[23:25]
    ga = refs[25:29]
    (dq_s, dk_s, dv_s, dh_s, gat_s, gatt_s, datt_s) = refs[29:]
    rows_all = x.shape[0]

    def total(sums, *adds):
        return sums + jnp.concatenate([jnp.sum(a, 0, keepdims=True) for a in adds], 0)

    def ln2_back(m, sums):
        here = pl.ds(pl.multiple_of(m * BR, BR), BR)
        hidden = hid[here, :]
        block_o[here, :] = (hidden + mlp[here, :] + bdown[...].astype(F32)).astype(BF)
        xhat2, rstd2 = normalise(hidden)
        dn = dn2[here, :]
        e = dn * g2[...]
        cotf = cot[here, :].astype(F32)
        dh = cotf + rstd2 * (e - jnp.mean(e, -1, keepdims=True) - xhat2 * jnp.mean(e * xhat2, -1, keepdims=True))
        dh_s[here, :] = dh
        gat = dh.astype(BF)
        gat_s[here, :] = gat
        gatt_s[:, here] = gat.T
        return total(sums, gat.astype(F32), dn * xhat2, dn, cotf)

    sums2 = lax.fori_loop(0, rows_all // BR, ln2_back, jnp.zeros((4, D), F32))
    for c in range(4):
        wo = jnp.concatenate([w[c][b * 128 : (b + 1) * 128, 384:512] for b in range(4)], 1)
        datt_s[:, c * 128 : (c + 1) * 128] = dot_nt(gat_s[...], wo).astype(BF)

    def slot(s, _):
        rows = pl.ds(pl.multiple_of(s * SLOT, SLOT), SLOT)
        for c in range(4):
            q, k, v, pt_r = ((q0, k0, v0, pt0), (q1, k1, v1, pt1))[c // 2]
            cols = slice((c % 2) * 128, (c % 2 + 1) * 128)
            out = slice(c * 128, (c + 1) * 128)
            qs = head_stack(q[rows, cols])
            ks = head_stack(k[rows, cols])
            das = head_stack(datt_s[rows, out])
            pt = pt_r[rows, (c % 2) * 256 : (c % 2 + 1) * 256]
            dpt = dot_nt(v[rows, cols], das)
            ptf = pt.astype(F32)
            delta = jnp.sum(ptf * dpt, 0, keepdims=True)
            ds = (ptf * (dpt - delta)).astype(BF)
            dv_s[rows, out] = dot(pt, das).astype(BF)
            dk_s[rows, out] = dot(ds, qs).astype(BF)
            dq_s[rows, out] = (dot(untranspose(ds), ks) * 0.125).astype(BF)
        return 0

    lax.fori_loop(0, rows_all // SLOT, slot, 0, unroll=SLOT_UNROLL)

    def ln1_back(m, sums):
        here = pl.ds(pl.multiple_of(m * BR, BR), BR)
        dn1 = None
        for c in range(4):
            cols = slice(c * 128, (c + 1) * 128)
            grads = jnp.concatenate([dq_s[here, cols], dk_s[here, cols], dv_s[here, cols]], 1)
            part = dot_nt(grads, w[c][0:D, 0:384])
            dn1 = part if dn1 is None else dn1 + part
        xhat1, rstd1 = normalise(x[here, :].astype(F32))
        e = dn1 * g1[...]
        back = rstd1 * (e - jnp.mean(e, -1, keepdims=True) - xhat1 * jnp.mean(e * xhat1, -1, keepdims=True))
        gin_o[here, :] = (dh_s[here, :] + back).astype(BF)
        return total(sums, dn1 * xhat1, dn1, dq_s[here, :].astype(F32), dv_s[here, :].astype(F32))

    sums1 = lax.fori_loop(0, rows_all // BR, ln1_back, jnp.zeros((4, D), F32), unroll=True)
    zero = jnp.zeros((1, 128), F32)
    for j, s in enumerate((dq_s, dk_s, dv_s)):
        g = dot(n1t[...], s[...]).astype(BF)
        for c in range(4):
            ga[c][0:D, j * 128 : (j + 1) * 128] = g[:, c * 128 : (c + 1) * 128]
    go = [dot(gatt_s[...], a[...]).astype(BF) for a in (att0, att1)]
    for c in range(4):
        cols = slice(c * 128, (c + 1) * 128)
        ga[c][0:D, 384:512] = go[c // 2][:, (c % 2) * 128 : (c % 2 + 1) * 128]
        own = jnp.concatenate([sums1[2:3, cols], zero, sums1[3:4, cols], zero], 1)
        block = jnp.concatenate([own, sums1[0:2], sums2, jnp.zeros((1, D), F32)], 0)
        high = block.astype(BF)
        ga[c][D : D + 8, :] = high
        ga[c][D + 8 : D + 16, :] = (block - high.astype(F32)).astype(BF)


def bias_sum(refs, n):
    total = None
    for r in refs:
        v = r[n : n + BIAS, :].astype(F32)
        v = v[0:8] + v[8:16]
        total = v if total is None else total + v
    return total


def bias_block(total):
    high = total.astype(BF)
    return jnp.concatenate([high, (total - high.astype(F32)).astype(BF)], 0)


def combine_kernel(n_in, split, biased, last, *refs):
    scal = refs[0]
    ins, outs = refs[1 : 1 + n_in], refs[1 + n_in :]
    n = ins[0].shape[0] - (BIAS if biased else 0)

    def summed(rows):
        total = ins[0][rows, :].astype(F32)
        for r in ins[1:]:
            total += r[rows, :].astype(F32)
        return total.astype(BF)

    if split is None:
        outs[0][0:n, :] = summed(slice(0, n))
    else:
        bit = scal[split]
        h = n // 2
        outs[0][0:h, :] = summed(pl.ds(pl.multiple_of((1 - bit) * h, h), h))
        outs[1][0:h, :] = summed(pl.ds(pl.multiple_of(bit * h, h), h))
    if biased:
        total = bias_sum(ins, n)
        if last:
            outs[-1][...] = total
        else:
            block = bias_block(total)
            for o in outs:
                o[o.shape[0] - BIAS :, :] = block


def combine(scal, ins, split=None, biased=False, last=False):
    n = ins[0].shape[0] - (BIAS if biased else 0)
    extra = BIAS if biased and not last else 0
    if split is None:
        shapes = [sds((n + extra, D))]
    else:
        shapes = [sds((n // 2 + extra, D))] * 2
    if biased and last:
        shapes.append(sds((8, D), F32))
    return pl.pallas_call(
        functools.partial(combine_kernel, len(ins), split, biased, last),
        out_shape=shapes,
        in_specs=[SMEM()] + [VMEM()] * len(ins),
        out_specs=[VMEM()] * len(shapes),
        compiler_params=params(16),
        cost_estimate=cost(n * D * len(ins), 2 * n * D * (len(ins) + 1)),
        name="combine",
    )(scal, *ins)


def join_kernel(bit_at, scal, mine, other, out):
    bit = scal[bit_at]
    h = mine.shape[0]
    out[pl.ds(pl.multiple_of(bit * h, h), h), :] = mine[...]
    out[pl.ds(pl.multiple_of((1 - bit) * h, h), h), :] = other[...]


def join(scal, mine, other, bit_at):
    h = mine.shape[0]
    return pl.pallas_call(
        functools.partial(join_kernel, bit_at),
        out_shape=sds((2 * h, D)),
        in_specs=[SMEM(), VMEM(), VMEM()],
        out_specs=VMEM(),
        compiler_params=params(16),
        cost_estimate=cost(h, 8 * h * D),
        name="join",
    )(scal, mine, other)


def final_kernel(kind, bit_at, scal, mine, other, *outs):
    bit = scal[bit_at]
    h = mine.shape[0]
    for place, ref in ((bit, mine), (1 - bit, other)):
        at = pl.ds(pl.multiple_of(place * h, h), h)
        v = ref[...].astype(F32)
        if kind == "up":
            outs[0][at, :] = v
        elif kind == "down":
            outs[0][:, at] = v.T
        else:
            for j in range(3):
                outs[j][at, :] = v[:, j * 128 : (j + 1) * 128]
            outs[3][:, at] = v[:, 384:512].T


def final(scal, kind, mine, other, bit_at):
    if kind == "attn":
        shapes = [sds((D, 128), F32)] * 3 + [sds((128, D), F32)]
    else:
        shapes = [sds((D, D), F32)]
    return pl.pallas_call(
        functools.partial(final_kernel, kind, bit_at),
        out_shape=shapes,
        in_specs=[SMEM(), VMEM(), VMEM()],
        out_specs=[VMEM()] * len(shapes),
        compiler_params=params(16),
        cost_estimate=cost(D * D, 6 * D * D),
        name="final_" + kind,
    )(scal, mine, other)


def layer(
    n_dp, n_t, x, lengths, ln1_gain, ln1_bias, w_query, b_query, w_key, w_value, b_value, w_out, b_out,
    ln2_gain, ln2_bias, w_up, b_up, w_down, b_down, cot,
):
    rows = x.shape[0]
    dp_at, t_at = lax.axis_index("dp"), lax.axis_index("tensor")
    slots = rows // SLOT
    scal = jnp.stack([dp_at & 1, (dp_at >> 1) & 1, t_at, t_at * slots]).astype(jnp.int32)
    lens = lengths.reshape(-1)

    def swap(v, dp_mask=0, t_mask=0):
        pairs = [(d * n_t + t, (d ^ dp_mask) * n_t + (t ^ t_mask)) for d in range(n_dp) for t in range(n_t)]
        return lax.ppermute(v, ("dp", "tensor"), pairs)

    row = lambda v: v.reshape(1, -1)
    wa = [None] * 4
    wa[0] = pl.pallas_call(
        pack_kernel, out_shape=sds((D + BIAS, D)), in_specs=[VMEM()] * 7, out_specs=VMEM(),
        compiler_params=params(16), cost_estimate=cost(D, 4 * D * D), name="pack",
    )(w_query, w_key, w_value, w_out, row(b_query), row(b_value), row(b_up))
    wu, wd = [w_up, None, None, None], [w_down, None, None, None]
    wa[2] = swap(wa[0], t_mask=2)
    wa[1] = swap(wa[0], t_mask=1)
    wu[1] = swap(wu[0], t_mask=1)
    wd[1] = swap(wd[0], t_mask=1)
    wu[2] = swap(wu[0], t_mask=2)
    wd[2] = swap(wd[0], t_mask=2)
    wa[3] = swap(wa[2], t_mask=1)
    wu[3] = swap(wu[2], t_mask=1)
    wd[3] = swap(wd[2], t_mask=1)

    def call(kernel, name, out_shape, args, scratch=(), mib=16, flops=1e9, nbytes=1e7):
        return pl.pallas_call(
            kernel,
            out_shape=out_shape,
            in_specs=[SMEM() if a.dtype == jnp.int32 else VMEM() for a in args],
            out_specs=[VMEM()] * len(out_shape),
            scratch_shapes=list(scratch),
            compiler_params=params(mib),
            cost_estimate=cost(flops, nbytes),
            name=name,
        )(*args)

    wide, tall = sds((rows, D)), sds((D, rows))
    acc = sds((rows, D), F32)
    n1, n1t, cott, base = call(
        prep_kernel, "prep", [wide, tall, tall, acc], [x, row(ln1_gain), row(ln1_bias), row(b_out), cot]
    )
    saved = [sds((rows, 256))] * 4 + [sds((rows, 512)), acc]
    q0, k0, v0, att0, pt0, base = call(
        functools.partial(attn_fwd_kernel, False), "attn_fwd_own", saved, [scal, lens, n1, base, wa[0], wa[1]]
    )
    q1, k1, v1, att1, pt1, hid, n2, n2t = call(
        functools.partial(attn_fwd_kernel, True), "attn_fwd_other", saved + [wide, tall],
        [scal, lens, n1, base, wa[2], wa[3], row(ln2_gain), row(ln2_bias)],
    )

    def mlp(ia, ib, sums):
        return call(
            functools.partial(mlp_kernel, not sums), "mlp_other" if sums else "mlp_own",
            [sds((D + BIAS, D))] * 2 + [sds((D, D))] * 2 + [acc] * 2,
            [n2, n2t, cot, cott, wa[ia], wa[ib], wu[ia], wu[ib], wd[ia], wd[ib], *sums],
            [pltpu.VMEM((rows, 2 * D), BF)] * 2,
        )

    gu, gd, ga = [None] * 4, [None] * 4, [None] * 4
    gu[1], gu[0], gd[1], gd[0], out_a, dn2_a = mlp(1, 0, ())
    gu[3], gu[2], gd[3], gd[2], out_sum, dn2 = mlp(3, 2, (out_a, dn2_a))
    half = pltpu.VMEM((rows, D), BF)
    block_out, grad_in, *ga = call(
        attn_bwd_kernel, "attn_bwd", [wide] * 2 + [sds((D + BIAS, D))] * 4,
        [x, hid, out_sum, dn2, cot, row(ln1_gain), row(ln2_gain), row(b_down),
         q0, k0, v0, att0, pt0, q1, k1, v1, att1, pt1, *wa, n1t],
        [half] * 3 + [pltpu.VMEM((rows, D), F32), half, pltpu.VMEM((D, rows), BF), half],
        mib=24,
    )

    def reduce(g, kind, biased):
        got1, got3 = swap(g[1], t_mask=1), swap(g[3], t_mask=1)
        (for_y,) = combine(scal, [g[2], got3], biased=biased)
        from_y = swap(for_y, t_mask=2)
        send, keep = combine(scal, [g[0], got1, from_y], split=0, biased=biased)
        got = swap(send, dp_mask=1)
        send, keep = combine(scal, [keep, got], split=1, biased=biased)
        got = swap(send, dp_mask=2)
        parts, bit = [keep, got], 4
        while bit < n_dp:
            (total,) = combine(scal, parts, biased=biased)
            parts, bit = [total, swap(total, dp_mask=bit)], 2 * bit
        total, *sums = combine(scal, parts, biased=biased, last=True)
        quarter = join(scal, total, swap(total, dp_mask=2), 1)
        other = swap(quarter, dp_mask=1)
        return final(scal, kind, quarter, other, 0), sums

    (grad_w_down,), _ = reduce(gd, "down", False)
    (grad_w_up,), (sums_up,) = reduce(gu, "up", True)
    (gwq, gwk, gwv, gwo), (sums,) = reduce(ga, "attn", True)
    return (
        block_out, grad_in, sums[1], sums[2], gwq, sums[0, 0:128], gwk, gwv, sums[0, 256:384], gwo, sums[3],
        sums[4], sums[5], grad_w_up, sums_up[0], grad_w_down, sums[6],
    )


def solution(mesh):
    n_dp, n_t = mesh.shape["dp"], mesh.shape["tensor"]
    rows, cols, split, copied = P(("dp", "tensor"), None), P(None, "tensor"), P("tensor"), P()
    down = P("tensor", None)
    return jax.shard_map(
        functools.partial(layer, n_dp, n_t),
        mesh=mesh,
        in_specs=(
            rows, P("dp", None, None), copied, copied, cols, split, cols, cols, split, down, copied, copied, copied,
            cols, split, down, copied, rows,
        ),
        out_specs=(
            rows, rows, copied, copied, cols, split, cols, cols, split, down, copied, copied, copied, cols, split, down,
            copied,
        ),
        check_vma=False,
    )
```

time: 706 us -> 194 us (0.27); the launches traced: 696 us -> 194 us
  waiting for transfers between devices: 341 us -> 84.2 us
  matrix products: 152 us -> 0 us
  blocking collectives: 64.8 us -> 0 us
  local copies, waits for them, and re-layouts: 77.9 us -> 13.4 us
  Pallas kernels: 0 us -> 63.2 us
  other arithmetic: 43.5 us -> 0.08 us
  starting transfers between devices: 1.47 us -> 32 us
  between operations: 14.6 us -> 1.05 us
    dot_general x74 -> x0, matrix products: 152 us -> none  [the longest x6 38.6 us: matmul_nt(): lax.dot_general(left, right, (((1,), (1,)), ((), ())), preferred_element_...]
    all_gather x4 -> x0, waiting for transfers between devices: 133 us -> none  [the longest x1 37.1 us: gather_attn(): return lax.all_gather(rows_low, 'tensor', axis=0, tiled=True)]
    reduce_scatter x4 -> x0, waiting for transfers between devices: 118 us -> none  [the longest x1 44.6 us: sum_mlp(): lax.psum_scatter(partial_rows.astype(jnp.bfloat16), 'tensor', scatter_dim...]
    psum x1 -> x0, waiting for transfers between devices: 88.3 us -> none  [per_device(): lax.psum((grad_w_up, grad_b_up, grad_w_down, grad_w_query, grad_b_query,...]
    ppermute x0 -> x33, waiting for transfers between devices: none -> 84.2 us  [swap(): return lax.ppermute(v, ('dp', 'tensor'), pairs)]
    psum x2 -> x0, blocking collectives: 64.8 us -> none  [the longest x1 42.8 us: per_device(): lax.psum((grad_ln1_gain, grad_ln1_bias, grad_b_out, grad_ln2_gain, grad_l...]
    pallas_call x0 -> x28, Pallas kernels: none -> 63.2 us  [the longest x6 47 us: call(): pl.pallas_call(kernel, out_shape=out_shape, in_specs=[SMEM() if a.dtype =...]
    ppermute x0 -> x33, starting transfers between devices: none -> 32 us  [swap(): return lax.ppermute(v, ('dp', 'tensor'), pairs)]
  transfers between devices with their start and end apart: 9 -> 33, of which waited for: 9 -> 14; matrix products, arithmetic and copies ran while one was open for 7% -> 2% of each run, Pallas kernels for 0% -> 27%
where the time goes in v1:
time: 194 us
  waiting for transfers between devices  84.2 us (43%)
  Pallas kernels  63.2 us (33%)
  starting transfers between devices  32 us (16%)
  local copies, waits for them, and re-layouts  13.4 us (7%)
    ppermute x33, waiting for transfers between devices, swap(): return lax.ppermute(v, ('dp', 'tensor'), pairs)  84.2 us
    pallas_call x6, Pallas kernels, call(): pl.pallas_call(kernel, out_shape=out_shape, in_specs=[SMEM() if a.dtype =...  47 us
    ppermute x33, starting transfers between devices, swap(): return lax.ppermute(v, ('dp', 'tensor'), pairs)  32 us
    pallas_call x15, Pallas kernels, combine(): pl.pallas_call(functools.partial(combine_kernel, len(ins), split, biased,...  9.54 us
    unnamed x35, local copies, waits for them, and re-layouts  9.53 us
    pallas_call x3, Pallas kernels, final(): pl.pallas_call(functools.partial(final_kernel, kind, bit_at), out_shape=s...  4.87 us
  transfers between devices with their start and end apart: 33, of which 14 were waited for; matrix products, arithmetic and copies ran while one was open for 2% of the time, Pallas kernels for 27%

profile of v1, /device:TPU:0, one launch (start us, length us, event | category | flops | bytes accessed | tf_op | source)
XLA Modules:
  0.0 194.0 jit_solution(12640319025534234362)
XLA Ops:
  6.4 3.0 %collective-permute-start.1 = (bf16[528,512]{1,0:T(8,128)(2,1)S(1)}, bf16[528,512]{1,0:T(8,128)(2,1)S(1)}, u32[]{:S(2)}, u32[]{:S(2)}) collective-permute-start(bf16[528,512]{1,0:T(8,128)(2,1)S(1)} %pack.1.refs_4_.refs_5_.refs_18_), channel_id=1, source_target_pairs={{0,2},{1,3},{2,0},{3,1},{4,6},{5,7},{6,4},{7,5},{8,10},{9,11},{10,... | collective-permute-start | bytes 1622024 | tf_op jit(solution)/shard_map/ppermute | solution.py:411
  9.5 1.9 %collective-permute-start.5 = (bf16[512,512]{1,0:T(8,128)(2,1)}, bf16[512,512]{1,0:T(8,128)(2,1)}, u32[]{:S(2)}, u32[]{:S(2)}) collective-permute-start(bf16[512,512]{1,0:T(8,128)(2,1)} %refs_9_.1), channel_id=1, source_target_pairs={{0,2},{1,3},{2,0},{3,1},{4,6},{5,7},{6,4},{7,5},{8,10},{9,11},{10,... | collective-permute-start | bytes 1572872 | tf_op jit(solution)/shard_map/ppermute | solution.py:411
  11.4 11.1 %collective-permute-done.1.refs_4_.refs_5_.refs_20_ = bf16[528,512]{1,0:T(8,128)(2,1)S(1)} collective-permute-done((bf16[528,512]{1,0:T(8,128)(2,1)S(1)}, bf16[528,512]{1,0:T(8,128)(2,1)S(1)}, u32[]{:S(2)}, u32[]{:S(2)}) %collective-permute-start.1) | collective-permute-done | bytes 540704 | tf_op jit(solution)/shard_map/ppermute | solution.py:411
  23.0 10.8 %collective-permute-done.3.refs_7_ = bf16[512,512]{1,0:T(8,128)(2,1)} collective-permute-done((bf16[512,512]{1,0:T(8,128)(2,1)}, bf16[512,512]{1,0:T(8,128)(2,1)}, u32[]{:S(2)}, u32[]{:S(2)}) %collective-permute-start.3) | collective-permute-done | bytes 524320 | tf_op jit(solution)/shard_map/ppermute | solution.py:411
  33.8 10.4 %collective-permute-done.5.refs_9_ = bf16[512,512]{1,0:T(8,128)(2,1)} collective-permute-done((bf16[512,512]{1,0:T(8,128)(2,1)}, bf16[512,512]{1,0:T(8,128)(2,1)}, u32[]{:S(2)}, u32[]{:S(2)}) %collective-permute-start.5) | collective-permute-done | bytes 524320 | tf_op jit(solution)/shard_map/ppermute | solution.py:411
  52.5 5.7 %attn_fwd_own.1 = (bf16[1024,256]{1,0:T(8,128)(2,1)S(1)}, bf16[1024,256]{1,0:T(8,128)(2,1)S(1)}, bf16[1024,256]{1,0:T(8,128)(2,1)S(1)}, bf16[1024,256]{1,0:T(8,1...) custom-call(s32[4]{0:T(128)S(1)} %pad_add_fusion.refs_0_.scal, s32[64]{0:T(128)S(1)} %reshape.66.refs_1_, ...), custom_call_target="tpu_custom_call" | custom-call | flops 1000000000 | bytes 10000000 | tf_op jit(solution)/shard_map/attn_fwd_own/pallas_call | solution.py:431
  58.3 7.2 %attn_fwd_other.1 = (bf16[1024,256]{1,0:T(8,128)(2,1)S(1)}, bf16[1024,256]{1,0:T(8,128)(2,1)S(1)}, bf16[1024,256]{1,0:T(8,128)(2,1)S(1)}, bf16[1024,256]{1,0:T(8...) custom-call(s32[4]{0:T(128)S(1)} %pad_add_fusion.refs_0_.scal, ...), custom_call_target="tpu_custom_call" | custom-call | flops 1000000000 | bytes 10000000 | tf_op jit(solution)/shard_map/attn_fwd_other/pallas_call | solution.py:431
  65.6 7.4 %mlp_own.1 = (bf16[528,512]{1,0:T(8,128)(2,1)S(1)}, bf16[528,512]{1,0:T(8,128)(2,1)S(1)}, bf16[512,512]{1,0:T(8,128)(2,1)S(1)}, bf16[512,512]{1,0:T(8,128)(2,1)S...) custom-call(bf16[1024,512]{1,0:T(8,128)(2,1)S(1)} %get-tuple-element.77.refs_0_, ...), custom_call_target="tpu_custom_call" | custom-call | flops 1000000000 | bytes 10000000 | tf_op jit(solution)/shard_map/mlp_own/pallas_call | solution.py:431
  73.1 9.0 %mlp_other.1 = (bf16[528,512]{1,0:T(8,128)(2,1)S(1)}, bf16[528,512]{1,0:T(8,128)(2,1)S(1)}, bf16[512,512]{1,0:T(8,128)(2,1)S(1)}, bf16[512,512]{1,0:T(8,128)(2,1...) custom-call(bf16[1024,512]{1,0:T(8,128)(2,1)S(1)} %get-tuple-element.77.refs_0_, ...), custom_call_target="tpu_custom_call" | custom-call | flops 1000000000 | bytes 10000000 | tf_op jit(solution)/shard_map/mlp_other/pallas_call | solution.py:431
  82.2 16.1 %attn_bwd.1 = (bf16[1024,512]{1,0:T(8,128)(2,1)}, bf16[1024,512]{1,0:T(8,128)(2,1)}, bf16[528,512]{1,0:T(8,128)(2,1)S(1)}, bf16[528,512]{1,0:T(8,128)(2,1)S(1)},...) custom-call(bf16[1024,512]{1,0:T(8,128)(2,1)S(1)} %copy-done.3, f32[1024,512]{1,0:T(8,128)S(1)} %get-tuple-element.76.refs_1_, ...), custom_call_target="tpu_custom_call" | custom-call | flops 1000000000 | bytes 10000000 | tf_op jit(solution)/shard_map/attn_bwd/pallas_call | solution.py:431
  99.7 1.8 collective-permute-start.19
  105.3 9.6 %collective-permute-done.19.refs_3_ = bf16[528,512]{1,0:T(8,128)(2,1)S(1)} collective-permute-done((bf16[528,512]{1,0:T(8,128)(2,1)S(1)}, bf16[528,512]{1,0:T(8,128)(2,1)S(1)}, u32[]{:S(2)}, u32[]{:S(2)}) %collective-permute-start.19) | collective-permute-done | bytes 540704 | tf_op jit(solution)/shard_map/ppermute | solution.py:411
  115.7 1.8 collective-permute-start.20
  117.4 9.1 %collective-permute-done.11.refs_3_ = bf16[528,512]{1,0:T(8,128)(2,1)S(1)} collective-permute-done((bf16[528,512]{1,0:T(8,128)(2,1)S(1)}, bf16[528,512]{1,0:T(8,128)(2,1)S(1)}, u32[]{:S(2)}, u32[]{:S(2)}) %collective-permute-start.11) | collective-permute-done | bytes 540704 | tf_op jit(solution)/shard_map/ppermute | solution.py:411
  127.3 1.8 collective-permute-start.12
  129.0 8.0 %collective-permute-done.27.refs_3_ = bf16[512,512]{1,0:T(8,128)(2,1)S(1)} collective-permute-done((bf16[512,512]{1,0:T(8,128)(2,1)S(1)}, bf16[512,512]{1,0:T(8,128)(2,1)S(1)}, u32[]{:S(2)}, u32[]{:S(2)}) %collective-permute-start.27) | collective-permute-done | bytes 524320 | tf_op jit(solution)/shard_map/ppermute | solution.py:411
  143.0 2.5 %collective-permute-done.28.refs_2_ = bf16[256,512]{1,0:T(8,128)(2,1)S(1)} collective-permute-done((bf16[256,512]{1,0:T(8,128)(2,1)S(1)}, bf16[256,512]{1,0:T(8,128)(2,1)S(1)}, u32[]{:S(2)}, u32[]{:S(2)}) %collective-permute-start.28) | collective-permute-done | bytes 262176 | tf_op jit(solution)/shard_map/ppermute | solution.py:411
  146.2 1.9 collective-permute-start.29
  148.6 2.6 %collective-permute-start.22 = (bf16[144,512]{1,0:T(8,128)(2,1)S(1)}, bf16[144,512]{1,0:T(8,128)(2,1)S(1)}, u32[]{:S(2)}, u32[]{:S(2)}) collective-permute-start(bf16[144,512]{1,0:T(8,128)(2,1)S(1)} %combine.23.refs_1_), channel_id=1, source_target_pairs={{0,16},{1,17},{2,18},{3,19},{4,20},{5,21},{6,22},{7,23},{8,24},{9,... | collective-permute-start | bytes 442376 | tf_op jit(solution)/shard_map/ppermute | solution.py:411
  153.6 2.6 %collective-permute-start.30 = (bf16[128,512]{1,0:T(8,128)(2,1)S(1)}, bf16[128,512]{1,0:T(8,128)(2,1)S(1)}, u32[]{:S(2)}, u32[]{:S(2)}) collective-permute-start(bf16[128,512]{1,0:T(8,128)(2,1)S(1)} %combine.28.refs_1_), channel_id=1, source_target_pairs={{0,16},{1,17},{2,18},{3,19},{4,20},{5,21},{6,22},{7,23},{8,24},{9,... | collective-permute-start | bytes 393224 | tf_op jit(solution)/shard_map/ppermute | solution.py:411
  156.1 13.1 %collective-permute-done.30.refs_2_ = bf16[128,512]{1,0:T(8,128)(2,1)S(1)} collective-permute-done((bf16[128,512]{1,0:T(8,128)(2,1)S(1)}, bf16[128,512]{1,0:T(8,128)(2,1)S(1)}, u32[]{:S(2)}, u32[]{:S(2)}) %collective-permute-start.30) | collective-permute-done | bytes 131104 | tf_op jit(solution)/shard_map/ppermute | solution.py:411
  170.5 2.1 %collective-permute-start.23 = (bf16[128,512]{1,0:T(8,128)(2,1)S(1)}, bf16[128,512]{1,0:T(8,128)(2,1)S(1)}, u32[]{:S(2)}, u32[]{:S(2)}) collective-permute-start(bf16[128,512]{1,0:T(8,128)(2,1)S(1)} %get-tuple-element.119.mine), channel_id=1, source_target_pairs={{0,8},{1,9},{2,10},{3,11},{4,12},{5,13},{6,14},{7,15},{8,0},{9,1},... | collective-permute-start | bytes 393224 | tf_op jit(solution)/shard_map/ppermute | solution.py:411
  173.2 3.1 %collective-permute-done.31.other = bf16[128,512]{1,0:T(8,128)(2,1)S(1)} collective-permute-done((bf16[128,512]{1,0:T(8,128)(2,1)S(1)}, bf16[128,512]{1,0:T(8,128)(2,1)S(1)}, u32[]{:S(2)}, u32[]{:S(2)}) %collective-permute-start.31) | collective-permute-done | bytes 131104 | tf_op jit(solution)/shard_map/ppermute | solution.py:411
  183.1 3.0 %collective-permute-done.32.other = bf16[256,512]{1,0:T(8,128)(2,1)S(1)} collective-permute-done((bf16[256,512]{1,0:T(8,128)(2,1)S(1)}, bf16[256,512]{1,0:T(8,128)(2,1)S(1)}, u32[]{:S(2)}, u32[]{:S(2)}) %collective-permute-start.32) | collective-permute-done | bytes 262176 | tf_op jit(solution)/shard_map/ppermute | solution.py:411
  (113 shorter events, 47.3 us)
Async XLA Ops:
  6.4 16.1 %collective-permute-start.1 = (bf16[528,512]{1,0:T(8,128)(2,1)S(1)}, bf16[528,512]{1,0:T(8,128)(2,1)S(1)}, u32[]{:S(2)}, u32[]{:S(2)}) collective-permute-start(bf16[528,512]{1,0:T(8,128)(2,1)S(1)} %pack.1.refs_4_.refs_5_.refs_18_), channel_id=1, source_target_pairs={{0,2},{1,3},{2,0},{3,1},{4,6},{5,7},{6,4},{7,5},{8,10},{9,11},{10,... | collective-permute-start | bytes 1622024 | tf_op jit(solution)/shard_map/ppermute | solution.py:411
  9.4 24.4 %collective-permute-start.3 = (bf16[512,512]{1,0:T(8,128)(2,1)}, bf16[512,512]{1,0:T(8,128)(2,1)}, u32[]{:S(2)}, u32[]{:S(2)}) collective-permute-start(bf16[512,512]{1,0:T(8,128)(2,1)} %refs_7_.1), channel_id=1, source_target_pairs={{0,2},{1,3},{2,0},{3,1},{4,6},{5,7},{6,4},{7,5},{8,10},{9,11},{10,... | collective-permute-start | bytes 1572872 | tf_op jit(solution)/shard_map/ppermute | solution.py:411
  9.5 34.8 %collective-permute-start = (bf16[528,512]{1,0:T(8,128)(2,1)S(1)}, bf16[528,512]{1,0:T(8,128)(2,1)S(1)}, u32[]{:S(2)}, u32[]{:S(2)}) collective-permute-start(bf16[528,512]{1,0:T(8,128)(2,1)S(1)} %pack.1.refs_4_.refs_5_.refs_18_), channel_id=1, source_target_pairs={{0,1},{1,0},{2,3},{3,2},{4,5},{5,4},{6,7},{7,6},{8,9},{9,8},{10,11... | collective-permute-start | bytes 1622024 | tf_op jit(solution)/shard_map/ppermute | solution.py:411
  9.5 34.8 %collective-permute-start.5 = (bf16[512,512]{1,0:T(8,128)(2,1)}, bf16[512,512]{1,0:T(8,128)(2,1)}, u32[]{:S(2)}, u32[]{:S(2)}) collective-permute-start(bf16[512,512]{1,0:T(8,128)(2,1)} %refs_9_.1), channel_id=1, source_target_pairs={{0,2},{1,3},{2,0},{3,1},{4,6},{5,7},{6,4},{7,5},{8,10},{9,11},{10,... | collective-permute-start | bytes 1572872 | tf_op jit(solution)/shard_map/ppermute | solution.py:411
  22.5 35.8 %collective-permute-start.2 = (bf16[528,512]{1,0:T(8,128)(2,1)S(1)}, bf16[528,512]{1,0:T(8,128)(2,1)S(1)}, u32[]{:S(2)}, u32[]{:S(2)}) collective-permute-start(bf16[528,512]{1,0:T(8,128)(2,1)S(1)} %collective-permute-done.1.refs_4_.refs_5_.refs_20_), channel_id=1, source_target_pairs={{0,1},{1,0},{2,3},{3,2},{4,5},{5,4},{6,7},{7,6},{8,9},{9,8},{10,11... | collective-permute-start | bytes 1622024 | tf_op jit(solution)/shard_map/ppermute | solution.py:411
  22.5 43.1 %collective-permute-start.7 = (bf16[512,512]{1,0:T(8,128)(2,1)}, bf16[512,512]{1,0:T(8,128)(2,1)S(1)}, u32[]{:S(2)}, u32[]{:S(2)}) collective-permute-start(bf16[512,512]{1,0:T(8,128)(2,1)} %refs_7_.1), channel_id=1, source_target_pairs={{0,1},{1,0},{2,3},{3,2},{4,5},{5,4},{6,7},{7,6},{8,9},{9,8},{10,11... | collective-permute-start | bytes 1572872 | tf_op jit(solution)/shard_map/ppermute | solution.py:411
  33.8 31.7 %collective-permute-start.8 = (bf16[512,512]{1,0:T(8,128)(2,1)}, bf16[512,512]{1,0:T(8,128)(2,1)S(1)}, u32[]{:S(2)}, u32[]{:S(2)}) collective-permute-start(bf16[512,512]{1,0:T(8,128)(2,1)} %refs_9_.1), channel_id=1, source_target_pairs={{0,1},{1,0},{2,3},{3,2},{4,5},{5,4},{6,7},{7,6},{8,9},{9,8},{10,11... | collective-permute-start | bytes 1572872 | tf_op jit(solution)/shard_map/ppermute | solution.py:411
  44.3 28.8 %collective-permute-start.4 = (bf16[512,512]{1,0:T(8,128)(2,1)}, bf16[512,512]{1,0:T(8,128)(2,1)}, u32[]{:S(2)}, u32[]{:S(2)}) collective-permute-start(bf16[512,512]{1,0:T(8,128)(2,1)} %collective-permute-done.3.refs_7_), channel_id=1, source_target_pairs={{0,1},{1,0},{2,3},{3,2},{4,5},{5,4},{6,7},{7,6},{8,9},{9,8},{10,11... | collective-permute-start | bytes 1572872 | tf_op jit(solution)/shard_map/ppermute | solution.py:411
  44.3 28.8 %collective-permute-start.6 = (bf16[512,512]{1,0:T(8,128)(2,1)}, bf16[512,512]{1,0:T(8,128)(2,1)}, u32[]{:S(2)}, u32[]{:S(2)}) collective-permute-start(bf16[512,512]{1,0:T(8,128)(2,1)} %collective-permute-done.5.refs_9_), channel_id=1, source_target_pairs={{0,1},{1,0},{2,3},{3,2},{4,5},{5,4},{6,7},{7,6},{8,9},{9,8},{10,11... | collective-permute-start | bytes 1572872 | tf_op jit(solution)/shard_map/ppermute | solution.py:411
  82.1 17.0 %collective-permute-start.18 = (bf16[528,512]{1,0:T(8,128)(2,1)S(1)}, bf16[528,512]{1,0:T(8,128)(2,1)S(1)}, u32[]{:S(2)}, u32[]{:S(2)}) collective-permute-start(bf16[528,512]{1,0:T(8,128)(2,1)S(1)} %get-tuple-element.114), channel_id=1, source_target_pairs={{0,1},{1,0},{2,3},{3,2},{4,5},{5,4},{6,7},{7,6},{8,9},{9,8},{10,11... | collective-permute-start | bytes 1622024 | tf_op jit(solution)/shard_map/ppermute | solution.py:411
  99.7 15.2 %collective-permute-start.19 = (bf16[528,512]{1,0:T(8,128)(2,1)S(1)}, bf16[528,512]{1,0:T(8,128)(2,1)S(1)}, u32[]{:S(2)}, u32[]{:S(2)}) collective-permute-start(bf16[528,512]{1,0:T(8,128)(2,1)S(1)} %combine.20), channel_id=1, source_target_pairs={{0,2},{1,3},{2,0},{3,1},{4,6},{5,7},{6,4},{7,5},{8,10},{9,11},{10,... | collective-permute-start | bytes 1622024 | tf_op jit(solution)/shard_map/ppermute | solution.py:411
  101.5 15.9 %collective-permute-start.9 = (bf16[528,512]{1,0:T(8,128)(2,1)S(1)}, bf16[528,512]{1,0:T(8,128)(2,1)S(1)}, u32[]{:S(2)}, u32[]{:S(2)}) collective-permute-start(bf16[528,512]{1,0:T(8,128)(2,1)S(1)} %get-tuple-element.98), channel_id=1, source_target_pairs={{0,1},{1,0},{2,3},{3,2},{4,5},{5,4},{6,7},{7,6},{8,9},{9,8},{10,11... | collective-permute-start | bytes 1622024 | tf_op jit(solution)/shard_map/ppermute | solution.py:411
  102.2 24.3 %collective-permute-start.11 = (bf16[528,512]{1,0:T(8,128)(2,1)S(1)}, bf16[528,512]{1,0:T(8,128)(2,1)S(1)}, u32[]{:S(2)}, u32[]{:S(2)}) collective-permute-start(bf16[528,512]{1,0:T(8,128)(2,1)S(1)} %combine.15), channel_id=1, source_target_pairs={{0,2},{1,3},{2,0},{3,1},{4,6},{5,7},{6,4},{7,5},{8,10},{9,11},{10,... | collective-permute-start | bytes 1622024 | tf_op jit(solution)/shard_map/ppermute | solution.py:411
  102.7 26.3 %collective-permute-start.25 = (bf16[512,512]{1,0:T(8,128)(2,1)S(1)}, bf16[512,512]{1,0:T(8,128)(2,1)S(1)}, u32[]{:S(2)}, u32[]{:S(2)}) collective-permute-start(bf16[512,512]{1,0:T(8,128)(2,1)S(1)} %get-tuple-element.122), channel_id=1, source_target_pairs={{0,1},{1,0},{2,3},{3,2},{4,5},{5,4},{6,7},{7,6},{8,9},{9,8},{10,11... | collective-permute-start | bytes 1572872 | tf_op jit(solution)/shard_map/ppermute | solution.py:411
  103.6 33.5 %collective-permute-start.27 = (bf16[512,512]{1,0:T(8,128)(2,1)S(1)}, bf16[512,512]{1,0:T(8,128)(2,1)S(1)}, u32[]{:S(2)}, u32[]{:S(2)}) collective-permute-start(bf16[512,512]{1,0:T(8,128)(2,1)S(1)} %combine.25), channel_id=1, source_target_pairs={{0,2},{1,3},{2,0},{3,1},{4,6},{5,7},{6,4},{7,5},{8,10},{9,11},{10,... | collective-permute-start | bytes 1572872 | tf_op jit(solution)/shard_map/ppermute | solution.py:411
  115.7 23.9 %collective-permute-start.20 = (bf16[272,512]{1,0:T(8,128)(2,1)S(1)}, bf16[272,512]{1,0:T(8,128)(2,1)S(1)}, u32[]{:S(2)}, u32[]{:S(2)}) collective-permute-start(bf16[272,512]{1,0:T(8,128)(2,1)S(1)} %get-tuple-element.116), channel_id=1, source_target_pairs={{0,4},{1,5},{2,6},{3,7},{4,0},{5,1},{6,2},{7,3},{8,12},{9,13},{10,... | collective-permute-start | bytes 835592 | tf_op jit(solution)/shard_map/ppermute | solution.py:411
  127.3 14.6 %collective-permute-start.12 = (bf16[272,512]{1,0:T(8,128)(2,1)S(1)}, bf16[272,512]{1,0:T(8,128)(2,1)S(1)}, u32[]{:S(2)}, u32[]{:S(2)}) collective-permute-start(bf16[272,512]{1,0:T(8,128)(2,1)S(1)} %get-tuple-element.102), channel_id=1, source_target_pairs={{0,4},{1,5},{2,6},{3,7},{4,0},{5,1},{6,2},{7,3},{8,12},{9,13},{10,... | collective-permute-start | bytes 835592 | tf_op jit(solution)/shard_map/ppermute | solution.py:411
  142.5 8.8 %collective-permute-start.13 = (bf16[144,512]{1,0:T(8,128)(2,1)S(1)}, bf16[144,512]{1,0:T(8,128)(2,1)S(1)}, u32[]{:S(2)}, u32[]{:S(2)}) collective-permute-start(bf16[144,512]{1,0:T(8,128)(2,1)S(1)} %get-tuple-element.104), channel_id=1, source_target_pairs={{0,8},{1,9},{2,10},{3,11},{4,12},{5,13},{6,14},{7,15},{8,0},{9,1},... | collective-permute-start | bytes 442376 | tf_op jit(solution)/shard_map/ppermute | solution.py:411
  148.6 21.3 %collective-permute-start.22 = (bf16[144,512]{1,0:T(8,128)(2,1)S(1)}, bf16[144,512]{1,0:T(8,128)(2,1)S(1)}, u32[]{:S(2)}, u32[]{:S(2)}) collective-permute-start(bf16[144,512]{1,0:T(8,128)(2,1)S(1)} %combine.23.refs_1_), channel_id=1, source_target_pairs={{0,16},{1,17},{2,18},{3,19},{4,20},{5,21},{6,22},{7,23},{8,24},{9,... | collective-permute-start | bytes 442376 | tf_op jit(solution)/shard_map/ppermute | solution.py:411
  151.9 20.7 %collective-permute-start.14 = (bf16[144,512]{1,0:T(8,128)(2,1)S(1)}, bf16[144,512]{1,0:T(8,128)(2,1)S(1)}, u32[]{:S(2)}, u32[]{:S(2)}) collective-permute-start(bf16[144,512]{1,0:T(8,128)(2,1)S(1)} %combine.18.refs_1_), channel_id=1, source_target_pairs={{0,16},{1,17},{2,18},{3,19},{4,20},{5,21},{6,22},{7,23},{8,24},{9,... | collective-permute-start | bytes 442376 | tf_op jit(solution)/shard_map/ppermute | solution.py:411
  153.6 15.7 %collective-permute-start.30 = (bf16[128,512]{1,0:T(8,128)(2,1)S(1)}, bf16[128,512]{1,0:T(8,128)(2,1)S(1)}, u32[]{:S(2)}, u32[]{:S(2)}) collective-permute-start(bf16[128,512]{1,0:T(8,128)(2,1)S(1)} %combine.28.refs_1_), channel_id=1, source_target_pairs={{0,16},{1,17},{2,18},{3,19},{4,20},{5,21},{6,22},{7,23},{8,24},{9,... | collective-permute-start | bytes 393224 | tf_op jit(solution)/shard_map/ppermute | solution.py:411
  176.9 9.3 %collective-permute-start.32 = (bf16[256,512]{1,0:T(8,128)(2,1)S(1)}, bf16[256,512]{1,0:T(8,128)(2,1)S(1)}, u32[]{:S(2)}, u32[]{:S(2)}) collective-permute-start(bf16[256,512]{1,0:T(8,128)(2,1)S(1)} %join.5.mine), channel_id=1, source_target_pairs={{0,4},{1,5},{2,6},{3,7},{4,0},{5,1},{6,2},{7,3},{8,12},{9,13},{10,... | collective-permute-start | bytes 786440 | tf_op jit(solution)/shard_map/ppermute | solution.py:411
  178.7 10.9 %collective-permute-start.24 = (bf16[256,512]{1,0:T(8,128)(2,1)S(1)}, bf16[256,512]{1,0:T(8,128)(2,1)S(1)}, u32[]{:S(2)}, u32[]{:S(2)}) collective-permute-start(bf16[256,512]{1,0:T(8,128)(2,1)S(1)} %join.4.mine), channel_id=1, source_target_pairs={{0,4},{1,5},{2,6},{3,7},{4,0},{5,1},{6,2},{7,3},{8,12},{9,13},{10,... | collective-permute-start | bytes 786440 | tf_op jit(solution)/shard_map/ppermute | solution.py:411
  180.5 11.9 %collective-permute-start.16 = (bf16[256,512]{1,0:T(8,128)(2,1)S(1)}, bf16[256,512]{1,0:T(8,128)(2,1)S(1)}, u32[]{:S(2)}, u32[]{:S(2)}) collective-permute-start(bf16[256,512]{1,0:T(8,128)(2,1)S(1)} %join.3.mine), channel_id=1, source_target_pairs={{0,4},{1,5},{2,6},{3,7},{4,0},{5,1},{6,2},{7,3},{8,12},{9,13},{10,... | collective-permute-start | bytes 786440 | tf_op jit(solution)/shard_map/ppermute | solution.py:411
  (26 other events, 115.8 us)

commit v2 on v1

v2 whole, which is shorter than its diff:
```python
import functools

import jax
import jax.numpy as jnp
from jax import lax
from jax.experimental import pallas as pl
from jax.experimental.pallas import tpu as pltpu
from jax.sharding import PartitionSpec as P

BF, F32 = jnp.bfloat16, jnp.float32
D = 512
HD = 64
SLOT = 128
BR = 256
BIAS = 16
EPS = 1e-5
WEIGHTS = {"attn_dw_sent": 1, "attn_core_bwd": 1, "attn_dx": 1, "add_d_x": 0, "add_l_y": 0, "add_h_x": 0, "add_u_y": 0}
LN1_G, LN1_B, B_OUT, LN2_G, LN2_B, B_DOWN, B_UP, B_QV = range(8)
SMEM = functools.partial(pl.BlockSpec, memory_space=pltpu.SMEM)
VMEM = functools.partial(pl.BlockSpec, memory_space=pltpu.VMEM)


def dot(a, b):
    return lax.dot_general(a, b, (((1,), (0,)), ((), ())), preferred_element_type=F32)


def dot_nt(a, b):
    return lax.dot_general(a, b, (((1,), (1,)), ((), ())), preferred_element_type=F32)


def dot_tn(a, b):
    return lax.dot_general(a, b, (((0,), (0,)), ((), ())), preferred_element_type=F32)


def params(mib, **kw):
    return pltpu.CompilerParams(vmem_limit_bytes=mib << 20, **kw)


def cost(flops, nbytes, trans=0):
    return pl.CostEstimate(flops=int(flops), bytes_accessed=int(nbytes), transcendentals=int(trans))


def sds(shape, dtype=BF):
    return jax.ShapeDtypeStruct(shape, dtype)


def whole(shape):
    return pl.BlockSpec(shape, lambda *i: (0,) * len(shape))


def normalise(v):
    mean = jnp.mean(v, -1, keepdims=True)
    centred = v - mean
    rstd = lax.rsqrt(jnp.mean(centred * centred, -1, keepdims=True) + EPS)
    return centred * rstd, rstd


def head_stack(v):
    first = lax.broadcasted_iota(jnp.int32, v.shape, 1) < HD
    zero = jnp.zeros_like(v)
    return jnp.concatenate([jnp.where(first, v, zero), jnp.where(first, zero, v)], 0)


def untranspose(v):
    return jnp.concatenate([v[:, :SLOT].T, v[:, SLOT:].T], 1)


def slot_bias(len1, len2):
    def places(shape, dim):
        p = lax.broadcasted_iota(jnp.int32, shape, dim) & (SLOT - 1)
        second = (p >= SLOT // 2) & (len2 > 0)
        local = jnp.where(second, p - SLOT // 2, p)
        valid = local < jnp.where(second, len2, len1)
        base = jnp.where(second, 1000, 0)
        return valid, base, base + ((local * 43) >> 8)

    valid_k, _, frame_k = places((SLOT, 1), 0)
    valid_q, base_q, frame_q = places((1, 2 * SLOT), 1)
    frame_k = jnp.where(valid_k, frame_k, 1 << 20)
    frame_q = jnp.where(valid_q, frame_q, -1)
    allowed = (frame_k <= frame_q) & (frame_k >= base_q)
    return jnp.where(allowed, 0.0, -1e30).astype(F32)


def pack_kernel(*refs):
    wq, wk, wv, wo = refs[:4]
    small, (out, vecs), held, sems = refs[4:13], refs[13:15], refs[15:24], refs[24]
    copies = [pltpu.make_async_copy(v, h, sems.at[7 + i]) for i, (v, h) in enumerate(zip(small, held))]
    for i, ref in enumerate((wq, wk, wv)):
        copies.append(pltpu.make_async_copy(ref, out.at[0:D, i * 128 : (i + 1) * 128], sems.at[i]))
    for b in range(4):
        blk = slice(b * 128, (b + 1) * 128)
        copies.append(pltpu.make_async_copy(wo.at[:, blk], out.at[blk, 384:512], sems.at[3 + b]))
    for c in copies:
        c.start()
    for c in copies[: len(small)]:
        c.wait()
    rows = [h[...].astype(F32).reshape(1, h.shape[0]) for h in held]
    gap = jnp.zeros((1, 128), F32)
    rows[7:] = [jnp.concatenate([rows[7], gap, rows[8], gap], 1)]
    table = jnp.concatenate(rows, 0)
    vecs[...] = table
    row = lax.broadcasted_iota(jnp.int32, (BIAS, D), 0)
    block = jnp.where(row == 0, table[B_QV : B_QV + 1], jnp.where(row == 1, table[B_UP : B_UP + 1], 0.0))
    out[D : D + BIAS, :] = block.astype(BF)
    for c in copies[len(small) :]:
        c.wait()


def prep_kernel(x, vecs, n1_o):
    def tile(m, _):
        here = pl.ds(pl.multiple_of(m * BR, BR), BR)
        xhat, _ = normalise(x[here, :].astype(F32))
        n1_o[here, :] = (xhat * vecs[LN1_G : LN1_G + 1, :] + vecs[LN1_B : LN1_B + 1, :]).astype(BF)
        return 0

    lax.fori_loop(0, x.shape[0] // BR, tile, 0, unroll=2)


def attn_fwd_kernel(shares, first, last, *refs):
    (scal, lens, n1, base), w = refs[:4], refs[4 : 4 + shares]
    vecs, (q_o, k_o, v_o, att_o, pt_o, hid_o), n2_o = refs[4 + shares], refs[5 + shares : 11 + shares], refs[-1]
    slots = n1.shape[0] // SLOT

    for c in range(shares):
        brow = w[c][D : D + BIAS, :].astype(F32)[0:1]
        cols = slice(c * 128, (c + 1) * 128)
        qkv = dot(n1[...], w[c][0:D, 0:384])
        q_o[:, cols] = (qkv[:, 0:128] + brow[:, 0:128]).astype(BF) * jnp.asarray(0.125, BF)
        k_o[:, cols] = qkv[:, 128:256].astype(BF)
        v_o[:, cols] = (qkv[:, 256:384] + brow[:, 256:384]).astype(BF)

    def slot(s, _):
        rows = pl.ds(pl.multiple_of(s * SLOT, SLOT), SLOT)
        place = scal[3] + s
        mask = slot_bias(lens[0, place, 0], lens[0, place, 1])
        for c in range(shares):
            cols = slice(c * 128, (c + 1) * 128)
            st = dot_nt(k_o[rows, cols], head_stack(q_o[rows, cols])) + mask
            top = jnp.maximum(jnp.max(st, 0, keepdims=True), -1e29)
            e = jnp.exp(st - top)
            den = jnp.sum(e, 0, keepdims=True)
            pt = (e * (1.0 / jnp.where(den == 0.0, 1.0, den))).astype(BF)
            pt_o[rows, c * 256 : (c + 1) * 256] = pt
            att_o[rows, cols] = dot(untranspose(pt), head_stack(v_o[rows, cols])).astype(BF)
        return 0

    lax.fori_loop(0, slots, slot, 0, unroll=True)
    hid = base[...].astype(F32)
    if first:
        hid += vecs[B_OUT : B_OUT + 1, :]
    for c in range(shares):
        wo = jnp.concatenate([w[c][b * 128 : (b + 1) * 128, 384:512] for b in range(4)], 1)
        hid += dot(att_o[:, c * 128 : (c + 1) * 128], wo)
    hid_o[...] = hid
    if last:

        def tile(m, _):
            here = pl.ds(pl.multiple_of(m * BR, BR), BR)
            xhat, _ = normalise(hid_o[here, :])
            n2_o[here, :] = (xhat * vecs[LN2_G : LN2_G + 1, :] + vecs[LN2_B : LN2_B + 1, :]).astype(BF)
            return 0

        lax.fori_loop(0, n1.shape[0] // BR, tile, 0, unroll=2)


def gelu_pair(u):
    phi = 0.5 + 0.5 * lax.erf(u * 0.7071067811865476)
    return u * phi, phi + u * (jnp.exp(-0.5 * (u * u)) * 0.3989422804014327)


def mlp_kernel(first, *refs):
    if first:
        (n2, cot, ba, bb, ua, ub, da, db, gua, gub, gda, gdb, out, dn2, act_s, gup_s) = refs
    else:
        (n2, cot, ba, bb, ua, ub, da, db, out_i, dn2_i, gua, gub, gda, gdb, out, dn2, act_s, gup_s) = refs
    bias = [b[D : D + BIAS, :].astype(F32)[1:2] for b in (ba, bb)]

    def tile(m, sums):
        here = pl.ds(pl.multiple_of(m * BR, BR), BR)
        n, c = n2[here, :], cot[here, :]
        new, acts, gups = [], [], []
        for j, (u, d) in enumerate(((ua, da), (ub, db))):
            up = dot(n, u[...]) + bias[j]
            dact = dot_nt(c, d[...])
            act, slope = gelu_pair(up)
            gup = (slope * dact).astype(BF)
            act = act.astype(BF)
            act_s[here, j * D : (j + 1) * D] = act
            gup_s[here, j * D : (j + 1) * D] = gup
            new.append(sums[j] + jnp.sum(gup.astype(F32), 0, keepdims=True))
            acts.append(act)
            gups.append(gup)
        o = dot(acts[0], da[...]) + dot(acts[1], db[...])
        e = dot_nt(gups[0], ua[...]) + dot_nt(gups[1], ub[...])
        out[here, :] = o if first else out_i[here, :] + o
        dn2[here, :] = e if first else dn2_i[here, :] + e
        return tuple(new)

    zero = jnp.zeros((1, D), F32)
    sums = lax.fori_loop(0, n2.shape[0] // BR, tile, (zero, zero), unroll=True)
    row = lax.broadcasted_iota(jnp.int32, (BIAS, D), 0)
    for j, (gu_o, gd_o) in enumerate(((gua, gda), (gub, gdb))):
        cols = slice(j * D, (j + 1) * D)
        gu_o[0:D, :] = dot_tn(n2[...], gup_s[:, cols]).astype(BF)
        gd_o[0:D, :] = dot_tn(cot[...], act_s[:, cols]).astype(BF)
        high = sums[j].astype(BF).astype(F32)
        gu_o[D : D + BIAS, :] = jnp.where(row == 0, high, jnp.where(row == 8, sums[j] - high, 0.0)).astype(BF)


def act_kernel(n2, cot, bias, u, act_o, slope_o, gd_o):
    add = bias[D : D + BIAS, :].astype(F32)[1:2]

    def tile(m, _):
        here = pl.ds(pl.multiple_of(m * BR, BR), BR)
        act, slope = gelu_pair(dot(n2[here, :], u[...]) + add)
        act_o[here, :] = act.astype(BF)
        slope_o[here, :] = slope
        return 0

    lax.fori_loop(0, n2.shape[0] // BR, tile, 0, unroll=True)
    gd_o[...] = dot_tn(cot[...], act_o[...]).astype(BF)


def down_kernel(n2, cot, act, slope, u, d, out_i, dn2_i, gu_o, out, dn2, gup_s):
    def tile(m, sums):
        here = pl.ds(pl.multiple_of(m * BR, BR), BR)
        gup = (slope[here, :] * dot_nt(cot[here, :], d[...])).astype(BF)
        gup_s[here, :] = gup
        out[here, :] = out_i[here, :] + dot(act[here, :], d[...])
        dn2[here, :] = dn2_i[here, :] + dot_nt(gup, u[...])
        return sums + jnp.sum(gup.astype(F32), 0, keepdims=True)

    sums = lax.fori_loop(0, n2.shape[0] // BR, tile, jnp.zeros((1, D), F32), unroll=True)
    gu_o[0:D, :] = dot_tn(n2[...], gup_s[...]).astype(BF)
    gu_o[D : D + BIAS, :] = bias_block(jnp.concatenate([sums, jnp.zeros((7, D), F32)], 0))


def total(sums, *adds):
    return sums + jnp.concatenate([jnp.sum(a, 0, keepdims=True) for a in adds], 0)


def ln2_bwd_kernel(hid, mlp, dn2, cot, vecs, *refs):
    w, (block_o, dh_o, gat_s, datt_o, sums_o) = refs[:4], refs[4:]
    rows = hid.shape[0]

    def tile(m, sums):
        here = pl.ds(pl.multiple_of(m * BR, BR), BR)
        hidden = hid[here, :]
        block_o[here, :] = (hidden + mlp[here, :] + vecs[B_DOWN : B_DOWN + 1, :]).astype(BF)
        xhat, rstd = normalise(hidden)
        dn = dn2[here, :]
        e = dn * vecs[LN2_G : LN2_G + 1, :]
        cotf = cot[here, :].astype(F32)
        dh = cotf + rstd * (e - jnp.mean(e, -1, keepdims=True) - xhat * jnp.mean(e * xhat, -1, keepdims=True))
        dh_o[here, :] = dh
        gat = dh.astype(BF)
        gat_s[here, :] = gat
        return total(sums, gat.astype(F32), dn * xhat, dn, cotf)

    sums_o[0:4, :] = lax.fori_loop(0, rows // BR, tile, jnp.zeros((4, D), F32), unroll=2)
    sums_o[4:8, :] = jnp.zeros((4, D), F32)
    for c in range(4):
        wo = jnp.concatenate([w[c][b * 128 : (b + 1) * 128, 384:512] for b in range(4)], 1)
        datt_o[:, c * 128 : (c + 1) * 128] = dot_nt(gat_s[...], wo).astype(BF)


def attn_core_bwd_kernel(*refs):
    saved, (datt, dq_o, dk_o, dv_o) = refs[:12], refs[12:]
    where = ((0, 0), (0, 1), (1, 0), (2, 0))

    def slot(s, _):
        rows = pl.ds(pl.multiple_of(s * SLOT, SLOT), SLOT)
        held = []
        for c, (group, at) in enumerate(where):
            q, k, v, pt_r = saved[4 * group : 4 * group + 4]
            cols = slice(at * 128, (at + 1) * 128)
            out = slice(c * 128, (c + 1) * 128)
            das = head_stack(datt[rows, out])
            pt = pt_r[rows, at * 256 : (at + 1) * 256]
            dpt = dot_nt(v[rows, cols], das)
            dv_o[rows, out] = dot(pt, das).astype(BF)
            held.append((q, k, cols, out, pt, dpt))
        ready = []
        for q, k, cols, out, pt, dpt in held:
            ptf = pt.astype(F32)
            delta = jnp.sum(ptf * dpt, 0, keepdims=True)
            ds = (ptf * (dpt - delta)).astype(BF)
            ready.append((q, k, cols, out, ds, untranspose(ds)))
        for q, k, cols, out, ds, dst in ready:
            dq_o[rows, out] = (dot(dst, head_stack(k[rows, cols])) * 0.125).astype(BF)
            dk_o[rows, out] = dot(ds, head_stack(q[rows, cols])).astype(BF)
        return 0

    lax.fori_loop(0, datt.shape[0] // SLOT, slot, 0, unroll=True)


def attn_dw_kernel(one, two, dq, dk, dv, n1, gat, shared, att_one, att_two, *ga):
    gap, rest = jnp.zeros((1, 128), F32), shared[0:7, :]
    grads = [[s[:, c * 128 : (c + 1) * 128] for s in (dq, dk, dv)] for c in (one, two)]
    sums = [[jnp.sum(g[j].astype(F32), 0, keepdims=True) for j in (0, 2)] for g in grads]
    g = dot_tn(n1[...], jnp.concatenate(grads[0] + grads[1], 1)).astype(BF)
    att = [a[...] if a.shape[1] == 128 else a[:, (c % 2) * 128 : (c % 2 + 1) * 128] for a, c in zip((att_one, att_two), (one, two))]
    go = dot_tn(gat[...], jnp.concatenate(att, 1)).astype(BF)
    for i in range(2):
        o, at = ga[i % len(ga)], 0 if len(ga) == 2 else i * (D + BIAS)
        o[at : at + D, 0:384] = g[:, i * 384 : (i + 1) * 384]
        o[at : at + D, 384:512] = go[:, i * 128 : (i + 1) * 128]
        own = jnp.concatenate([sums[i][0], gap, sums[i][1], gap], 1)
        o[at + D : at + D + BIAS, :] = bias_block(jnp.concatenate([own, rest], 0))


def attn_dx_kernel(x, dh, dq, dk, dv, sums2, vecs, *refs):
    w, (gin_o, shared_o) = refs[:4], refs[4:]

    def tile(m, sums):
        here = pl.ds(pl.multiple_of(m * BR, BR), BR)
        dn1 = None
        for c in range(4):
            cols = slice(c * 128, (c + 1) * 128)
            grads = jnp.concatenate([dq[here, cols], dk[here, cols], dv[here, cols]], 1)
            part = dot_nt(grads, w[c][0:D, 0:384])
            dn1 = part if dn1 is None else dn1 + part
        xhat, rstd = normalise(x[here, :].astype(F32))
        e = dn1 * vecs[LN1_G : LN1_G + 1, :]
        back = rstd * (e - jnp.mean(e, -1, keepdims=True) - xhat * jnp.mean(e * xhat, -1, keepdims=True))
        gin_o[here, :] = (dh[here, :] + back).astype(BF)
        return total(sums, dn1 * xhat, dn1)

    sums1 = lax.fori_loop(0, x.shape[0] // BR, tile, jnp.zeros((2, D), F32), unroll=True)
    shared_o[...] = jnp.concatenate([sums1, sums2[0:4, :], jnp.zeros((2, D), F32)], 0)


def bias_block(total):
    high = total.astype(BF)
    return jnp.concatenate([high, (total - high.astype(F32)).astype(BF)], 0)


class Part:
    def __init__(self, n, sources, sums=()):
        self.n, self.sources, self.sums = n, sources, sums
        self.extra = BIAS if sums else 0


def combine_kernel(parts, op, *refs):
    scal, ins = refs[0], refs[1:]
    n_in = 1 + max(i for part in parts for i, _ in part[1] + part[2])
    ins, outs = ins[:n_in], ins[n_in:]

    def summed(part, start, size):
        acc = None
        for i, first in part[1]:
            v = ins[i][pl.ds(first + start, size), :].astype(F32)
            acc = v if acc is None else acc + v
        return acc.astype(BF)

    def sums(part):
        rows = [ins[i][first : first + BIAS, :].astype(F32) for i, first in part[2]]
        terms = [v[0:8] + v[8:16] for v in rows]
        while len(terms) > 1:
            terms = [sum(terms[i + 1 : i + 2], terms[i]) for i in range(0, len(terms), 2)]
        return terms[0]

    if op == "y":
        for o, part in zip(outs, (parts[1], parts[0])):
            n = part[0]
            o[0:n, :] = summed(part, 0, n)
            if part[2]:
                o[n : n + BIAS, :] = bias_block(sums(part))
        return
    at, side = 0, 1
    for part in parts:
        n, biased = part[0], bool(part[2])
        if op in ("all", "last"):
            outs[0][at : at + n, :] = summed(part, 0, n)
            at += n
            if biased and op == "last":
                outs[side][...] = sums(part)
                side += 1
            elif biased:
                outs[0][at : at + BIAS, :] = bias_block(sums(part))
                at += BIAS
        else:
            bit, h = scal[op], n // 2
            outs[0][at : at + h, :] = summed(part, pl.multiple_of((1 - bit) * h, h), h)
            outs[1][at : at + h, :] = summed(part, pl.multiple_of(bit * h, h), h)
            at += h
            if biased:
                block = bias_block(sums(part))
                for o in outs:
                    o[at : at + BIAS, :] = block
                at += BIAS


def join_kernel(scal, mine, other, out):
    bit, n = scal[1], mine.shape[0]
    out[pl.ds(pl.multiple_of(bit * n, n), n), :] = mine[...]
    out[pl.ds(pl.multiple_of((1 - bit) * n, n), n), :] = other[...]


def final_kernel(kind, *refs):
    scal, outs = refs[0], refs[-1:] if kind != "attn" else refs[-5:]
    got = refs[1 : len(refs) - len(outs)]
    x, z = scal[0], scal[1]
    if len(got) == 2:
        places = (x, 1 - x)
    else:
        places = (x * 2 + z, x * 2 + 1 - z, (1 - x) * 2 + z, (1 - x) * 2 + 1 - z)
    halves = 2 if kind == "attn" else 1
    n = got[0].shape[0] // halves
    for half in range(halves):
        for place, ref in zip(places, got):
            at = pl.ds(pl.multiple_of(half * 4 * n + place * n, n), n)
            v = ref[half * n : (half + 1) * n, :].astype(F32)
            if kind == "up":
                outs[0][at, :] = v
            elif kind == "down":
                outs[0][:, at] = v.T
            else:
                for j in range(3):
                    outs[j][at, :] = v[:, j * 128 : (j + 1) * 128]
                outs[4][at, :] = v[:, 384:512]
    if kind == "attn":
        outs[3][...] = outs[4][...].T


def layer(
    n_dp, n_t, x, lengths, ln1_gain, ln1_bias, w_query, b_query, w_key, w_value, b_value, w_out, b_out,
    ln2_gain, ln2_bias, w_up, b_up, w_down, b_down, cot,
):
    rows = x.shape[0]
    dp_at, t_at = lax.axis_index("dp"), lax.axis_index("tensor")
    scal = jnp.stack([dp_at & 1, (dp_at >> 1) & 1, t_at, t_at * (rows // SLOT)]).astype(jnp.int32)
    last = [scal]

    class Swap:
        def __init__(self, v, dp_mask=0, t_mask=0):
            self.v, self.masks, self.shape, self.made = v, (dp_mask, t_mask), v.shape, None

        def get(self):
            if self.made is None:
                self.made = swap_now(self.v, *self.masks)
            return self.made

    def real(v):
        return v.get() if isinstance(v, Swap) else v

    def swap(v, dp_mask=0, t_mask=0):
        return Swap(real(v), dp_mask, t_mask)

    def swap_now(v, dp_mask=0, t_mask=0):
        pairs = [(d * n_t + t, (d ^ dp_mask) * n_t + (t ^ t_mask)) for d in range(n_dp) for t in range(n_t)]
        return lax.ppermute(v, ("dp", "tensor"), pairs)

    def after(v, *tokens):
        return lax.optimization_barrier((real(v), *tokens))[0]

    def hbm(v):
        return pltpu.with_memory_space_constraint(v, pltpu.HBM)

    def call(kernel, name, out_shape, args, scratch=(), mib=16, in_hbm=False, weight=10):
        args = [real(a) for a in args]
        if last[0] is not scal:
            i = max(range(len(args)), key=lambda j: args[j].size)
            args[i] = after(args[i], last[0])
        specs = [SMEM() if a.dtype == jnp.int32 else VMEM() for a in args]
        if in_hbm:
            args = [hbm(a) for a in args]
            specs = [pl.BlockSpec(memory_space=pltpu.HBM)] * len(args)
        out = pl.pallas_call(
            kernel,
            out_shape=out_shape,
            in_specs=specs,
            out_specs=[VMEM()] * len(out_shape),
            scratch_shapes=list(scratch),
            compiler_params=params(mib),
            cost_estimate=cost(WEIGHTS.get(name, weight) * 10**9, 10**8),
            name=name,
        )(*args)
        last[0] = min(out, key=lambda o: o.size)
        return out

    def combine(op, *parts, tag="z"):
        arrays = []
        for part in parts:
            for array, _ in (*part.sources, *part.sums):
                array = real(array)
                if not any(array is known for known in arrays):
                    arrays.append(array)
        place = lambda array: next(i for i, known in enumerate(arrays) if known is real(array))
        spec = tuple((p.n, *(tuple((place(v), first) for v, first in w) for w in (p.sources, p.sums))) for p in parts)
        if op == "y":
            shapes = [sds((p.n + p.extra, D)) for p in (parts[1], parts[0])]
        elif op == "all":
            shapes = [sds((sum(p.n + p.extra for p in parts), D))]
        elif op == "last":
            shapes = [sds((sum(p.n for p in parts), D))] + [sds((8, D), F32) for p in parts if p.sums]
        else:
            shapes = [sds((sum(p.n // 2 + p.extra for p in parts), D))] * 2
        return call(functools.partial(combine_kernel, spec, op), "add_" + tag, shapes, [scal, *arrays], mib=8)

    own, vecs = call(
        pack_kernel, "pack", [sds((D + BIAS, D)), sds((8, D), F32)],
        [w_query, w_key, w_value, w_out, ln1_gain, ln1_bias, b_out, ln2_gain, ln2_bias, b_down, b_up, b_query, b_value],
        [pltpu.VMEM((D,), F32)] * 2 + [pltpu.VMEM((D,), BF)] + [pltpu.VMEM((D,), F32)] * 2 + [pltpu.VMEM((D,), BF)] * 2
        + [pltpu.VMEM((128,), BF)] * 2 + [pltpu.SemaphoreType.DMA((16,))],
        in_hbm=True,
    )
    wide, acc = sds((rows, D)), sds((rows, D), F32)
    wa_y, wa_c = swap(own, t_mask=2), swap(own, t_mask=1)
    (n1,) = call(prep_kernel, "prep", [wide], [x, vecs])
    wu_y = swap(after(w_up, n1), t_mask=2)
    wd_y = swap(after(w_down, n1), t_mask=2)

    def attn_fwd(name, weights, hid, first=False, last=False):
        n = 128 * len(weights)
        shapes = [sds((rows, n))] * 4 + [sds((rows, 2 * n)), acc] + [wide] * last
        args = [scal, lengths, n1, hid, *weights, vecs]
        return call(functools.partial(attn_fwd_kernel, len(weights), first, last), name, shapes, args)

    *saved_0, att0, pt0, hid = attn_fwd("attn_fwd_own", [own, wa_c], x, first=True)
    wa_y = after(wa_y, hid)
    wa_yc = swap(wa_y, t_mask=1)
    *saved_2, att2, pt2, hid = attn_fwd("attn_fwd_y", [wa_y], hid)
    wu_c, wd_c = swap(after(w_up, hid), t_mask=1), swap(after(w_down, hid), t_mask=1)
    *saved_3, att3, pt3, hid, n2 = attn_fwd("attn_fwd_yc", [wa_yc], hid, last=True)
    wa = [own, wa_c, wa_y, wa_yc]

    def part(n, *arrays, first=0, sums=True):
        return Part(n, [(v, first) for v in arrays], [(v, v.shape[0] - BIAS) for v in arrays] if sums else ())

    h, q = D // 2, D // 4
    bits = [1 << b for b in range(2, n_dp.bit_length() - 1)]
    gu1, gu0, gd1, gd0, out_sum, dn2 = call(
        functools.partial(mlp_kernel, True), "mlp_own", [sds((D + BIAS, D))] * 2 + [sds((D, D))] * 2 + [acc] * 2,
        [n2, cot, wa_c, own, wu_c, w_up, wd_c, w_down], [pltpu.VMEM((rows, 2 * D), BF)] * 2,
    )
    gd1, gu1 = swap(gd1, t_mask=1), swap(gu1, t_mask=1)
    wu_y = after(wu_y, out_sum)
    wu_yc = swap(wu_y, t_mask=1)

    def up(name, bias, u):
        return call(act_kernel, name, [wide, acc, sds((D, D))], [n2, cot, bias, u])

    def down(name, act, slope, u, d, *sums):
        return call(
            down_kernel, name, [sds((D + BIAS, D))] + [acc] * 2, [n2, cot, act, slope, u, d, *sums],
            [pltpu.VMEM((rows, D), BF)],
        )

    act2, slope2, gd2 = up("mlp_up_y", wa_y, wu_y)
    act3, slope3, gd3 = up("mlp_up_yc", wa_yc, wu_yc)
    gd3 = swap(gd3, t_mask=1)
    send, keep_u0 = combine(0, part(D, gu0, gu1), tag="u0")
    got_u0 = swap(send, dp_mask=1)
    send, keep_d = combine("y", part(D, gd0, gd1, sums=False), part(D, gd2, gd3, sums=False), tag="d_y")
    got_d = swap(send, t_mask=2)
    wd_y = after(wd_y, send)
    wd_yc = swap(wd_y, t_mask=1)
    gu2, out_sum, dn2 = down("mlp_down_y", act2, slope2, wu_y, wd_y, out_sum, dn2)
    gu3, out_sum, dn2 = down("mlp_down_yc", act3, slope3, wu_yc, wd_yc, out_sum, dn2)
    gu3 = swap(gu3, t_mask=1)
    block_out, dh, gat, datt, sums2 = call(
        ln2_bwd_kernel, "ln2_bwd", [wide, acc, wide, wide, sds((8, D), F32)], [hid, out_sum, dn2, cot, vecs, *wa]
    )
    send, keep_u2 = combine(0, part(D, gu2, gu3), tag="u2")
    got_u2 = swap(send, dp_mask=1)
    send, keep_d = combine(0, part(D, keep_d, got_d, sums=False), tag="d_x")
    got_d = swap(send, dp_mask=1)
    dq, dk, dv = call(
        attn_core_bwd_kernel, "attn_core_bwd", [wide] * 3, [*saved_0, pt0, *saved_2, pt2, *saved_3, pt3, datt]
    )
    grad_in, shared = call(
        attn_dx_kernel, "attn_dx", [wide, sds((8, D), F32)], [x, dh, dq, dk, dv, sums2, vecs, *wa]
    )
    send, keep_u = combine("y", part(h, keep_u0, got_u0), part(h, keep_u2, got_u2), tag="u_y")
    got_u = swap(send, t_mask=2)

    def attn_dw(name, shapes, one, two, *atts):
        return call(functools.partial(attn_dw_kernel, one, two), name, shapes, [dq, dk, dv, n1, gat, shared, *atts])

    (got_a,) = attn_dw("attn_dw_sent", [sds((2 * (D + BIAS), D))], 1, 3, att0, att3)
    got_a = swap(got_a, t_mask=1)
    ga = attn_dw("attn_dw_kept", [sds((D + BIAS, D))] * 2, 0, 2, att0, att2)
    send, keep_d = combine(1, part(h, keep_d, got_d, sums=False), tag="d_z")
    got_d = swap(send, dp_mask=2)
    ab = lambda first, sums: [
        Part(h, [(ga[i], first), (got_a, i * (D + BIAS) + first)], [(ga[i], D), (got_a, i * (D + BIAS) + D)] if sums else ())
        for i in range(2)
    ]
    send, keep_l = combine("y", *ab(0, True), tag="l_y")
    got_l = swap(send, t_mask=2)
    send, keep_h = combine(0, *ab(h, False), tag="h_x")
    got_h = swap(send, dp_mask=1)

    def over_z(*parts):
        parts = list(parts)
        for bit in bits:
            (one,) = combine("all", *parts)
            two = swap(one, dp_mask=bit)
            at, new = 0, []
            for p in parts:
                new.append(Part(p.n, [(v, at) for v in (one, two)], [(v, at + p.n) for v in (one, two)] if p.sums else ()))
                at += p.n + p.extra
            parts = new
            yield None
        yield combine("last", *parts)

    def gather(mine):
        return [mine] + [swap(mine, dp_mask=m) for m in (2, 1, 3)]

    def finish(kind, shapes, quarters):
        return call(
            functools.partial(final_kernel, kind), "final_" + kind, shapes, [scal, *quarters],
            [pltpu.VMEM((D, 128), F32)] if kind == "attn" else [],
        )

    send, keep_u = combine(1, part(h, keep_u, got_u), tag="u_z")
    got_u = swap(send, dp_mask=2)
    z_d = over_z(part(q, keep_d, got_d, sums=False))
    for _ in bits:
        next(z_d)
    send, keep_l = combine(0, part(h, keep_l, got_l), tag="l_x")
    got_l = swap(send, dp_mask=1)
    send, keep_h = combine("y", *(Part(q, [(keep_h, i * q), (got_h, i * q)]) for i in range(2)), tag="h_y")
    got_h = swap(send, t_mask=2)
    z_u = over_z(part(q, keep_u, got_u))
    for _ in bits:
        next(z_u)
    (mine_d,) = next(z_d)
    d_other = swap(mine_d, dp_mask=2)
    send, keep_a = combine(1, part(q, keep_l, got_l), part(q, keep_h, got_h, sums=False), tag="a_z")
    got_a = swap(send, dp_mask=2)
    e = q // 2
    z_a = over_z(
        Part(e, [(v, 0) for v in (keep_a, got_a)], [(v, e) for v in (keep_a, got_a)]),
        Part(e, [(v, e + BIAS) for v in (keep_a, got_a)]),
    )
    def joined(mine, other, name):
        (half,) = call(join_kernel, name, [sds((2 * mine.shape[0], D))], [scal, mine, other], mib=8)
        return [half, swap(half, dp_mask=1)]

    all_d = joined(mine_d, d_other, "join_d")
    for _ in bits:
        next(z_a)

    mine_u, sums_up = next(z_u)
    u_other = swap(mine_u, dp_mask=2)
    all_u = joined(mine_u, u_other, "join_u")
    mine_a, sums = next(z_a)
    all_a = gather(mine_a)
    (grad_w_down,) = finish("down", [sds((D, D), F32)], all_d)
    (grad_w_up,) = finish("up", [sds((D, D), F32)], all_u)
    gwq, gwk, gwv, gwo = finish("attn", [sds((D, 128), F32)] * 3 + [sds((128, D), F32)], all_a)
    return (
        block_out, grad_in, sums[1], sums[2], gwq, sums[0, 0:128], gwk, gwv, sums[0, 256:384], gwo, sums[3],
        sums[4], sums[5], grad_w_up, sums_up[0], grad_w_down, sums[6],
    )


def solution(mesh):
    n_dp, n_t = mesh.shape["dp"], mesh.shape["tensor"]
    rows, cols, split, copied = P(("dp", "tensor"), None), P(None, "tensor"), P("tensor"), P()
    down = P("tensor", None)
    return jax.shard_map(
        functools.partial(layer, n_dp, n_t),
        mesh=mesh,
        in_specs=(
            rows, P("dp", None, None), copied, copied, cols, split, cols, cols, split, down, copied, copied, copied,
            cols, split, down, copied, rows,
        ),
        out_specs=(
            rows, rows, copied, copied, cols, split, cols, cols, split, down, copied, copied, copied, cols, split, down,
            copied,
        ),
        check_vma=False,
    )
```

time: 194 us -> 123 us (0.63)
  waiting for transfers between devices: 84.2 us -> 19.5 us
  local copies, waits for them, and re-layouts: 13.4 us -> 1.8 us
  starting transfers between devices: 32 us -> 35.6 us
    ppermute x33 -> x36, waiting for transfers between devices: 84.2 us -> 19.5 us  [swap_now(): return lax.ppermute(v, ('dp', 'tensor'), pairs)]
    unnamed x35 -> x7, local copies, waits for them, and re-layouts: 9.53 us -> 0.1 us
    ppermute x33 -> x36, starting transfers between devices: 32 us -> 35.6 us  [swap_now(): return lax.ppermute(v, ('dp', 'tensor'), pairs)]
    reshape x4 -> x0, local copies, waits for them, and re-layouts: 2.15 us -> none  [the longest x3 2.05 us: layer(): row = lambda v: v.reshape(1, -1)]
    pallas_call x28 -> x38, Pallas kernels: 63.2 us -> 64.4 us  [call(): pl.pallas_call(kernel, out_shape=out_shape, in_specs=specs, out_specs=[VM...]
  transfers between devices with their start and end apart: 33 -> 36, of which waited for: 14 -> 9; matrix products, arithmetic and copies ran while one was open for 2% -> 2% of each run, Pallas kernels for 27% -> 50%
where the time goes in v2:
time: 123 us; the launch traced here: 122 us
  Pallas kernels  64.4 us (52%)
  starting transfers between devices  35.6 us (29%)
  waiting for transfers between devices  19.5 us (16%)
  local copies, waits for them, and re-layouts  1.8 us (1%)
    pallas_call x38, Pallas kernels, call(): pl.pallas_call(kernel, out_shape=out_shape, in_specs=specs, out_specs=[VM...  64.4 us
    ppermute x36, starting transfers between devices, swap_now(): return lax.ppermute(v, ('dp', 'tensor'), pairs)  35.6 us
    ppermute x36, waiting for transfers between devices, swap_now(): return lax.ppermute(v, ('dp', 'tensor'), pairs)  19.5 us
  transfers between devices with their start and end apart: 36, of which 9 were waited for; matrix products, arithmetic and copies ran while one was open for 2% of the time, Pallas kernels for 50%

profile of v2, /device:TPU:0, one launch (start us, length us, event | category | flops | bytes accessed | tf_op | source)
XLA Modules:
  0.0 122.4 jit_solution(3163819307338892066)
XLA Ops:
  2.1 3.0 %collective-permute-start.1 = (bf16[528,512]{1,0:T(8,128)(2,1)S(1)}, bf16[528,512]{1,0:T(8,128)(2,1)S(1)}, u32[]{:S(2)}, u32[]{:S(2)}) collective-permute-start(bf16[528,512]{1,0:T(8,128)(2,1)S(1)} %get-tuple-element.147.refs_4_.refs_3_.refs_0_), channel_id=1, source_target_pairs={{0,2},{1,3},{2,0},{3,1},{4,6},{5,7},{6,4},{7,5},{8,10},{9,11},{10,... | collective-permute-start | bytes 1622024 | tf_op jit(solution)/shard_map/ppermute | solution.py:453
  6.1 1.9 %collective-permute-start.10 = (bf16[512,512]{1,0:T(8,128)(2,1)}, bf16[512,512]{1,0:T(8,128)(2,1)}, u32[]{:S(2)}, u32[]{:S(2)}) collective-permute-start(bf16[512,512]{1,0:T(8,128)(2,1)} %refs_7_.3), channel_id=1, source_target_pairs={{0,2},{1,3},{2,0},{3,1},{4,6},{5,7},{6,4},{7,5},{8,10},{9,11},{10,... | collective-permute-start | bytes 1572872 | tf_op jit(solution)/shard_map/ppermute | solution.py:453
  8.1 4.2 %attn_fwd_own.1 = (bf16[1024,256]{1,0:T(8,128)(2,1)S(1)}, bf16[1024,256]{1,0:T(8,128)(2,1)S(1)}, bf16[1024,256]{1,0:T(8,128)(2,1)S(1)}, bf16[1024,256]{1,0:T(8,1...) custom-call(s32[4]{0:T(128)S(1)} %pad_add_fusion.refs_0_.scal, s32[1,32,2]{2,1,0:T(8,128)S(1)} %copy.37.refs_1_, ...), custom_call_target="tpu_custom_call" | custom-call | flops 10000000000 | bytes 100000000 | tf_op jit(solution)/shard_map/attn_fwd_own/pallas_call | solution.py:470
  12.3 5.9 %collective-permute-done.1.refs_4_.bias.refs_2_ = bf16[528,512]{1,0:T(8,128)(2,1)S(1)} collective-permute-done((bf16[528,512]{1,0:T(8,128)(2,1)S(1)}, bf16[528,512]{1,0:T(8,128)(2,1)S(1)}, u32[]{:S(2)}, u32[]{:S(2)}) %collective-permute-start.1) | collective-permute-done | bytes 540704 | tf_op jit(solution)/shard_map/ppermute | solution.py:453
  18.2 2.6 %attn_fwd_y.1 = (bf16[1024,128]{1,0:T(8,128)(2,1)S(1)}, bf16[1024,128]{1,0:T(8,128)(2,1)S(1)}, bf16[1024,128]{1,0:T(8,128)(2,1)S(1)}, bf16[1024,128]{1,0:T(8,128...) custom-call(s32[4]{0:T(128)S(1)} %pad_add_fusion.refs_0_.scal, s32[1,32,2]{2,1,0:T(8,128)S(1)} %copy.37.refs_1_, ...), custom_call_target="tpu_custom_call" | custom-call | flops 10000000000 | bytes 100000000 | tf_op jit(solution)/shard_map/attn_fwd_y/pallas_call | solution.py:470
  21.5 3.5 %attn_fwd_yc.1 = (bf16[1024,128]{1,0:T(8,128)(2,1)S(1)}, bf16[1024,128]{1,0:T(8,128)(2,1)S(1)}, bf16[1024,128]{1,0:T(8,128)(2,1)S(1)}, bf16[1024,128]{1,0:T(8,12...) custom-call(s32[4]{0:T(128)S(1)} %pad_add_fusion.refs_0_.scal, ...), custom_call_target="tpu_custom_call" | custom-call | flops 10000000000 | bytes 100000000 | tf_op jit(solution)/shard_map/attn_fwd_yc/pallas_call | solution.py:470
  25.1 8.7 %mlp_own.1 = (bf16[528,512]{1,0:T(8,128)(2,1)S(1)}, bf16[528,512]{1,0:T(8,128)(2,1)S(1)}, bf16[512,512]{1,0:T(8,128)(2,1)S(1)}, bf16[512,512]{1,0:T(8,128)(2,1)S...) custom-call(bf16[1024,512]{1,0:T(8,128)(2,1)S(1)} %get-tuple-element.183.refs_0_.n2, ...), custom_call_target="tpu_custom_call" | custom-call | flops 10000000000 | bytes 100000000 | tf_op jit(solution)/shard_map/mlp_own/pallas_call | solution.py:470
  34.8 2.7 %mlp_up_y.1 = (bf16[1024,512]{1,0:T(8,128)(2,1)S(1)}, f32[1024,512]{1,0:T(8,128)S(1)}, bf16[512,512]{1,0:T(8,128)(2,1)S(1)}) custom-call(bf16[1024,512]{1,0:T(8,128)(2,1)S(1)} %get-tuple-element.183.refs_0_.n2, bf16[1024,512]{1,0:T(8,128)(2,1)S(1)} %copy-done.1, bf16[528,512]{1,0:T(8,128)(2,1)S(1)} %collective-permute-done.1.refs_4_.bias.refs_2_, ...), custom_call_target="tpu_custom_call" | custom-call | flops 10000000000 | bytes 100000000 | tf_op jit(solution)/shard_map/mlp_up_y/pallas_call | solution.py:470
  37.6 1.7 %mlp_up_yc.1 = (bf16[1024,512]{1,0:T(8,128)(2,1)S(1)}, f32[1024,512]{1,0:T(8,128)S(1)}, bf16[512,512]{1,0:T(8,128)(2,1)S(1)}) custom-call(bf16[1024,512]{1,0:T(8,128)(2,1)S(1)} %get-tuple-element.183.refs_0_.n2, bf16[1024,512]{1,0:T(8,128)(2,1)S(1)} %copy-done.1, bf16[528,512]{1,0:T(8,128)(2,1)S(1)} %collective-permute-done.2.refs_4_.bias.refs_3_, ...), custom_call_target="tpu_custom_call" | custom-call | flops 10000000000 | bytes 100000000 | tf_op jit(solution)/shard_map/mlp_up_yc/pallas_call | solution.py:470
  40.4 2.1 %collective-permute-start.14 = (bf16[272,512]{1,0:T(8,128)(2,1)S(1)}, bf16[272,512]{1,0:T(8,128)(2,1)S(1)}, u32[]{:S(2)}, u32[]{:S(2)}) collective-permute-start(bf16[272,512]{1,0:T(8,128)(2,1)S(1)} %get-tuple-element.173), channel_id=1, source_target_pairs={{0,4},{1,5},{2,6},{3,7},{4,0},{5,1},{6,2},{7,3},{8,12},{9,13},{10,... | collective-permute-start | bytes 835592 | tf_op jit(solution)/shard_map/ppermute | solution.py:453
  44.9 3.6 %mlp_down_y.1 = (bf16[528,512]{1,0:T(8,128)(2,1)S(1)}, f32[1024,512]{1,0:T(8,128)S(1)}, f32[1024,512]{1,0:T(8,128)S(1)}) custom-call(bf16[1024,512]{1,0:T(8,128)(2,1)S(1)} %get-tuple-element.183.refs_0_.n2, bf16[1024,512]{1,0:T(8,128)(2,1)S(1)} %copy-done.1, bf16[1024,512]{1,0:T(8,128)(2,1)S(1)} %get-tuple-element.177.act, ...), custom_call_target="tpu_custom_call" | custom-call | flops 10000000000 | bytes 100000000 | tf_op jit(solution)/shard_map/mlp_down_y/pallas_call | solution.py:470
  48.5 2.6 %mlp_down_yc.1 = (bf16[528,512]{1,0:T(8,128)(2,1)S(1)}, f32[1024,512]{1,0:T(8,128)S(1)}, f32[1024,512]{1,0:T(8,128)S(1)}) custom-call(bf16[1024,512]{1,0:T(8,128)(2,1)S(1)} %get-tuple-element.183.refs_0_.n2, bf16[1024,512]{1,0:T(8,128)(2,1)S(1)} %copy-done.1, bf16[1024,512]{1,0:T(8,128)(2,1)S(1)} %get-tuple-element.184.act, ...), custom_call_target="tpu_custom_call" | custom-call | flops 10000000000 | bytes 100000000 | tf_op jit(solution)/shard_map/mlp_down_yc/pallas_call | solution.py:470
  51.7 4.5 %ln2_bwd.1 = (bf16[1024,512]{1,0:T(8,128)(2,1)}, f32[1024,512]{1,0:T(8,128)S(1)}, bf16[1024,512]{1,0:T(8,128)(2,1)S(1)}, bf16[1024,512]{1,0:T(8,128)(2,1)S(1)}, f32[8,512]{1,0:T(8,128)S(1)}) custom-call(f32[1024,512]{1,0:T(8,128)S(1)} %get-tuple-element.189.hid, f32[1024,512]{1,0:T(8,128)S(1)} %get-tuple-element.190.mlp, ...), custom_call_target="tpu_custom_call" | custom-call | flops 10000000000 | bytes 100000000 | tf_op jit(solution)/shard_map/ln2_bwd/pallas_call | solution.py:470
  59.8 3.2 %attn_core_bwd.1 = (bf16[1024,512]{1,0:T(8,128)(2,1)S(1)}, bf16[1024,512]{1,0:T(8,128)(2,1)S(1)}, bf16[1024,512]{1,0:T(8,128)(2,1)S(1)}) custom-call(bf16[1024,256]{1,0:T(8,128)(2,1)S(1)} %get-tuple-element.148.refs_0_, bf16[1024,256]{1,0:T(8,128)(2,1)S(1)} %get-tuple-element.193.refs_1_, bf16[1024,256]{1,0:T(8,128)(2,1)S(1)} %get-tuple-element.194.refs_2_, ...), custom_call_target="tpu_custom_call" | custom-call | flops 1000000000 | bytes 100000000 | tf_op jit(solution)/shard_map/attn_core_bwd/pallas_call | solution.py:470
  63.0 4.8 %attn_dx.1 = (bf16[1024,512]{1,0:T(8,128)(2,1)}, f32[8,512]{1,0:T(8,128)S(1)}) custom-call(bf16[1024,512]{1,0:T(8,128)(2,1)S(1)} %copy-done, f32[1024,512]{1,0:T(8,128)S(1)} %get-tuple-element.212.dh, bf16[1024,512]{1,0:T(8,128)(2,1)S(1)} %get-tuple-element.225.dq, bf16[1024,512]{1,0:T(8,128)(2,1)S(1)} %get-tuple-element.213.dk, ...), custom_call_target="tpu_custom_call" | custom-call | flops 1000000000 | bytes 100000000 | tf_op jit(solution)/shard_map/attn_dx/pallas_call | solution.py:470
  72.7 1.6 %collective-permute-start.19 = (bf16[128,512]{1,0:T(8,128)(2,1)S(1)}, bf16[128,512]{1,0:T(8,128)(2,1)S(1)}, u32[]{:S(2)}, u32[]{:S(2)}) collective-permute-start(bf16[128,512]{1,0:T(8,128)(2,1)S(1)} %get-tuple-element.230), channel_id=1, source_target_pairs={{0,8},{1,9},{2,10},{3,11},{4,12},{5,13},{6,14},{7,15},{8,0},{9,1},... | collective-permute-start | bytes 393224 | tf_op jit(solution)/shard_map/ppermute | solution.py:453
  79.8 2.6 %collective-permute-start.23 = (bf16[128,512]{1,0:T(8,128)(2,1)S(1)}, bf16[128,512]{1,0:T(8,128)(2,1)S(1)}, u32[]{:S(2)}, u32[]{:S(2)}) collective-permute-start(bf16[128,512]{1,0:T(8,128)(2,1)S(1)} %add_z.6.refs_1_), channel_id=1, source_target_pairs={{0,16},{1,17},{2,18},{3,19},{4,20},{5,21},{6,22},{7,23},{8,24},{9,... | collective-permute-start | bytes 393224 | tf_op jit(solution)/shard_map/ppermute | solution.py:453
  87.2 2.6 %collective-permute-start.28 = (bf16[144,512]{1,0:T(8,128)(2,1)S(1)}, bf16[144,512]{1,0:T(8,128)(2,1)S(1)}, u32[]{:S(2)}, u32[]{:S(2)}) collective-permute-start(bf16[144,512]{1,0:T(8,128)(2,1)S(1)} %add_z.7.refs_1_), channel_id=1, source_target_pairs={{0,16},{1,17},{2,18},{3,19},{4,20},{5,21},{6,22},{7,23},{8,24},{9,... | collective-permute-start | bytes 442376 | tf_op jit(solution)/shard_map/ppermute | solution.py:453
  91.9 3.1 %collective-permute-done.24.refs_2_ = bf16[144,512]{1,0:T(8,128)(2,1)S(1)} collective-permute-done((bf16[144,512]{1,0:T(8,128)(2,1)S(1)}, bf16[144,512]{1,0:T(8,128)(2,1)S(1)}, u32[]{:S(2)}, u32[]{:S(2)}) %collective-permute-start.24) | collective-permute-done | bytes 147488 | tf_op jit(solution)/shard_map/ppermute | solution.py:453
  96.3 2.4 %collective-permute-done.26.other = bf16[128,512]{1,0:T(8,128)(2,1)S(1)} collective-permute-done((bf16[128,512]{1,0:T(8,128)(2,1)S(1)}, bf16[128,512]{1,0:T(8,128)(2,1)S(1)}, u32[]{:S(2)}, u32[]{:S(2)}) %collective-permute-start.26) | collective-permute-done | bytes 131104 | tf_op jit(solution)/shard_map/ppermute | solution.py:453
  103.5 2.0 %collective-permute-start.30 = (bf16[144,512]{1,0:T(8,128)(2,1)S(1)}, bf16[144,512]{1,0:T(8,128)(2,1)S(1)}, u32[]{:S(2)}, u32[]{:S(2)}) collective-permute-start(bf16[144,512]{1,0:T(8,128)(2,1)S(1)} %add_z.9.refs_1_), channel_id=1, source_target_pairs={{0,16},{1,17},{2,18},{3,19},{4,20},{5,21},{6,22},{7,23},{8,24},{9,... | collective-permute-start | bytes 442376 | tf_op jit(solution)/shard_map/ppermute | solution.py:453
  106.1 2.5 %collective-permute-done.29.other = bf16[128,512]{1,0:T(8,128)(2,1)S(1)} collective-permute-done((bf16[128,512]{1,0:T(8,128)(2,1)S(1)}, bf16[128,512]{1,0:T(8,128)(2,1)S(1)}, u32[]{:S(2)}, u32[]{:S(2)}) %collective-permute-start.29) | collective-permute-done | bytes 131104 | tf_op jit(solution)/shard_map/ppermute | solution.py:453
  113.6 2.4 %collective-permute-start.33 = (bf16[128,512]{1,0:T(8,128)(2,1)S(1)}, bf16[128,512]{1,0:T(8,128)(2,1)S(1)}, u32[]{:S(2)}, u32[]{:S(2)}) collective-permute-start(bf16[128,512]{1,0:T(8,128)(2,1)S(1)} %get-tuple-element.264.refs_1_), channel_id=1, source_target_pairs={{0,8},{1,9},{2,10},{3,11},{4,12},{5,13},{6,14},{7,15},{8,0},{9,1},... | collective-permute-start | bytes 393224 | tf_op jit(solution)/shard_map/ppermute | solution.py:453
  116.5 1.7 %final_down.1 = f32[512,512]{1,0:T(8,128)} custom-call(s32[4]{0:T(128)S(1)} %pad_add_fusion.refs_0_.scal, bf16[256,512]{1,0:T(8,128)(2,1)S(1)} %join_d.1.refs_1_, bf16[256,512]{1,0:T(8,128)(2,1)S(1)} %collective-permute-done.31.refs_2_), custom_call_target="tpu_custom_call" | custom-call | flops 10000000000 | bytes 100000000 | tf_op jit(solution)/shard_map/final_down/pallas_call | solution.py:470
  (97 shorter events, 45.1 us)
Async XLA Ops:
  2.1 16.1 %collective-permute-start.1 = (bf16[528,512]{1,0:T(8,128)(2,1)S(1)}, bf16[528,512]{1,0:T(8,128)(2,1)S(1)}, u32[]{:S(2)}, u32[]{:S(2)}) collective-permute-start(bf16[528,512]{1,0:T(8,128)(2,1)S(1)} %get-tuple-element.147.refs_4_.refs_3_.refs_0_), channel_id=1, source_target_pairs={{0,2},{1,3},{2,0},{3,1},{4,6},{5,7},{6,4},{7,5},{8,10},{9,11},{10,... | collective-permute-start | bytes 1622024 | tf_op jit(solution)/shard_map/ppermute | solution.py:453
  5.9 28.4 %collective-permute-start.5 = (bf16[512,512]{1,0:T(8,128)(2,1)}, bf16[512,512]{1,0:T(8,128)(2,1)}, u32[]{:S(2)}, u32[]{:S(2)}) collective-permute-start(bf16[512,512]{1,0:T(8,128)(2,1)} %refs_5_.3), channel_id=1, source_target_pairs={{0,2},{1,3},{2,0},{3,1},{4,6},{5,7},{6,4},{7,5},{8,10},{9,11},{10,... | collective-permute-start | bytes 1572872 | tf_op jit(solution)/shard_map/ppermute | solution.py:453
  6.1 38.8 %collective-permute-start.10 = (bf16[512,512]{1,0:T(8,128)(2,1)}, bf16[512,512]{1,0:T(8,128)(2,1)}, u32[]{:S(2)}, u32[]{:S(2)}) collective-permute-start(bf16[512,512]{1,0:T(8,128)(2,1)} %refs_7_.3), channel_id=1, source_target_pairs={{0,2},{1,3},{2,0},{3,1},{4,6},{5,7},{6,4},{7,5},{8,10},{9,11},{10,... | collective-permute-start | bytes 1572872 | tf_op jit(solution)/shard_map/ppermute | solution.py:453
  33.8 8.7 %collective-permute-start.8 = (bf16[512,512]{1,0:T(8,128)(2,1)S(1)}, bf16[512,512]{1,0:T(8,128)(2,1)S(1)}, u32[]{:S(2)}, u32[]{:S(2)}) collective-permute-start(bf16[512,512]{1,0:T(8,128)(2,1)S(1)} %get-tuple-element.163), channel_id=1, source_target_pairs={{0,1},{1,0},{2,3},{3,2},{4,5},{5,4},{6,7},{7,6},{8,9},{9,8},{10,11... | collective-permute-start | bytes 1572872 | tf_op jit(solution)/shard_map/ppermute | solution.py:453
  40.4 27.4 %collective-permute-start.14 = (bf16[272,512]{1,0:T(8,128)(2,1)S(1)}, bf16[272,512]{1,0:T(8,128)(2,1)S(1)}, u32[]{:S(2)}, u32[]{:S(2)}) collective-permute-start(bf16[272,512]{1,0:T(8,128)(2,1)S(1)} %get-tuple-element.173), channel_id=1, source_target_pairs={{0,4},{1,5},{2,6},{3,7},{4,0},{5,1},{6,2},{7,3},{8,12},{9,13},{10,... | collective-permute-start | bytes 835592 | tf_op jit(solution)/shard_map/ppermute | solution.py:453
  43.3 14.5 %collective-permute-start.13 = (bf16[512,512]{1,0:T(8,128)(2,1)S(1)}, bf16[512,512]{1,0:T(8,128)(2,1)S(1)}, u32[]{:S(2)}, u32[]{:S(2)}) collective-permute-start(bf16[512,512]{1,0:T(8,128)(2,1)S(1)} %get-tuple-element.175), channel_id=1, source_target_pairs={{0,2},{1,3},{2,0},{3,1},{4,6},{5,7},{6,4},{7,5},{8,10},{9,11},{10,... | collective-permute-start | bytes 1572872 | tf_op jit(solution)/shard_map/ppermute | solution.py:453
  56.9 10.9 %collective-permute-start.15 = (bf16[272,512]{1,0:T(8,128)(2,1)S(1)}, bf16[272,512]{1,0:T(8,128)(2,1)S(1)}, u32[]{:S(2)}, u32[]{:S(2)}) collective-permute-start(bf16[272,512]{1,0:T(8,128)(2,1)S(1)} %get-tuple-element.199), channel_id=1, source_target_pairs={{0,4},{1,5},{2,6},{3,7},{4,0},{5,1},{6,2},{7,3},{8,12},{9,13},{10,... | collective-permute-start | bytes 835592 | tf_op jit(solution)/shard_map/ppermute | solution.py:453
  58.5 13.5 %collective-permute-start.17 = (bf16[256,512]{1,0:T(8,128)(2,1)S(1)}, bf16[256,512]{1,0:T(8,128)(2,1)S(1)}, u32[]{:S(2)}, u32[]{:S(2)}) collective-permute-start(bf16[256,512]{1,0:T(8,128)(2,1)S(1)} %get-tuple-element.201), channel_id=1, source_target_pairs={{0,4},{1,5},{2,6},{3,7},{4,0},{5,1},{6,2},{7,3},{8,12},{9,13},{10,... | collective-permute-start | bytes 786440 | tf_op jit(solution)/shard_map/ppermute | solution.py:453
  68.5 9.3 %collective-permute-start.18 = (bf16[272,512]{1,0:T(8,128)(2,1)S(1)}, bf16[272,512]{1,0:T(8,128)(2,1)S(1)}, u32[]{:S(2)}, u32[]{:S(2)}) collective-permute-start(bf16[272,512]{1,0:T(8,128)(2,1)S(1)} %get-tuple-element.220), channel_id=1, source_target_pairs={{0,2},{1,3},{2,0},{3,1},{4,6},{5,7},{6,4},{7,5},{8,10},{9,11},{10,... | collective-permute-start | bytes 835592 | tf_op jit(solution)/shard_map/ppermute | solution.py:453
  72.7 6.5 %collective-permute-start.19 = (bf16[128,512]{1,0:T(8,128)(2,1)S(1)}, bf16[128,512]{1,0:T(8,128)(2,1)S(1)}, u32[]{:S(2)}, u32[]{:S(2)}) collective-permute-start(bf16[128,512]{1,0:T(8,128)(2,1)S(1)} %get-tuple-element.230), channel_id=1, source_target_pairs={{0,8},{1,9},{2,10},{3,11},{4,12},{5,13},{6,14},{7,15},{8,0},{9,1},... | collective-permute-start | bytes 393224 | tf_op jit(solution)/shard_map/ppermute | solution.py:453
  75.0 8.8 %collective-permute-start.20 = (bf16[272,512]{1,0:T(8,128)(2,1)S(1)}, bf16[272,512]{1,0:T(8,128)(2,1)S(1)}, u32[]{:S(2)}, u32[]{:S(2)}) collective-permute-start(bf16[272,512]{1,0:T(8,128)(2,1)S(1)} %get-tuple-element.236), channel_id=1, source_target_pairs={{0,2},{1,3},{2,0},{3,1},{4,6},{5,7},{6,4},{7,5},{8,10},{9,11},{10,... | collective-permute-start | bytes 835592 | tf_op jit(solution)/shard_map/ppermute | solution.py:453
  76.9 8.2 %collective-permute-start.21 = (bf16[256,512]{1,0:T(8,128)(2,1)S(1)}, bf16[256,512]{1,0:T(8,128)(2,1)S(1)}, u32[]{:S(2)}, u32[]{:S(2)}) collective-permute-start(bf16[256,512]{1,0:T(8,128)(2,1)S(1)} %get-tuple-element.238), channel_id=1, source_target_pairs={{0,4},{1,5},{2,6},{3,7},{4,0},{5,1},{6,2},{7,3},{8,12},{9,13},{10,... | collective-permute-start | bytes 786440 | tf_op jit(solution)/shard_map/ppermute | solution.py:453
  78.4 8.2 %collective-permute-start.22 = (bf16[144,512]{1,0:T(8,128)(2,1)S(1)}, bf16[144,512]{1,0:T(8,128)(2,1)S(1)}, u32[]{:S(2)}, u32[]{:S(2)}) collective-permute-start(bf16[144,512]{1,0:T(8,128)(2,1)S(1)} %get-tuple-element.240), channel_id=1, source_target_pairs={{0,8},{1,9},{2,10},{3,11},{4,12},{5,13},{6,14},{7,15},{8,0},{9,1},... | collective-permute-start | bytes 442376 | tf_op jit(solution)/shard_map/ppermute | solution.py:453
  79.8 10.9 %collective-permute-start.23 = (bf16[128,512]{1,0:T(8,128)(2,1)S(1)}, bf16[128,512]{1,0:T(8,128)(2,1)S(1)}, u32[]{:S(2)}, u32[]{:S(2)}) collective-permute-start(bf16[128,512]{1,0:T(8,128)(2,1)S(1)} %add_z.6.refs_1_), channel_id=1, source_target_pairs={{0,16},{1,17},{2,18},{3,19},{4,20},{5,21},{6,22},{7,23},{8,24},{9,... | collective-permute-start | bytes 393224 | tf_op jit(solution)/shard_map/ppermute | solution.py:453
  85.7 6.2 %collective-permute-start.25 = (bf16[128,512]{1,0:T(8,128)(2,1)S(1)}, bf16[128,512]{1,0:T(8,128)(2,1)S(1)}, u32[]{:S(2)}, u32[]{:S(2)}) collective-permute-start(bf16[128,512]{1,0:T(8,128)(2,1)S(1)} %get-tuple-element.248), channel_id=1, source_target_pairs={{0,2},{1,3},{2,0},{3,1},{4,6},{5,7},{6,4},{7,5},{8,10},{9,11},{10,... | collective-permute-start | bytes 393224 | tf_op jit(solution)/shard_map/ppermute | solution.py:453
  87.2 14.2 %collective-permute-start.28 = (bf16[144,512]{1,0:T(8,128)(2,1)S(1)}, bf16[144,512]{1,0:T(8,128)(2,1)S(1)}, u32[]{:S(2)}, u32[]{:S(2)}) collective-permute-start(bf16[144,512]{1,0:T(8,128)(2,1)S(1)} %add_z.7.refs_1_), channel_id=1, source_target_pairs={{0,16},{1,17},{2,18},{3,19},{4,20},{5,21},{6,22},{7,23},{8,24},{9,... | collective-permute-start | bytes 442376 | tf_op jit(solution)/shard_map/ppermute | solution.py:453
  91.2 7.6 %collective-permute-start.26 = (bf16[128,512]{1,0:T(8,128)(2,1)S(1)}, bf16[128,512]{1,0:T(8,128)(2,1)S(1)}, u32[]{:S(2)}, u32[]{:S(2)}) collective-permute-start(bf16[128,512]{1,0:T(8,128)(2,1)S(1)} %add_z.8.mine), channel_id=1, source_target_pairs={{0,8},{1,9},{2,10},{3,11},{4,12},{5,13},{6,14},{7,15},{8,0},{9,1},... | collective-permute-start | bytes 393224 | tf_op jit(solution)/shard_map/ppermute | solution.py:453
  102.0 6.6 %collective-permute-start.29 = (bf16[128,512]{1,0:T(8,128)(2,1)S(1)}, bf16[128,512]{1,0:T(8,128)(2,1)S(1)}, u32[]{:S(2)}, u32[]{:S(2)}) collective-permute-start(bf16[128,512]{1,0:T(8,128)(2,1)S(1)} %get-tuple-element.258.mine), channel_id=1, source_target_pairs={{0,8},{1,9},{2,10},{3,11},{4,12},{5,13},{6,14},{7,15},{8,0},{9,1},... | collective-permute-start | bytes 393224 | tf_op jit(solution)/shard_map/ppermute | solution.py:453
  102.7 13.8 %collective-permute-start.31 = (bf16[256,512]{1,0:T(8,128)(2,1)S(1)}, bf16[256,512]{1,0:T(8,128)(2,1)S(1)}, u32[]{:S(2)}, u32[]{:S(2)}) collective-permute-start(bf16[256,512]{1,0:T(8,128)(2,1)S(1)} %join_d.1.refs_1_), channel_id=1, source_target_pairs={{0,4},{1,5},{2,6},{3,7},{4,0},{5,1},{6,2},{7,3},{8,12},{9,13},{10,... | collective-permute-start | bytes 786440 | tf_op jit(solution)/shard_map/ppermute | solution.py:453
  103.5 8.3 %collective-permute-start.30 = (bf16[144,512]{1,0:T(8,128)(2,1)S(1)}, bf16[144,512]{1,0:T(8,128)(2,1)S(1)}, u32[]{:S(2)}, u32[]{:S(2)}) collective-permute-start(bf16[144,512]{1,0:T(8,128)(2,1)S(1)} %add_z.9.refs_1_), channel_id=1, source_target_pairs={{0,16},{1,17},{2,18},{3,19},{4,20},{5,21},{6,22},{7,23},{8,24},{9,... | collective-permute-start | bytes 442376 | tf_op jit(solution)/shard_map/ppermute | solution.py:453
  109.2 10.1 %collective-permute-start.32 = (bf16[256,512]{1,0:T(8,128)(2,1)S(1)}, bf16[256,512]{1,0:T(8,128)(2,1)S(1)}, u32[]{:S(2)}, u32[]{:S(2)}) collective-permute-start(bf16[256,512]{1,0:T(8,128)(2,1)S(1)} %join_u.1.refs_1_), channel_id=1, source_target_pairs={{0,4},{1,5},{2,6},{3,7},{4,0},{5,1},{6,2},{7,3},{8,12},{9,13},{10,... | collective-permute-start | bytes 786440 | tf_op jit(solution)/shard_map/ppermute | solution.py:453
  112.4 8.4 %collective-permute-start.35 = (bf16[128,512]{1,0:T(8,128)(2,1)S(1)}, bf16[128,512]{1,0:T(8,128)(2,1)S(1)}, u32[]{:S(2)}, u32[]{:S(2)}) collective-permute-start(bf16[128,512]{1,0:T(8,128)(2,1)S(1)} %get-tuple-element.264.refs_1_), channel_id=1, source_target_pairs={{0,12},{1,13},{2,14},{3,15},{4,8},{5,9},{6,10},{7,11},{8,4},{9,5},... | collective-permute-start | bytes 393224 | tf_op jit(solution)/shard_map/ppermute | solution.py:453
  112.6 8.3 %collective-permute-start.34 = (bf16[128,512]{1,0:T(8,128)(2,1)S(1)}, bf16[128,512]{1,0:T(8,128)(2,1)S(1)}, u32[]{:S(2)}, u32[]{:S(2)}) collective-permute-start(bf16[128,512]{1,0:T(8,128)(2,1)S(1)} %get-tuple-element.264.refs_1_), channel_id=1, source_target_pairs={{0,4},{1,5},{2,6},{3,7},{4,0},{5,1},{6,2},{7,3},{8,12},{9,13},{10,... | collective-permute-start | bytes 393224 | tf_op jit(solution)/shard_map/ppermute | solution.py:453
  113.6 7.3 %collective-permute-start.33 = (bf16[128,512]{1,0:T(8,128)(2,1)S(1)}, bf16[128,512]{1,0:T(8,128)(2,1)S(1)}, u32[]{:S(2)}, u32[]{:S(2)}) collective-permute-start(bf16[128,512]{1,0:T(8,128)(2,1)S(1)} %get-tuple-element.264.refs_1_), channel_id=1, source_target_pairs={{0,8},{1,9},{2,10},{3,11},{4,12},{5,13},{6,14},{7,15},{8,0},{9,1},... | collective-permute-start | bytes 393224 | tf_op jit(solution)/shard_map/ppermute | solution.py:453
  (15 other events, 60.2 us)

commit v3 on v2

--- a/solution.py
+++ b/solution.py
@@ -14,7 +14,7 @@
 BR = 256
 BIAS = 16
 EPS = 1e-5
-WEIGHTS = {"attn_dw_sent": 1, "attn_core_bwd": 1, "attn_dx": 1, "add_d_x": 0, "add_l_y": 0, "add_h_x": 0, "add_u_y": 0}
+WEIGHTS = {"attn_dw_sent": 1, "attn_core_bwd": 1, "attn_dx": 1, "add_d_x": 0, "add_ud_x": 0, "add_l_y": 0, "add_h_x": 0, "add_lyhx": 0, "add_u_y": 0, "add_last_d": 0}
 LN1_G, LN1_B, B_OUT, LN2_G, LN2_B, B_DOWN, B_UP, B_QV = range(8)
 SMEM = functools.partial(pl.BlockSpec, memory_space=pltpu.SMEM)
 VMEM = functools.partial(pl.BlockSpec, memory_space=pltpu.VMEM)
@@ -46,6 +46,23 @@
 
 def whole(shape):
     return pl.BlockSpec(shape, lambda *i: (0,) * len(shape))
+
+
+def fetch(src, dst, sems, at=0, pieces=4):
+    n = dst.shape[0] // pieces
+    copies = [
+        pltpu.make_async_copy(src.at[i * n : (i + 1) * n, :], dst.at[i * n : (i + 1) * n, :], sems.at[at + i])
+        for i in range(pieces)
+    ]
+    for c in copies:
+        c.start()
+    return copies
+
+
+def await_all(*groups):
+    for group in groups:
+        for c in group:
+            c.wait()
 
 
 def normalise(v):
@@ -118,8 +135,16 @@
 
 
 def attn_fwd_kernel(shares, first, last, *refs):
-    (scal, lens, n1, base), w = refs[:4], refs[4 : 4 + shares]
-    vecs, (q_o, k_o, v_o, att_o, pt_o, hid_o), n2_o = refs[4 + shares], refs[5 + shares : 11 + shares], refs[-1]
+    (scal, lens, n1, base), w = refs[:4], list(refs[4 : 4 + shares])
+    vecs, (q_o, k_o, v_o, att_o, pt_o, hid_o), n2_o = refs[4 + shares], refs[5 + shares + 2 * first : 11 + shares + 2 * first], refs[-1]
+    if first:
+        up_in, down_in, wa_o, up_o, down_o, sems = refs[7], refs[8], *refs[-4:]
+        fetched = fetch(w[1], wa_o, sems, pieces=3)
+        brought = [pltpu.make_async_copy(up_in, up_o, sems.at[3]), pltpu.make_async_copy(down_in, down_o, sems.at[4])]
+        for c in brought:
+            c.start()
+        await_all(fetched)
+        w[1] = wa_o
     slots = n1.shape[0] // SLOT
 
     for c in range(shares):
@@ -153,6 +178,8 @@
         wo = jnp.concatenate([w[c][b * 128 : (b + 1) * 128, 384:512] for b in range(4)], 1)
         hid += dot(att_o[:, c * 128 : (c + 1) * 128], wo)
     hid_o[...] = hid
+    if first:
+        await_all(brought)
     if last:
 
         def tile(m, _):
@@ -169,43 +196,37 @@
     return u * phi, phi + u * (jnp.exp(-0.5 * (u * u)) * 0.3989422804014327)
 
 
-def mlp_kernel(first, *refs):
-    if first:
-        (n2, cot, ba, bb, ua, ub, da, db, gua, gub, gda, gdb, out, dn2, act_s, gup_s) = refs
+def share_kernel(first, n2, cot, wa, u, d, *refs):
+    if not first:
+        out_i, dn2_i, up_in, refs, (up_o, act_s, gup_s, sem) = *refs[:3], refs[3:8], refs[8:]
+        brought = pltpu.make_async_copy(up_in, up_o, sem.at[0])
+        brought.start()
     else:
-        (n2, cot, ba, bb, ua, ub, da, db, out_i, dn2_i, gua, gub, gda, gdb, out, dn2, act_s, gup_s) = refs
-    bias = [b[D : D + BIAS, :].astype(F32)[1:2] for b in (ba, bb)]
+        act_s, gup_s = refs[5:]
+    gu_o, gd_o, out, dn2, bu_o = refs[:5]
+    bias = wa[D : D + BIAS, :].astype(F32)[1:2]
 
     def tile(m, sums):
         here = pl.ds(pl.multiple_of(m * BR, BR), BR)
         n, c = n2[here, :], cot[here, :]
-        new, acts, gups = [], [], []
-        for j, (u, d) in enumerate(((ua, da), (ub, db))):
-            up = dot(n, u[...]) + bias[j]
-            dact = dot_nt(c, d[...])
-            act, slope = gelu_pair(up)
-            gup = (slope * dact).astype(BF)
-            act = act.astype(BF)
-            act_s[here, j * D : (j + 1) * D] = act
-            gup_s[here, j * D : (j + 1) * D] = gup
-            new.append(sums[j] + jnp.sum(gup.astype(F32), 0, keepdims=True))
-            acts.append(act)
-            gups.append(gup)
-        o = dot(acts[0], da[...]) + dot(acts[1], db[...])
-        e = dot_nt(gups[0], ua[...]) + dot_nt(gups[1], ub[...])
+        up = dot(n, u[...]) + bias
+        dact = dot_nt(c, d[...])
+        act, slope = gelu_pair(up)
+        gup = (slope * dact).astype(BF)
+        act = act.astype(BF)
+        act_s[here, :] = act
+        gup_s[here, :] = gup
+        o, e = dot(act, d[...]), dot_nt(gup, u[...])
         out[here, :] = o if first else out_i[here, :] + o
         dn2[here, :] = e if first else dn2_i[here, :] + e
-        return tuple(new)
-
-    zero = jnp.zeros((1, D), F32)
-    sums = lax.fori_loop(0, n2.shape[0] // BR, tile, (zero, zero), unroll=True)
-    row = lax.broadcasted_iota(jnp.int32, (BIAS, D), 0)
-    for j, (gu_o, gd_o) in enumerate(((gua, gda), (gub, gdb))):
-        cols = slice(j * D, (j + 1) * D)
-        gu_o[0:D, :] = dot_tn(n2[...], gup_s[:, cols]).astype(BF)
-        gd_o[0:D, :] = dot_tn(cot[...], act_s[:, cols]).astype(BF)
-        high = sums[j].astype(BF).astype(F32)
-        gu_o[D : D + BIAS, :] = jnp.where(row == 0, high, jnp.where(row == 8, sums[j] - high, 0.0)).astype(BF)
+        return sums + jnp.sum(gup.astype(F32), 0, keepdims=True)
+
+    sums = lax.fori_loop(0, n2.shape[0] // BR, tile, jnp.zeros((1, D), F32), unroll=True)
+    gu_o[...] = dot_tn(n2[...], gup_s[...]).astype(BF)
+    gd_o[...] = dot_tn(cot[...], act_s[...]).astype(BF)
+    bu_o[...] = jnp.broadcast_to(sums, (8, D))
+    if not first:
+        brought.wait()
 
 
 def act_kernel(n2, cot, bias, u, act_o, slope_o, gd_o):
@@ -222,7 +243,7 @@
     gd_o[...] = dot_tn(cot[...], act_o[...]).astype(BF)
 
 
-def down_kernel(n2, cot, act, slope, u, d, out_i, dn2_i, gu_o, out, dn2, gup_s):
+def down_kernel(n2, cot, act, slope, u, d, out_i, dn2_i, gu_o, out, dn2, bu_o, gup_s):
     def tile(m, sums):
         here = pl.ds(pl.multiple_of(m * BR, BR), BR)
         gup = (slope[here, :] * dot_nt(cot[here, :], d[...])).astype(BF)
@@ -232,8 +253,8 @@
         return sums + jnp.sum(gup.astype(F32), 0, keepdims=True)
 
     sums = lax.fori_loop(0, n2.shape[0] // BR, tile, jnp.zeros((1, D), F32), unroll=True)
-    gu_o[0:D, :] = dot_tn(n2[...], gup_s[...]).astype(BF)
-    gu_o[D : D + BIAS, :] = bias_block(jnp.concatenate([sums, jnp.zeros((7, D), F32)], 0))
+    gu_o[...] = dot_tn(n2[...], gup_s[...]).astype(BF)
+    bu_o[...] = jnp.broadcast_to(sums, (8, D))
 
 
 def total(sums, *adds):
@@ -295,8 +316,8 @@
     lax.fori_loop(0, datt.shape[0] // SLOT, slot, 0, unroll=True)
 
 
-def attn_dw_kernel(one, two, dq, dk, dv, n1, gat, shared, att_one, att_two, *ga):
-    gap, rest = jnp.zeros((1, 128), F32), shared[0:7, :]
+def attn_dw_kernel(one, two, dq, dk, dv, n1, gat, shared, bu_one, bu_two, att_one, att_two, *ga):
+    gap = jnp.zeros((1, 128), F32)
     grads = [[s[:, c * 128 : (c + 1) * 128] for s in (dq, dk, dv)] for c in (one, two)]
     sums = [[jnp.sum(g[j].astype(F32), 0, keepdims=True) for j in (0, 2)] for g in grads]
     g = dot_tn(n1[...], jnp.concatenate(grads[0] + grads[1], 1)).astype(BF)
@@ -307,7 +328,7 @@
         o[at : at + D, 0:384] = g[:, i * 384 : (i + 1) * 384]
         o[at : at + D, 384:512] = go[:, i * 128 : (i + 1) * 128]
         own = jnp.concatenate([sums[i][0], gap, sums[i][1], gap], 1)
-        o[at + D : at + D + BIAS, :] = bias_block(jnp.concatenate([own, rest], 0))
+        o[at + D : at + D + BIAS, :] = bias_block(jnp.concatenate([own, shared[0:6, :], (bu_one, bu_two)[i][0:1, :]], 0))
 
 
 def attn_dx_kernel(x, dh, dq, dk, dv, sums2, vecs, *refs):
@@ -342,10 +363,10 @@
         self.extra = BIAS if sums else 0
 
 
-def combine_kernel(parts, op, *refs):
+def combine_kernel(groups, *refs):
     scal, ins = refs[0], refs[1:]
-    n_in = 1 + max(i for part in parts for i, _ in part[1] + part[2])
-    ins, outs = ins[:n_in], ins[n_in:]
+    n_in = 1 + max(i for _, parts in groups for part in parts for i, _ in part[1] + part[2])
+    ins, rest = ins[:n_in], list(ins[n_in:])
 
     def summed(part, start, size):
         acc = None
@@ -361,35 +382,36 @@
             terms = [sum(terms[i + 1 : i + 2], terms[i]) for i in range(0, len(terms), 2)]
         return terms[0]
 
-    if op == "y":
-        for o, part in zip(outs, (parts[1], parts[0])):
-            n = part[0]
-            o[0:n, :] = summed(part, 0, n)
-            if part[2]:
-                o[n : n + BIAS, :] = bias_block(sums(part))
-        return
-    at, side = 0, 1
-    for part in parts:
-        n, biased = part[0], bool(part[2])
-        if op in ("all", "last"):
-            outs[0][at : at + n, :] = summed(part, 0, n)
-            at += n
-            if biased and op == "last":
-                outs[side][...] = sums(part)
-                side += 1
-            elif biased:
-                outs[0][at : at + BIAS, :] = bias_block(sums(part))
-                at += BIAS
-        else:
-            bit, h = scal[op], n // 2
-            outs[0][at : at + h, :] = summed(part, pl.multiple_of((1 - bit) * h, h), h)
-            outs[1][at : at + h, :] = summed(part, pl.multiple_of(bit * h, h), h)
-            at += h
-            if biased:
-                block = bias_block(sums(part))
-                for o in outs:
-                    o[at : at + BIAS, :] = block
-                at += BIAS
+    for op, parts in groups:
+        if op == "y":
+            for part in (parts[1], parts[0]):
+                o, n = rest.pop(0), part[0]
+                o[0:n, :] = summed(part, 0, n)
+                if part[2]:
+                    o[n : n + BIAS, :] = bias_block(sums(part))
+            continue
+        outs = [rest.pop(0) for _ in range(1 if op in ("all", "last") else 2)]
+        at = 0
+        for part in parts:
+            n, biased = part[0], bool(part[2])
+            if op in ("all", "last"):
+                outs[0][at : at + n, :] = summed(part, 0, n)
+                at += n
+                if biased and op == "last":
+                    rest.pop(0)[...] = sums(part)
+                elif biased:
+                    outs[0][at : at + BIAS, :] = bias_block(sums(part))
+                    at += BIAS
+            else:
+                bit, h = scal[op], n // 2
+                outs[0][at : at + h, :] = summed(part, pl.multiple_of((1 - bit) * h, h), h)
+                outs[1][at : at + h, :] = summed(part, pl.multiple_of(bit * h, h), h)
+                at += h
+                if biased:
+                    block = bias_block(sums(part))
+                    for o in outs:
+                        o[at : at + BIAS, :] = block
+                    at += BIAS
 
 
 def join_kernel(scal, mine, other, out):
@@ -458,12 +480,14 @@
     def hbm(v):
         return pltpu.with_memory_space_constraint(v, pltpu.HBM)
 
-    def call(kernel, name, out_shape, args, scratch=(), mib=16, in_hbm=False, weight=10):
+    def call(kernel, name, out_shape, args, scratch=(), mib=16, in_hbm=False, weight=10, anywhere=()):
         args = [real(a) for a in args]
         if last[0] is not scal:
-            i = max(range(len(args)), key=lambda j: args[j].size)
+            i = max((j for j in range(len(args)) if j not in anywhere), key=lambda j: args[j].size)
             args[i] = after(args[i], last[0])
         specs = [SMEM() if a.dtype == jnp.int32 else VMEM() for a in args]
+        for j in anywhere:
+            specs[j] = pl.BlockSpec(memory_space=pl.ANY)
         if in_hbm:
             args = [hbm(a) for a in args]
             specs = [pl.BlockSpec(memory_space=pltpu.HBM)] * len(args)
@@ -480,24 +504,31 @@
         last[0] = min(out, key=lambda o: o.size)
         return out
 
-    def combine(op, *parts, tag="z"):
-        arrays = []
-        for part in parts:
-            for array, _ in (*part.sources, *part.sums):
-                array = real(array)
-                if not any(array is known for known in arrays):
-                    arrays.append(array)
+    def combine_all(*groups, tag):
+        arrays, spec, shapes, counts = [], [], [], []
+        for op, parts in groups:
+            for p in parts:
+                for array, _ in (*p.sources, *p.sums):
+                    if not any(real(array) is known for known in arrays):
+                        arrays.append(real(array))
         place = lambda array: next(i for i, known in enumerate(arrays) if known is real(array))
-        spec = tuple((p.n, *(tuple((place(v), first) for v, first in w) for w in (p.sources, p.sums))) for p in parts)
-        if op == "y":
-            shapes = [sds((p.n + p.extra, D)) for p in (parts[1], parts[0])]
-        elif op == "all":
-            shapes = [sds((sum(p.n + p.extra for p in parts), D))]
-        elif op == "last":
-            shapes = [sds((sum(p.n for p in parts), D))] + [sds((8, D), F32) for p in parts if p.sums]
-        else:
-            shapes = [sds((sum(p.n // 2 + p.extra for p in parts), D))] * 2
-        return call(functools.partial(combine_kernel, spec, op), "add_" + tag, shapes, [scal, *arrays], mib=8)
+        for op, parts in groups:
+            spec.append((op, tuple((p.n, *(tuple((place(v), at) for v, at in w) for w in (p.sources, p.sums))) for p in parts)))
+            if op == "y":
+                new = [sds((p.n + p.extra, D)) for p in (parts[1], parts[0])]
+            elif op == "all":
+                new = [sds((sum(p.n + p.extra for p in parts), D))]
+            elif op == "last":
+                new = [sds((sum(p.n for p in parts), D))] + [sds((8, D), F32) for p in parts if p.sums]
+            else:
+                new = [sds((sum(p.n // 2 + p.extra for p in parts), D))] * 2
+            shapes += new
+            counts.append(len(new))
+        out = list(call(functools.partial(combine_kernel, tuple(spec)), "add_" + tag, shapes, [scal, *arrays], mib=8))
+        return [[out.pop(0) for _ in range(n)] for n in counts]
+
+    def combine(op, *parts, tag):
+        return combine_all((op, parts), tag=tag)[0]
 
     own, vecs = call(
         pack_kernel, "pack", [sds((D + BIAS, D)), sds((8, D), F32)],
@@ -516,9 +547,15 @@
         n = 128 * len(weights)
         shapes = [sds((rows, n))] * 4 + [sds((rows, 2 * n)), acc] + [wide] * last
         args = [scal, lengths, n1, hid, *weights, vecs]
-        return call(functools.partial(attn_fwd_kernel, len(weights), first, last), name, shapes, args)
-
-    *saved_0, att0, pt0, hid = attn_fwd("attn_fwd_own", [own, wa_c], x, first=True)
+        if first:
+            shapes += [sds((D + BIAS, D)), sds((D, D)), sds((D, D))]
+            args += [w_up, w_down]
+        return call(
+            functools.partial(attn_fwd_kernel, len(weights), first, last), name, shapes, args,
+            [pltpu.SemaphoreType.DMA((5,))] if first else [], anywhere=(5, 7, 8) if first else (),
+        )
+
+    *saved_0, att0, pt0, hid, wa_c, u_own, d_own = attn_fwd("attn_fwd_own", [own, wa_c], x, first=True)
     wa_y = after(wa_y, hid)
     wa_yc = swap(wa_y, t_mask=1)
     *saved_2, att2, pt2, hid = attn_fwd("attn_fwd_y", [wa_y], hid)
@@ -531,40 +568,45 @@
 
     h, q = D // 2, D // 4
     bits = [1 << b for b in range(2, n_dp.bit_length() - 1)]
-    gu1, gu0, gd1, gd0, out_sum, dn2 = call(
-        functools.partial(mlp_kernel, True), "mlp_own", [sds((D + BIAS, D))] * 2 + [sds((D, D))] * 2 + [acc] * 2,
-        [n2, cot, wa_c, own, wu_c, w_up, wd_c, w_down], [pltpu.VMEM((rows, 2 * D), BF)] * 2,
-    )
-    gd1, gu1 = swap(gd1, t_mask=1), swap(gu1, t_mask=1)
+
+    def share(name, *args):
+        first = len(args) == 3
+        return call(
+            functools.partial(share_kernel, first), name,
+            [sds((D, D))] * 2 + [acc] * 2 + [sds((8, D), F32)] + ([] if first else [sds((D, D))]), [n2, cot, *args],
+            [pltpu.VMEM((rows, D), BF)] * 2 + ([] if first else [pltpu.SemaphoreType.DMA((1,))]),
+            anywhere=() if first else (7,),
+        )
+
+    def up(name, bias, u):
+        return call(act_kernel, name, [wide, acc, sds((D, D))], [n2, cot, bias, u])
+
+    def down(name, act, slope, u, d, *sums):
+        return call(
+            down_kernel, name, [sds((D, D))] + [acc] * 2 + [sds((8, D), F32)], [n2, cot, act, slope, u, d, *sums],
+            [pltpu.VMEM((rows, D), BF)],
+        )
+
+    gu0, gd0, out_sum, dn2, bu0 = share("mlp_own", own, u_own, d_own)
     wu_y = after(wu_y, out_sum)
     wu_yc = swap(wu_y, t_mask=1)
-
-    def up(name, bias, u):
-        return call(act_kernel, name, [wide, acc, sds((D, D))], [n2, cot, bias, u])
-
-    def down(name, act, slope, u, d, *sums):
-        return call(
-            down_kernel, name, [sds((D + BIAS, D))] + [acc] * 2, [n2, cot, act, slope, u, d, *sums],
-            [pltpu.VMEM((rows, D), BF)],
-        )
-
-    act2, slope2, gd2 = up("mlp_up_y", wa_y, wu_y)
+    gu1, gd1, out_sum, dn2, bu1, wu_y = share("mlp_c", wa_c, wu_c, wd_c, out_sum, dn2, wu_y)
+    gd1, gu1 = swap(gd1, t_mask=1), swap(gu1, t_mask=1)
     act3, slope3, gd3 = up("mlp_up_yc", wa_yc, wu_yc)
     gd3 = swap(gd3, t_mask=1)
-    send, keep_u0 = combine(0, part(D, gu0, gu1), tag="u0")
-    got_u0 = swap(send, dp_mask=1)
+    act2, slope2, gd2 = up("mlp_up_y", wa_y, wu_y)
     send, keep_d = combine("y", part(D, gd0, gd1, sums=False), part(D, gd2, gd3, sums=False), tag="d_y")
     got_d = swap(send, t_mask=2)
     wd_y = after(wd_y, send)
     wd_yc = swap(wd_y, t_mask=1)
-    gu2, out_sum, dn2 = down("mlp_down_y", act2, slope2, wu_y, wd_y, out_sum, dn2)
-    gu3, out_sum, dn2 = down("mlp_down_yc", act3, slope3, wu_yc, wd_yc, out_sum, dn2)
+    gu2, out_sum, dn2, bu2 = down("mlp_down_y", act2, slope2, wu_y, wd_y, out_sum, dn2)
+    gu3, out_sum, dn2, bu3 = down("mlp_down_yc", act3, slope3, wu_yc, wd_yc, out_sum, dn2)
     gu3 = swap(gu3, t_mask=1)
     block_out, dh, gat, datt, sums2 = call(
         ln2_bwd_kernel, "ln2_bwd", [wide, acc, wide, wide, sds((8, D), F32)], [hid, out_sum, dn2, cot, vecs, *wa]
     )
-    send, keep_u2 = combine(0, part(D, gu2, gu3), tag="u2")
-    got_u2 = swap(send, dp_mask=1)
+    send, keep_u = combine("y", part(D, gu0, gu1, sums=False), part(D, gu2, gu3, sums=False), tag="u_y")
+    got_u = swap(send, t_mask=2)
     send, keep_d = combine(0, part(D, keep_d, got_d, sums=False), tag="d_x")
     got_d = swap(send, dp_mask=1)
     dq, dk, dv = call(
@@ -573,30 +615,29 @@
     grad_in, shared = call(
         attn_dx_kernel, "attn_dx", [wide, sds((8, D), F32)], [x, dh, dq, dk, dv, sums2, vecs, *wa]
     )
-    send, keep_u = combine("y", part(h, keep_u0, got_u0), part(h, keep_u2, got_u2), tag="u_y")
-    got_u = swap(send, t_mask=2)
 
     def attn_dw(name, shapes, one, two, *atts):
         return call(functools.partial(attn_dw_kernel, one, two), name, shapes, [dq, dk, dv, n1, gat, shared, *atts])
 
-    (got_a,) = attn_dw("attn_dw_sent", [sds((2 * (D + BIAS), D))], 1, 3, att0, att3)
+    (got_a,) = attn_dw("attn_dw_sent", [sds((2 * (D + BIAS), D))], 1, 3, bu1, bu3, att0, att3)
     got_a = swap(got_a, t_mask=1)
-    ga = attn_dw("attn_dw_kept", [sds((D + BIAS, D))] * 2, 0, 2, att0, att2)
-    send, keep_d = combine(1, part(h, keep_d, got_d, sums=False), tag="d_z")
-    got_d = swap(send, dp_mask=2)
+    send, keep_u = combine(0, part(D, keep_u, got_u, sums=False), tag="u_x")
+    got_u = swap(send, dp_mask=1)
+    ga = attn_dw("attn_dw_kept", [sds((D + BIAS, D))] * 2, 0, 2, bu0, bu2, att0, att2)
     ab = lambda first, sums: [
         Part(h, [(ga[i], first), (got_a, i * (D + BIAS) + first)], [(ga[i], D), (got_a, i * (D + BIAS) + D)] if sums else ())
         for i in range(2)
     ]
+    send, keep_d = combine(1, part(h, keep_d, got_d, sums=False), tag="d_z")
+    got_d = swap(send, dp_mask=2)
     send, keep_l = combine("y", *ab(0, True), tag="l_y")
     got_l = swap(send, t_mask=2)
     send, keep_h = combine(0, *ab(h, False), tag="h_x")
     got_h = swap(send, dp_mask=1)
-
-    def over_z(*parts):
+    def over_z(kind, *parts):
         parts = list(parts)
         for bit in bits:
-            (one,) = combine("all", *parts)
+            (one,) = combine("all", *parts, tag="all_" + kind)
             two = swap(one, dp_mask=bit)
             at, new = 0, []
             for p in parts:
@@ -604,7 +645,7 @@
                 at += p.n + p.extra
             parts = new
             yield None
-        yield combine("last", *parts)
+        yield combine("last", *parts, tag="last_" + kind)
 
     def gather(mine):
         return [mine] + [swap(mine, dp_mask=m) for m in (2, 1, 3)]
@@ -615,46 +656,46 @@
             [pltpu.VMEM((D, 128), F32)] if kind == "attn" else [],
         )
 
-    send, keep_u = combine(1, part(h, keep_u, got_u), tag="u_z")
+    def joined(mine, other, name):
+        (half,) = call(join_kernel, name, [sds((2 * mine.shape[0], D))], [scal, mine, other], mib=8)
+        return [half, swap(half, dp_mask=1)]
+
+    def turn(z):
+        for _ in bits:
+            next(z)
+
+    send, keep_u = combine(1, part(h, keep_u, got_u, sums=False), tag="u_z")
     got_u = swap(send, dp_mask=2)
-    z_d = over_z(part(q, keep_d, got_d, sums=False))
-    for _ in bits:
-        next(z_d)
-    send, keep_l = combine(0, part(h, keep_l, got_l), tag="l_x")
-    got_l = swap(send, dp_mask=1)
-    send, keep_h = combine("y", *(Part(q, [(keep_h, i * q), (got_h, i * q)]) for i in range(2)), tag="h_y")
-    got_h = swap(send, t_mask=2)
-    z_u = over_z(part(q, keep_u, got_u))
-    for _ in bits:
-        next(z_u)
+    z_d = over_z("d", part(q, keep_d, got_d, sums=False))
+    turn(z_d)
+    (send_l, keep_l), (send_h, keep_h) = combine_all(
+        (0, [part(h, keep_l, got_l)]), ("y", [Part(q, [(keep_h, i * q), (got_h, i * q)]) for i in range(2)]), tag="lxhy"
+    )
+    got_l, got_h = swap(send_l, dp_mask=1), swap(send_h, t_mask=2)
+    z_u = over_z("u", part(q, keep_u, got_u, sums=False))
+    turn(z_u)
     (mine_d,) = next(z_d)
     d_other = swap(mine_d, dp_mask=2)
     send, keep_a = combine(1, part(q, keep_l, got_l), part(q, keep_h, got_h, sums=False), tag="a_z")
     got_a = swap(send, dp_mask=2)
+    all_d = joined(mine_d, d_other, "join_d")
     e = q // 2
     z_a = over_z(
-        Part(e, [(v, 0) for v in (keep_a, got_a)], [(v, e) for v in (keep_a, got_a)]),
+        "a", Part(e, [(v, 0) for v in (keep_a, got_a)], [(v, e) for v in (keep_a, got_a)]),
         Part(e, [(v, e + BIAS) for v in (keep_a, got_a)]),
     )
-    def joined(mine, other, name):
-        (half,) = call(join_kernel, name, [sds((2 * mine.shape[0], D))], [scal, mine, other], mib=8)
-        return [half, swap(half, dp_mask=1)]
-
-    all_d = joined(mine_d, d_other, "join_d")
-    for _ in bits:
-        next(z_a)
-
-    mine_u, sums_up = next(z_u)
+    turn(z_a)
+    (mine_u,) = next(z_u)
     u_other = swap(mine_u, dp_mask=2)
+    (grad_w_down,) = finish("down", [sds((D, D), F32)], all_d)
     all_u = joined(mine_u, u_other, "join_u")
     mine_a, sums = next(z_a)
     all_a = gather(mine_a)
-    (grad_w_down,) = finish("down", [sds((D, D), F32)], all_d)
     (grad_w_up,) = finish("up", [sds((D, D), F32)], all_u)
     gwq, gwk, gwv, gwo = finish("attn", [sds((D, 128), F32)] * 3 + [sds((128, D), F32)], all_a)
     return (
         block_out, grad_in, sums[1], sums[2], gwq, sums[0, 0:128], gwk, gwv, sums[0, 256:384], gwo, sums[3],
-        sums[4], sums[5], grad_w_up, sums_up[0], grad_w_down, sums[6],
+        sums[4], sums[5], grad_w_up, sums[7], grad_w_down, sums[6],
     )
 
 

time: 123 us -> 116 us (0.943)
  Pallas kernels: 64.4 us -> 60 us
  waiting for transfers between devices: 19.5 us -> 17.7 us
    pallas_call x38 -> x37, Pallas kernels: 64.4 us -> 60 us  [call(): pl.pallas_call(kernel, out_shape=out_shape, in_specs=specs, out_specs=[VM...]
    ppermute x36 -> x35, waiting for transfers between devices: 19.5 us -> 17.7 us  [swap_now(): return lax.ppermute(v, ('dp', 'tensor'), pairs)]
    ppermute x36 -> x35, starting transfers between devices: 35.6 us -> 36 us  [swap_now(): return lax.ppermute(v, ('dp', 'tensor'), pairs)]
  transfers between devices with their start and end apart: 36 -> 35, of which waited for: 9 -> 10; matrix products, arithmetic and copies ran while one was open for 2% -> 1% of each run, Pallas kernels for 50% -> 49%
where the time goes in v3:
time: 116 us
  Pallas kernels  60 us (52%)
  starting transfers between devices  36 us (31%)
  waiting for transfers between devices  17.7 us (15%)
  local copies, waits for them, and re-layouts  1.23 us (1%)
    pallas_call x37, Pallas kernels, call(): pl.pallas_call(kernel, out_shape=out_shape, in_specs=specs, out_specs=[VM...  60 us
    ppermute x35, starting transfers between devices, swap_now(): return lax.ppermute(v, ('dp', 'tensor'), pairs)  36 us
    ppermute x35, waiting for transfers between devices, swap_now(): return lax.ppermute(v, ('dp', 'tensor'), pairs)  17.7 us
  transfers between devices with their start and end apart: 35, of which 10 were waited for; matrix products, arithmetic and copies ran while one was open for 1% of the time, Pallas kernels for 49%

profile of v3, /device:TPU:0, one launch (start us, length us, event | category | flops | bytes accessed | tf_op | source)
XLA Modules:
  0.0 116.0 jit_solution(3676602025688121846)
XLA Ops:
  2.1 3.0 %collective-permute-start.1 = (bf16[528,512]{1,0:T(8,128)(2,1)S(1)}, bf16[528,512]{1,0:T(8,128)(2,1)S(1)}, u32[]{:S(2)}, u32[]{:S(2)}) collective-permute-start(bf16[528,512]{1,0:T(8,128)(2,1)S(1)} %get-tuple-element.152.refs_4_.wa.refs_0_), channel_id=1, source_target_pairs={{0,2},{1,3},{2,0},{3,1},{4,6},{5,7},{6,4},{7,5},{8,10},{9,11},{10,... | collective-permute-start | bytes 1622024 | tf_op jit(solution)/shard_map/ppermute | solution.py:475
  6.1 1.9 %collective-permute-start.9 = (bf16[512,512]{1,0:T(8,128)(2,1)}, bf16[512,512]{1,0:T(8,128)(2,1)}, u32[]{:S(2)}, u32[]{:S(2)}) collective-permute-start(bf16[512,512]{1,0:T(8,128)(2,1)} %refs_8_.3), channel_id=1, source_target_pairs={{0,2},{1,3},{2,0},{3,1},{4,6},{5,7},{6,4},{7,5},{8,10},{9,11},{10,... | collective-permute-start | bytes 1572872 | tf_op jit(solution)/shard_map/ppermute | solution.py:475
  8.1 5.1 %attn_fwd_own.1 = (bf16[1024,256]{1,0:T(8,128)(2,1)S(1)}, bf16[1024,256]{1,0:T(8,128)(2,1)S(1)}, bf16[1024,256]{1,0:T(8,128)(2,1)S(1)}, bf16[1024,256]{1,0:T(8,1...) custom-call(s32[4]{0:T(128)S(1)} %pad_add_fusion.refs_0_.scal, ...), custom_call_target="tpu_custom_call" | custom-call | flops 10000000000 | bytes 100000000 | tf_op jit(solution)/shard_map/attn_fwd_own/pallas_call | solution.py:494
  13.2 5.0 %collective-permute-done.1.refs_4_.bias.refs_2_ = bf16[528,512]{1,0:T(8,128)(2,1)S(1)} collective-permute-done((bf16[528,512]{1,0:T(8,128)(2,1)S(1)}, bf16[528,512]{1,0:T(8,128)(2,1)S(1)}, u32[]{:S(2)}, u32[]{:S(2)}) %collective-permute-start.1) | collective-permute-done | bytes 540704 | tf_op jit(solution)/shard_map/ppermute | solution.py:475
  18.2 2.6 %attn_fwd_y.1 = (bf16[1024,128]{1,0:T(8,128)(2,1)S(1)}, bf16[1024,128]{1,0:T(8,128)(2,1)S(1)}, bf16[1024,128]{1,0:T(8,128)(2,1)S(1)}, bf16[1024,128]{1,0:T(8,128...) custom-call(s32[4]{0:T(128)S(1)} %pad_add_fusion.refs_0_.scal, s32[1,32,2]{2,1,0:T(8,128)S(1)} %copy.37.refs_1_, ...), custom_call_target="tpu_custom_call" | custom-call | flops 10000000000 | bytes 100000000 | tf_op jit(solution)/shard_map/attn_fwd_y/pallas_call | solution.py:494
  21.5 3.5 %attn_fwd_yc.1 = (bf16[1024,128]{1,0:T(8,128)(2,1)S(1)}, bf16[1024,128]{1,0:T(8,128)(2,1)S(1)}, bf16[1024,128]{1,0:T(8,128)(2,1)S(1)}, bf16[1024,128]{1,0:T(8,12...) custom-call(s32[4]{0:T(128)S(1)} %pad_add_fusion.refs_0_.scal, ...), custom_call_target="tpu_custom_call" | custom-call | flops 10000000000 | bytes 100000000 | tf_op jit(solution)/shard_map/attn_fwd_yc/pallas_call | solution.py:494
  25.0 3.9 %mlp_own.1 = (bf16[512,512]{1,0:T(8,128)(2,1)S(1)}, bf16[512,512]{1,0:T(8,128)(2,1)S(1)}, f32[1024,512]{1,0:T(8,128)S(1)}, f32[1024,512]{1,0:T(8,128)S(1)}, f32[8,512]{1,0:T(8,128)S(1)}) custom-call(bf16[1024,512]{1,0:T(8,128)(2,1)S(1)} %get-tuple-element.193.n2, bf16[1024,512]{1,0:T(8,128)(2,1)S(1)} %copy-done.1, ...), custom_call_target="tpu_custom_call" | custom-call | flops 10000000000 | bytes 100000000 | tf_op jit(solution)/shard_map/mlp_own/pallas_call | solution.py:494
  29.6 3.9 %mlp_c.1 = (bf16[512,512]{1,0:T(8,128)(2,1)S(1)}, bf16[512,512]{1,0:T(8,128)(2,1)S(1)}, f32[1024,512]{1,0:T(8,128)S(1)}, f32[1024,512]{1,0:T(8,128)S(1)}, f32[8,...) custom-call(bf16[1024,512]{1,0:T(8,128)(2,1)S(1)} %get-tuple-element.193.n2, bf16[1024,512]{1,0:T(8,128)(2,1)S(1)} %copy-done.1, ...), custom_call_target="tpu_custom_call" | custom-call | flops 10000000000 | bytes 100000000 | tf_op jit(solution)/shard_map/mlp_c/pallas_call | solution.py:494
  34.1 1.7 %mlp_up_yc.1 = (bf16[1024,512]{1,0:T(8,128)(2,1)S(1)}, f32[1024,512]{1,0:T(8,128)S(1)}, bf16[512,512]{1,0:T(8,128)(2,1)S(1)}) custom-call(bf16[1024,512]{1,0:T(8,128)(2,1)S(1)} %get-tuple-element.193.n2, bf16[1024,512]{1,0:T(8,128)(2,1)S(1)} %copy-done.1, bf16[528,512]{1,0:T(8,128)(2,1)S(1)} %collective-permute-done.2.refs_4_.bias.refs_3_, ...), custom_call_target="tpu_custom_call" | custom-call | flops 10000000000 | bytes 100000000 | tf_op jit(solution)/shard_map/mlp_up_yc/pallas_call | solution.py:494
  36.4 1.7 %mlp_up_y.1 = (bf16[1024,512]{1,0:T(8,128)(2,1)S(1)}, f32[1024,512]{1,0:T(8,128)S(1)}, bf16[512,512]{1,0:T(8,128)(2,1)S(1)}) custom-call(bf16[1024,512]{1,0:T(8,128)(2,1)S(1)} %get-tuple-element.193.n2, bf16[1024,512]{1,0:T(8,128)(2,1)S(1)} %copy-done.1, bf16[528,512]{1,0:T(8,128)(2,1)S(1)} %collective-permute-done.1.refs_4_.bias.refs_2_, ...), custom_call_target="tpu_custom_call" | custom-call | flops 10000000000 | bytes 100000000 | tf_op jit(solution)/shard_map/mlp_up_y/pallas_call | solution.py:494
  38.9 2.1 %collective-permute-start.13 = (bf16[512,512]{1,0:T(8,128)(2,1)S(1)}, bf16[512,512]{1,0:T(8,128)(2,1)S(1)}, u32[]{:S(2)}, u32[]{:S(2)}) collective-permute-start(bf16[512,512]{1,0:T(8,128)(2,1)S(1)} %get-tuple-element.184), channel_id=1, source_target_pairs={{0,2},{1,3},{2,0},{3,1},{4,6},{5,7},{6,4},{7,5},{8,10},{9,11},{10,... | collective-permute-start | bytes 1572872 | tf_op jit(solution)/shard_map/ppermute | solution.py:475
  41.0 3.6 %mlp_down_y.1 = (bf16[512,512]{1,0:T(8,128)(2,1)S(1)}, f32[1024,512]{1,0:T(8,128)S(1)}, f32[1024,512]{1,0:T(8,128)S(1)}, f32[8,512]{1,0:T(8,128)S(1)}) custom-call(bf16[1024,512]{1,0:T(8,128)(2,1)S(1)} %get-tuple-element.193.n2, bf16[1024,512]{1,0:T(8,128)(2,1)S(1)} %copy-done.1, bf16[1024,512]{1,0:T(8,128)(2,1)S(1)} %get-tuple-element.186.act, ...), custom_call_target="tpu_custom_call" | custom-call | flops 10000000000 | bytes 100000000 | tf_op jit(solution)/shard_map/mlp_down_y/pallas_call | solution.py:494
  44.6 2.5 %mlp_down_yc.1 = (bf16[512,512]{1,0:T(8,128)(2,1)S(1)}, f32[1024,512]{1,0:T(8,128)S(1)}, f32[1024,512]{1,0:T(8,128)S(1)}, f32[8,512]{1,0:T(8,128)S(1)}) custom-call(bf16[1024,512]{1,0:T(8,128)(2,1)S(1)} %get-tuple-element.193.n2, bf16[1024,512]{1,0:T(8,128)(2,1)S(1)} %copy-done.1, bf16[1024,512]{1,0:T(8,128)(2,1)S(1)} %get-tuple-element.194.act, ...), custom_call_target="tpu_custom_call" | custom-call | flops 10000000000 | bytes 100000000 | tf_op jit(solution)/shard_map/mlp_down_yc/pallas_call | solution.py:494
  47.7 3.5 %ln2_bwd.1 = (bf16[1024,512]{1,0:T(8,128)(2,1)}, f32[1024,512]{1,0:T(8,128)S(1)}, bf16[1024,512]{1,0:T(8,128)(2,1)S(1)}, bf16[1024,512]{1,0:T(8,128)(2,1)S(1)}, f32[8,512]{1,0:T(8,128)S(1)}) custom-call(f32[1024,512]{1,0:T(8,128)S(1)} %get-tuple-element.199.hid, f32[1024,512]{1,0:T(8,128)S(1)} %get-tuple-element.200.mlp, ...), custom_call_target="tpu_custom_call" | custom-call | flops 10000000000 | bytes 100000000 | tf_op jit(solution)/shard_map/ln2_bwd/pallas_call | solution.py:494
  53.9 1.8 %collective-permute-start.16 = (bf16[256,512]{1,0:T(8,128)(2,1)S(1)}, bf16[256,512]{1,0:T(8,128)(2,1)S(1)}, u32[]{:S(2)}, u32[]{:S(2)}) collective-permute-start(bf16[256,512]{1,0:T(8,128)(2,1)S(1)} %get-tuple-element.215), channel_id=1, source_target_pairs={{0,4},{1,5},{2,6},{3,7},{4,0},{5,1},{6,2},{7,3},{8,12},{9,13},{10,... | collective-permute-start | bytes 786440 | tf_op jit(solution)/shard_map/ppermute | solution.py:475
  55.7 3.2 %attn_core_bwd.1 = (bf16[1024,512]{1,0:T(8,128)(2,1)S(1)}, bf16[1024,512]{1,0:T(8,128)(2,1)S(1)}, bf16[1024,512]{1,0:T(8,128)(2,1)S(1)}) custom-call(bf16[1024,256]{1,0:T(8,128)(2,1)S(1)} %get-tuple-element.153.refs_0_, bf16[1024,256]{1,0:T(8,128)(2,1)S(1)} %get-tuple-element.203.refs_1_, bf16[1024,256]{1,0:T(8,128)(2,1)S(1)} %get-tuple-element.204.refs_2_, ...), custom_call_target="tpu_custom_call" | custom-call | flops 1000000000 | bytes 100000000 | tf_op jit(solution)/shard_map/attn_core_bwd/pallas_call | solution.py:494
  59.0 3.7 %attn_dx.1 = (bf16[1024,512]{1,0:T(8,128)(2,1)}, f32[8,512]{1,0:T(8,128)S(1)}) custom-call(bf16[1024,512]{1,0:T(8,128)(2,1)S(1)} %copy-done, f32[1024,512]{1,0:T(8,128)S(1)} %get-tuple-element.226.dh, bf16[1024,512]{1,0:T(8,128)(2,1)S(1)} %get-tuple-element.238.dq, bf16[1024,512]{1,0:T(8,128)(2,1)S(1)} %get-tuple-element.227.dk, ...), custom_call_target="tpu_custom_call" | custom-call | flops 1000000000 | bytes 100000000 | tf_op jit(solution)/shard_map/attn_dx/pallas_call | solution.py:494
  64.1 1.9 %collective-permute-done.14.refs_2_ = bf16[512,512]{1,0:T(8,128)(2,1)S(1)} collective-permute-done((bf16[512,512]{1,0:T(8,128)(2,1)S(1)}, bf16[512,512]{1,0:T(8,128)(2,1)S(1)}, u32[]{:S(2)}, u32[]{:S(2)}) %collective-permute-start.14) | collective-permute-done | bytes 524320 | tf_op jit(solution)/shard_map/ppermute | solution.py:475
  77.2 2.7 %collective-permute-start.22 = (bf16[128,512]{1,0:T(8,128)(2,1)S(1)}, bf16[128,512]{1,0:T(8,128)(2,1)S(1)}, u32[]{:S(2)}, u32[]{:S(2)}) collective-permute-start(bf16[128,512]{1,0:T(8,128)(2,1)S(1)} %add_all_d.1.refs_1_), channel_id=1, source_target_pairs={{0,16},{1,17},{2,18},{3,19},{4,20},{5,21},{6,22},{7,23},{8,24},{9,... | collective-permute-start | bytes 393224 | tf_op jit(solution)/shard_map/ppermute | solution.py:475
  83.7 2.6 %collective-permute-start.27 = (bf16[128,512]{1,0:T(8,128)(2,1)S(1)}, bf16[128,512]{1,0:T(8,128)(2,1)S(1)}, u32[]{:S(2)}, u32[]{:S(2)}) collective-permute-start(bf16[128,512]{1,0:T(8,128)(2,1)S(1)} %add_all_u.1.refs_1_), channel_id=1, source_target_pairs={{0,16},{1,17},{2,18},{3,19},{4,20},{5,21},{6,22},{7,23},{8,24},{9,... | collective-permute-start | bytes 393224 | tf_op jit(solution)/shard_map/ppermute | solution.py:475
  89.7 2.9 %collective-permute-done.25.other = bf16[128,512]{1,0:T(8,128)(2,1)S(1)} collective-permute-done((bf16[128,512]{1,0:T(8,128)(2,1)S(1)}, bf16[128,512]{1,0:T(8,128)(2,1)S(1)}, u32[]{:S(2)}, u32[]{:S(2)}) %collective-permute-start.25) | collective-permute-done | bytes 131104 | tf_op jit(solution)/shard_map/ppermute | solution.py:475
  93.2 2.6 %collective-permute-start.28 = (bf16[256,512]{1,0:T(8,128)(2,1)S(1)}, bf16[256,512]{1,0:T(8,128)(2,1)S(1)}, u32[]{:S(2)}, u32[]{:S(2)}) collective-permute-start(bf16[256,512]{1,0:T(8,128)(2,1)S(1)} %join_d.1.refs_1_), channel_id=1, source_target_pairs={{0,4},{1,5},{2,6},{3,7},{4,0},{5,1},{6,2},{7,3},{8,12},{9,13},{10,... | collective-permute-start | bytes 786440 | tf_op jit(solution)/shard_map/ppermute | solution.py:475
  100.1 1.7 %final_down.1 = f32[512,512]{1,0:T(8,128)} custom-call(s32[4]{0:T(128)S(1)} %pad_add_fusion.refs_0_.scal, bf16[256,512]{1,0:T(8,128)(2,1)S(1)} %join_d.1.refs_1_, bf16[256,512]{1,0:T(8,128)(2,1)S(1)} %collective-permute-done.28.refs_2_), custom_call_target="tpu_custom_call" | custom-call | flops 10000000000 | bytes 100000000 | tf_op jit(solution)/shard_map/final_down/pallas_call | solution.py:494
  110.0 2.9 %collective-permute-done.31.refs_2_ = bf16[256,512]{1,0:T(8,128)(2,1)S(1)} collective-permute-done((bf16[256,512]{1,0:T(8,128)(2,1)S(1)}, bf16[256,512]{1,0:T(8,128)(2,1)S(1)}, u32[]{:S(2)}, u32[]{:S(2)}) %collective-permute-start.31) | collective-permute-done | bytes 262176 | tf_op jit(solution)/shard_map/ppermute | solution.py:475
  (93 shorter events, 44.8 us)
Async XLA Ops:
  2.1 16.1 %collective-permute-start.1 = (bf16[528,512]{1,0:T(8,128)(2,1)S(1)}, bf16[528,512]{1,0:T(8,128)(2,1)S(1)}, u32[]{:S(2)}, u32[]{:S(2)}) collective-permute-start(bf16[528,512]{1,0:T(8,128)(2,1)S(1)} %get-tuple-element.152.refs_4_.wa.refs_0_), channel_id=1, source_target_pairs={{0,2},{1,3},{2,0},{3,1},{4,6},{5,7},{6,4},{7,5},{8,10},{9,11},{10,... | collective-permute-start | bytes 1622024 | tf_op jit(solution)/shard_map/ppermute | solution.py:475
  5.9 23.7 %collective-permute-start.5 = (bf16[512,512]{1,0:T(8,128)(2,1)}, bf16[512,512]{1,0:T(8,128)(2,1)}, u32[]{:S(2)}, u32[]{:S(2)}) collective-permute-start(bf16[512,512]{1,0:T(8,128)(2,1)} %refs_7_.3), channel_id=1, source_target_pairs={{0,2},{1,3},{2,0},{3,1},{4,6},{5,7},{6,4},{7,5},{8,10},{9,11},{10,... | collective-permute-start | bytes 1572872 | tf_op jit(solution)/shard_map/ppermute | solution.py:475
  6.1 34.9 %collective-permute-start.9 = (bf16[512,512]{1,0:T(8,128)(2,1)}, bf16[512,512]{1,0:T(8,128)(2,1)}, u32[]{:S(2)}, u32[]{:S(2)}) collective-permute-start(bf16[512,512]{1,0:T(8,128)(2,1)} %refs_8_.3), channel_id=1, source_target_pairs={{0,2},{1,3},{2,0},{3,1},{4,6},{5,7},{6,4},{7,5},{8,10},{9,11},{10,... | collective-permute-start | bytes 1572872 | tf_op jit(solution)/shard_map/ppermute | solution.py:475
  20.9 8.7 %collective-permute-start.3 = (bf16[512,512]{1,0:T(8,128)(2,1)}, bf16[512,512]{1,0:T(8,128)(2,1)S(1)}, u32[]{:S(2)}, u32[]{:S(2)}) collective-permute-start(bf16[512,512]{1,0:T(8,128)(2,1)} %refs_7_.3), channel_id=1, source_target_pairs={{0,1},{1,0},{2,3},{3,2},{4,5},{5,4},{6,7},{7,6},{8,9},{9,8},{10,11... | collective-permute-start | bytes 1572872 | tf_op jit(solution)/shard_map/ppermute | solution.py:475
  21.4 8.1 %collective-permute-start.4 = (bf16[512,512]{1,0:T(8,128)(2,1)}, bf16[512,512]{1,0:T(8,128)(2,1)S(1)}, u32[]{:S(2)}, u32[]{:S(2)}) collective-permute-start(bf16[512,512]{1,0:T(8,128)(2,1)} %refs_8_.3), channel_id=1, source_target_pairs={{0,1},{1,0},{2,3},{3,2},{4,5},{5,4},{6,7},{7,6},{8,9},{9,8},{10,11... | collective-permute-start | bytes 1572872 | tf_op jit(solution)/shard_map/ppermute | solution.py:475
  34.1 17.1 %collective-permute-start.11 = (bf16[512,512]{1,0:T(8,128)(2,1)S(1)}, bf16[512,512]{1,0:T(8,128)(2,1)S(1)}, u32[]{:S(2)}, u32[]{:S(2)}) collective-permute-start(bf16[512,512]{1,0:T(8,128)(2,1)S(1)} %get-tuple-element.210), channel_id=1, source_target_pairs={{0,1},{1,0},{2,3},{3,2},{4,5},{5,4},{6,7},{7,6},{8,9},{9,8},{10,11... | collective-permute-start | bytes 1572872 | tf_op jit(solution)/shard_map/ppermute | solution.py:475
  38.9 14.4 %collective-permute-start.13 = (bf16[512,512]{1,0:T(8,128)(2,1)S(1)}, bf16[512,512]{1,0:T(8,128)(2,1)S(1)}, u32[]{:S(2)}, u32[]{:S(2)}) collective-permute-start(bf16[512,512]{1,0:T(8,128)(2,1)S(1)} %get-tuple-element.184), channel_id=1, source_target_pairs={{0,2},{1,3},{2,0},{3,1},{4,6},{5,7},{6,4},{7,5},{8,10},{9,11},{10,... | collective-permute-start | bytes 1572872 | tf_op jit(solution)/shard_map/ppermute | solution.py:475
  52.0 13.9 %collective-permute-start.14 = (bf16[512,512]{1,0:T(8,128)(2,1)S(1)}, bf16[512,512]{1,0:T(8,128)(2,1)S(1)}, u32[]{:S(2)}, u32[]{:S(2)}) collective-permute-start(bf16[512,512]{1,0:T(8,128)(2,1)S(1)} %get-tuple-element.213), channel_id=1, source_target_pairs={{0,2},{1,3},{2,0},{3,1},{4,6},{5,7},{6,4},{7,5},{8,10},{9,11},{10,... | collective-permute-start | bytes 1572872 | tf_op jit(solution)/shard_map/ppermute | solution.py:475
  53.9 15.5 %collective-permute-start.16 = (bf16[256,512]{1,0:T(8,128)(2,1)S(1)}, bf16[256,512]{1,0:T(8,128)(2,1)S(1)}, u32[]{:S(2)}, u32[]{:S(2)}) collective-permute-start(bf16[256,512]{1,0:T(8,128)(2,1)S(1)} %get-tuple-element.215), channel_id=1, source_target_pairs={{0,4},{1,5},{2,6},{3,7},{4,0},{5,1},{6,2},{7,3},{8,12},{9,13},{10,... | collective-permute-start | bytes 786440 | tf_op jit(solution)/shard_map/ppermute | solution.py:475
  64.0 7.7 %collective-permute-start.15 = (bf16[1056,512]{1,0:T(8,128)(2,1)S(1)}, bf16[1056,512]{1,0:T(8,128)(2,1)S(1)}, u32[]{:S(2)}, u32[]{:S(2)}) collective-permute-start(bf16[1056,512]{1,0:T(8,128)(2,1)S(1)} %attn_dw_sent.1), channel_id=1, source_target_pairs={{0,1},{1,0},{2,3},{3,2},{4,5},{5,4},{6,7},{7,6},{8,9},{9,8},{10,11... | collective-permute-start | bytes 3244040 | tf_op jit(solution)/shard_map/ppermute | solution.py:475
  66.6 7.8 %collective-permute-start.17 = (bf16[256,512]{1,0:T(8,128)(2,1)S(1)}, bf16[256,512]{1,0:T(8,128)(2,1)S(1)}, u32[]{:S(2)}, u32[]{:S(2)}) collective-permute-start(bf16[256,512]{1,0:T(8,128)(2,1)S(1)} %get-tuple-element.237), channel_id=1, source_target_pairs={{0,4},{1,5},{2,6},{3,7},{4,0},{5,1},{6,2},{7,3},{8,12},{9,13},{10,... | collective-permute-start | bytes 786440 | tf_op jit(solution)/shard_map/ppermute | solution.py:475
  72.4 8.0 %collective-permute-start.19 = (bf16[272,512]{1,0:T(8,128)(2,1)S(1)}, bf16[272,512]{1,0:T(8,128)(2,1)S(1)}, u32[]{:S(2)}, u32[]{:S(2)}) collective-permute-start(bf16[272,512]{1,0:T(8,128)(2,1)S(1)} %get-tuple-element.249), channel_id=1, source_target_pairs={{0,2},{1,3},{2,0},{3,1},{4,6},{5,7},{6,4},{7,5},{8,10},{9,11},{10,... | collective-permute-start | bytes 835592 | tf_op jit(solution)/shard_map/ppermute | solution.py:475
  73.8 6.6 %collective-permute-start.20 = (bf16[256,512]{1,0:T(8,128)(2,1)S(1)}, bf16[256,512]{1,0:T(8,128)(2,1)S(1)}, u32[]{:S(2)}, u32[]{:S(2)}) collective-permute-start(bf16[256,512]{1,0:T(8,128)(2,1)S(1)} %get-tuple-element.251), channel_id=1, source_target_pairs={{0,4},{1,5},{2,6},{3,7},{4,0},{5,1},{6,2},{7,3},{8,12},{9,13},{10,... | collective-permute-start | bytes 786440 | tf_op jit(solution)/shard_map/ppermute | solution.py:475
  75.0 8.0 %collective-permute-start.21 = (bf16[128,512]{1,0:T(8,128)(2,1)S(1)}, bf16[128,512]{1,0:T(8,128)(2,1)S(1)}, u32[]{:S(2)}, u32[]{:S(2)}) collective-permute-start(bf16[128,512]{1,0:T(8,128)(2,1)S(1)} %get-tuple-element.253), channel_id=1, source_target_pairs={{0,8},{1,9},{2,10},{3,11},{4,12},{5,13},{6,14},{7,15},{8,0},{9,1},... | collective-permute-start | bytes 393224 | tf_op jit(solution)/shard_map/ppermute | solution.py:475
  77.2 9.1 %collective-permute-start.22 = (bf16[128,512]{1,0:T(8,128)(2,1)S(1)}, bf16[128,512]{1,0:T(8,128)(2,1)S(1)}, u32[]{:S(2)}, u32[]{:S(2)}) collective-permute-start(bf16[128,512]{1,0:T(8,128)(2,1)S(1)} %add_all_d.1.refs_1_), channel_id=1, source_target_pairs={{0,16},{1,17},{2,18},{3,19},{4,20},{5,21},{6,22},{7,23},{8,24},{9,... | collective-permute-start | bytes 393224 | tf_op jit(solution)/shard_map/ppermute | solution.py:475
  81.1 6.9 %collective-permute-start.24 = (bf16[128,512]{1,0:T(8,128)(2,1)S(1)}, bf16[128,512]{1,0:T(8,128)(2,1)S(1)}, u32[]{:S(2)}, u32[]{:S(2)}) collective-permute-start(bf16[128,512]{1,0:T(8,128)(2,1)S(1)} %get-tuple-element.259), channel_id=1, source_target_pairs={{0,2},{1,3},{2,0},{3,1},{4,6},{5,7},{6,4},{7,5},{8,10},{9,11},{10,... | collective-permute-start | bytes 393224 | tf_op jit(solution)/shard_map/ppermute | solution.py:475
  83.7 12.7 %collective-permute-start.27 = (bf16[128,512]{1,0:T(8,128)(2,1)S(1)}, bf16[128,512]{1,0:T(8,128)(2,1)S(1)}, u32[]{:S(2)}, u32[]{:S(2)}) collective-permute-start(bf16[128,512]{1,0:T(8,128)(2,1)S(1)} %add_all_u.1.refs_1_), channel_id=1, source_target_pairs={{0,16},{1,17},{2,18},{3,19},{4,20},{5,21},{6,22},{7,23},{8,24},{9,... | collective-permute-start | bytes 393224 | tf_op jit(solution)/shard_map/ppermute | solution.py:475
  88.7 7.1 %collective-permute-start.26 = (bf16[144,512]{1,0:T(8,128)(2,1)S(1)}, bf16[144,512]{1,0:T(8,128)(2,1)S(1)}, u32[]{:S(2)}, u32[]{:S(2)}) collective-permute-start(bf16[144,512]{1,0:T(8,128)(2,1)S(1)} %get-tuple-element.266), channel_id=1, source_target_pairs={{0,8},{1,9},{2,10},{3,11},{4,12},{5,13},{6,14},{7,15},{8,0},{9,1},... | collective-permute-start | bytes 442376 | tf_op jit(solution)/shard_map/ppermute | solution.py:475
  93.2 7.0 %collective-permute-start.28 = (bf16[256,512]{1,0:T(8,128)(2,1)S(1)}, bf16[256,512]{1,0:T(8,128)(2,1)S(1)}, u32[]{:S(2)}, u32[]{:S(2)}) collective-permute-start(bf16[256,512]{1,0:T(8,128)(2,1)S(1)} %join_d.1.refs_1_), channel_id=1, source_target_pairs={{0,4},{1,5},{2,6},{3,7},{4,0},{5,1},{6,2},{7,3},{8,12},{9,13},{10,... | collective-permute-start | bytes 786440 | tf_op jit(solution)/shard_map/ppermute | solution.py:475
  97.0 7.7 %collective-permute-start.30 = (bf16[144,512]{1,0:T(8,128)(2,1)S(1)}, bf16[144,512]{1,0:T(8,128)(2,1)S(1)}, u32[]{:S(2)}, u32[]{:S(2)}) collective-permute-start(bf16[144,512]{1,0:T(8,128)(2,1)S(1)} %add_all_a.1.refs_1_), channel_id=1, source_target_pairs={{0,16},{1,17},{2,18},{3,19},{4,20},{5,21},{6,22},{7,23},{8,24},{9,... | collective-permute-start | bytes 442376 | tf_op jit(solution)/shard_map/ppermute | solution.py:475
  104.0 8.9 %collective-permute-start.31 = (bf16[256,512]{1,0:T(8,128)(2,1)S(1)}, bf16[256,512]{1,0:T(8,128)(2,1)S(1)}, u32[]{:S(2)}, u32[]{:S(2)}) collective-permute-start(bf16[256,512]{1,0:T(8,128)(2,1)S(1)} %join_u.1.refs_1_), channel_id=1, source_target_pairs={{0,4},{1,5},{2,6},{3,7},{4,0},{5,1},{6,2},{7,3},{8,12},{9,13},{10,... | collective-permute-start | bytes 786440 | tf_op jit(solution)/shard_map/ppermute | solution.py:475
  105.9 8.6 %collective-permute-start.34 = (bf16[128,512]{1,0:T(8,128)(2,1)S(1)}, bf16[128,512]{1,0:T(8,128)(2,1)S(1)}, u32[]{:S(2)}, u32[]{:S(2)}) collective-permute-start(bf16[128,512]{1,0:T(8,128)(2,1)S(1)} %get-tuple-element.276.refs_1_), channel_id=1, source_target_pairs={{0,12},{1,13},{2,14},{3,15},{4,8},{5,9},{6,10},{7,11},{8,4},{9,5},... | collective-permute-start | bytes 393224 | tf_op jit(solution)/shard_map/ppermute | solution.py:475
  106.7 7.8 %collective-permute-start.33 = (bf16[128,512]{1,0:T(8,128)(2,1)S(1)}, bf16[128,512]{1,0:T(8,128)(2,1)S(1)}, u32[]{:S(2)}, u32[]{:S(2)}) collective-permute-start(bf16[128,512]{1,0:T(8,128)(2,1)S(1)} %get-tuple-element.276.refs_1_), channel_id=1, source_target_pairs={{0,4},{1,5},{2,6},{3,7},{4,0},{5,1},{6,2},{7,3},{8,12},{9,13},{10,... | collective-permute-start | bytes 393224 | tf_op jit(solution)/shard_map/ppermute | solution.py:475
  107.7 6.7 %collective-permute-start.32 = (bf16[128,512]{1,0:T(8,128)(2,1)S(1)}, bf16[128,512]{1,0:T(8,128)(2,1)S(1)}, u32[]{:S(2)}, u32[]{:S(2)}) collective-permute-start(bf16[128,512]{1,0:T(8,128)(2,1)S(1)} %get-tuple-element.276.refs_1_), channel_id=1, source_target_pairs={{0,8},{1,9},{2,10},{3,11},{4,12},{5,13},{6,14},{7,15},{8,0},{9,1},... | collective-permute-start | bytes 393224 | tf_op jit(solution)/shard_map/ppermute | solution.py:475
  (14 other events, 61.2 us)

commit v4 on v3

--- a/solution.py
+++ b/solution.py
@@ -14,7 +14,7 @@
 BR = 256
 BIAS = 16
 EPS = 1e-5
-WEIGHTS = {"attn_dw_sent": 1, "attn_core_bwd": 1, "attn_dx": 1, "add_d_x": 0, "add_ud_x": 0, "add_l_y": 0, "add_h_x": 0, "add_lyhx": 0, "add_u_y": 0, "add_last_d": 0}
+WEIGHTS = {"attn_dw_sent": 1, "attn_core_bwd": 1, "attn_dx": 1, "add_d_x": 0, "add_ud_x": 0, "add_l_y": 0, "add_h_x": 0, "add_lyhx": 0, "add_u_y": 0, "add_last_d": 0, "rows_out": 1}
 LN1_G, LN1_B, B_OUT, LN2_G, LN2_B, B_DOWN, B_UP, B_QV = range(8)
 SMEM = functools.partial(pl.BlockSpec, memory_space=pltpu.SMEM)
 VMEM = functools.partial(pl.BlockSpec, memory_space=pltpu.VMEM)
@@ -42,10 +42,6 @@
 
 def sds(shape, dtype=BF):
     return jax.ShapeDtypeStruct(shape, dtype)
-
-
-def whole(shape):
-    return pl.BlockSpec(shape, lambda *i: (0,) * len(shape))
 
 
 def fetch(src, dst, sems, at=0, pieces=4):
@@ -136,9 +132,9 @@
 
 def attn_fwd_kernel(shares, first, last, *refs):
     (scal, lens, n1, base), w = refs[:4], list(refs[4 : 4 + shares])
-    vecs, (q_o, k_o, v_o, att_o, pt_o, hid_o), n2_o = refs[4 + shares], refs[5 + shares + 2 * first : 11 + shares + 2 * first], refs[-1]
+    vecs, (q_o, k_o, v_o, att_o, pt_o, hid_o), n2_o = refs[4 + shares], refs[5 + shares + 3 * first : 11 + shares + 3 * first], refs[-1]
     if first:
-        up_in, down_in, wa_o, up_o, down_o, sems = refs[7], refs[8], *refs[-4:]
+        up_in, down_in, cot, wa_o, up_o, down_o, csum_o, sems = *refs[7:10], *refs[-5:]
         fetched = fetch(w[1], wa_o, sems, pieces=3)
         brought = [pltpu.make_async_copy(up_in, up_o, sems.at[3]), pltpu.make_async_copy(down_in, down_o, sems.at[4])]
         for c in brought:
@@ -179,6 +175,7 @@
         hid += dot(att_o[:, c * 128 : (c + 1) * 128], wo)
     hid_o[...] = hid
     if first:
+        csum_o[...] = jnp.broadcast_to(jnp.sum(cot[...].astype(F32), 0, keepdims=True), (8, D))
         await_all(brought)
     if last:
 
@@ -261,15 +258,13 @@
     return sums + jnp.concatenate([jnp.sum(a, 0, keepdims=True) for a in adds], 0)
 
 
-def ln2_bwd_kernel(hid, mlp, dn2, cot, vecs, *refs):
-    w, (block_o, dh_o, gat_s, datt_o, sums_o) = refs[:4], refs[4:]
+def ln2_bwd_kernel(hid, dn2, cot, vecs, *refs):
+    w, (dh_o, gat_s, datt_o, sums_o) = refs[:4], refs[4:]
     rows = hid.shape[0]
 
     def tile(m, sums):
         here = pl.ds(pl.multiple_of(m * BR, BR), BR)
-        hidden = hid[here, :]
-        block_o[here, :] = (hidden + mlp[here, :] + vecs[B_DOWN : B_DOWN + 1, :]).astype(BF)
-        xhat, rstd = normalise(hidden)
+        xhat, rstd = normalise(hid[here, :])
         dn = dn2[here, :]
         e = dn * vecs[LN2_G : LN2_G + 1, :]
         cotf = cot[here, :].astype(F32)
@@ -277,10 +272,10 @@
         dh_o[here, :] = dh
         gat = dh.astype(BF)
         gat_s[here, :] = gat
-        return total(sums, gat.astype(F32), dn * xhat, dn, cotf)
-
-    sums_o[0:4, :] = lax.fori_loop(0, rows // BR, tile, jnp.zeros((4, D), F32), unroll=2)
-    sums_o[4:8, :] = jnp.zeros((4, D), F32)
+        return total(sums, gat.astype(F32), dn * xhat, dn)
+
+    sums_o[0:3, :] = lax.fori_loop(0, rows // BR, tile, jnp.zeros((3, D), F32), unroll=2)
+    sums_o[3:8, :] = jnp.zeros((5, D), F32)
     for c in range(4):
         wo = jnp.concatenate([w[c][b * 128 : (b + 1) * 128, 384:512] for b in range(4)], 1)
         datt_o[:, c * 128 : (c + 1) * 128] = dot_nt(gat_s[...], wo).astype(BF)
@@ -331,8 +326,8 @@
         o[at + D : at + D + BIAS, :] = bias_block(jnp.concatenate([own, shared[0:6, :], (bu_one, bu_two)[i][0:1, :]], 0))
 
 
-def attn_dx_kernel(x, dh, dq, dk, dv, sums2, vecs, *refs):
-    w, (gin_o, shared_o) = refs[:4], refs[4:]
+def attn_dx_kernel(x, dq, dk, dv, sums2, csum, *refs):
+    w, (dn1_o, shared_o) = refs[:4], refs[4:]
 
     def tile(m, sums):
         here = pl.ds(pl.multiple_of(m * BR, BR), BR)
@@ -342,14 +337,25 @@
             grads = jnp.concatenate([dq[here, cols], dk[here, cols], dv[here, cols]], 1)
             part = dot_nt(grads, w[c][0:D, 0:384])
             dn1 = part if dn1 is None else dn1 + part
+        dn1_o[here, :] = dn1
+        xhat, _ = normalise(x[here, :].astype(F32))
+        return total(sums, dn1 * xhat, dn1)
+
+    sums1 = lax.fori_loop(0, x.shape[0] // BR, tile, jnp.zeros((2, D), F32), unroll=True)
+    shared_o[...] = jnp.concatenate([sums1, sums2[0:3, :], csum[0:1, :], jnp.zeros((2, D), F32)], 0)
+
+
+def rows_kernel(x, dh, dn1, hid, mlp, vecs, gin_o, block_o):
+    def tile(m, _):
+        here = pl.ds(pl.multiple_of(m * BR, BR), BR)
         xhat, rstd = normalise(x[here, :].astype(F32))
-        e = dn1 * vecs[LN1_G : LN1_G + 1, :]
+        e = dn1[here, :] * vecs[LN1_G : LN1_G + 1, :]
         back = rstd * (e - jnp.mean(e, -1, keepdims=True) - xhat * jnp.mean(e * xhat, -1, keepdims=True))
         gin_o[here, :] = (dh[here, :] + back).astype(BF)
-        return total(sums, dn1 * xhat, dn1)
-
-    sums1 = lax.fori_loop(0, x.shape[0] // BR, tile, jnp.zeros((2, D), F32), unroll=True)
-    shared_o[...] = jnp.concatenate([sums1, sums2[0:4, :], jnp.zeros((2, D), F32)], 0)
+        block_o[here, :] = (hid[here, :] + mlp[here, :] + vecs[B_DOWN : B_DOWN + 1, :]).astype(BF)
+        return 0
+
+    lax.fori_loop(0, x.shape[0] // BR, tile, 0, unroll=2)
 
 
 def bias_block(total):
@@ -548,14 +554,14 @@
         shapes = [sds((rows, n))] * 4 + [sds((rows, 2 * n)), acc] + [wide] * last
         args = [scal, lengths, n1, hid, *weights, vecs]
         if first:
-            shapes += [sds((D + BIAS, D)), sds((D, D)), sds((D, D))]
-            args += [w_up, w_down]
+            shapes += [sds((D + BIAS, D)), sds((D, D)), sds((D, D)), sds((8, D), F32)]
+            args += [w_up, w_down, cot]
         return call(
             functools.partial(attn_fwd_kernel, len(weights), first, last), name, shapes, args,
             [pltpu.SemaphoreType.DMA((5,))] if first else [], anywhere=(5, 7, 8) if first else (),
         )
 
-    *saved_0, att0, pt0, hid, wa_c, u_own, d_own = attn_fwd("attn_fwd_own", [own, wa_c], x, first=True)
+    *saved_0, att0, pt0, hid, wa_c, u_own, d_own, csum = attn_fwd("attn_fwd_own", [own, wa_c], x, first=True)
     wa_y = after(wa_y, hid)
     wa_yc = swap(wa_y, t_mask=1)
     *saved_2, att2, pt2, hid = attn_fwd("attn_fwd_y", [wa_y], hid)
@@ -602,8 +608,8 @@
     gu2, out_sum, dn2, bu2 = down("mlp_down_y", act2, slope2, wu_y, wd_y, out_sum, dn2)
     gu3, out_sum, dn2, bu3 = down("mlp_down_yc", act3, slope3, wu_yc, wd_yc, out_sum, dn2)
     gu3 = swap(gu3, t_mask=1)
-    block_out, dh, gat, datt, sums2 = call(
-        ln2_bwd_kernel, "ln2_bwd", [wide, acc, wide, wide, sds((8, D), F32)], [hid, out_sum, dn2, cot, vecs, *wa]
+    dh, gat, datt, sums2 = call(
+        ln2_bwd_kernel, "ln2_bwd", [acc, wide, wide, sds((8, D), F32)], [hid, dn2, cot, vecs, *wa]
     )
     send, keep_u = combine("y", part(D, gu0, gu1, sums=False), part(D, gu2, gu3, sums=False), tag="u_y")
     got_u = swap(send, t_mask=2)
@@ -612,8 +618,8 @@
     dq, dk, dv = call(
         attn_core_bwd_kernel, "attn_core_bwd", [wide] * 3, [*saved_0, pt0, *saved_2, pt2, *saved_3, pt3, datt]
     )
-    grad_in, shared = call(
-        attn_dx_kernel, "attn_dx", [wide, sds((8, D), F32)], [x, dh, dq, dk, dv, sums2, vecs, *wa]
+    dn1, shared = call(
+        attn_dx_kernel, "attn_dx", [acc, sds((8, D), F32)], [x, dq, dk, dv, sums2, csum, *wa]
     )
 
     def attn_dw(name, shapes, one, two, *atts):
@@ -679,16 +685,17 @@
     send, keep_a = combine(1, part(q, keep_l, got_l), part(q, keep_h, got_h, sums=False), tag="a_z")
     got_a = swap(send, dp_mask=2)
     all_d = joined(mine_d, d_other, "join_d")
+    (mine_u,) = next(z_u)
+    u_other = swap(mine_u, dp_mask=2)
     e = q // 2
     z_a = over_z(
         "a", Part(e, [(v, 0) for v in (keep_a, got_a)], [(v, e) for v in (keep_a, got_a)]),
         Part(e, [(v, e + BIAS) for v in (keep_a, got_a)]),
     )
     turn(z_a)
-    (mine_u,) = next(z_u)
-    u_other = swap(mine_u, dp_mask=2)
+    grad_in, block_out = call(rows_kernel, "rows_out", [wide] * 2, [x, dh, dn1, hid, out_sum, vecs])
+    all_u = joined(mine_u, u_other, "join_u")
     (grad_w_down,) = finish("down", [sds((D, D), F32)], all_d)
-    all_u = joined(mine_u, u_other, "join_u")
     mine_a, sums = next(z_a)
     all_a = gather(mine_a)
     (grad_w_up,) = finish("up", [sds((D, D), F32)], all_u)

time: 116 us -> 115 us (level)
  waiting for transfers between devices: 17.7 us -> 13.3 us
  local copies, waits for them, and re-layouts: 1.23 us -> 2.45 us
    ppermute x35, waiting for transfers between devices: 17.7 us -> 13.3 us  [swap_now(): return lax.ppermute(v, ('dp', 'tensor'), pairs)]
    unnamed x7 -> x9, local copies, waits for them, and re-layouts: 0.1 us -> 1.33 us
    pallas_call x37 -> x38, Pallas kernels: 60 us -> 61 us  [call(): pl.pallas_call(kernel, out_shape=out_shape, in_specs=specs, out_specs=[VM...]
  transfers between devices with their start and end apart: 35 -> 35, of which waited for: 10 -> 10; matrix products, arithmetic and copies ran while one was open for 1% -> 1% of each run, Pallas kernels for 49% -> 51%
where the time goes in v4:
time: 115 us
  Pallas kernels  61 us (53%)
  starting transfers between devices  36.8 us (32%)
  waiting for transfers between devices  13.3 us (12%)
  local copies, waits for them, and re-layouts  2.45 us (2%)
    pallas_call x38, Pallas kernels, call(): pl.pallas_call(kernel, out_shape=out_shape, in_specs=specs, out_specs=[VM...  61 us
    ppermute x35, starting transfers between devices, swap_now(): return lax.ppermute(v, ('dp', 'tensor'), pairs)  36.8 us
    ppermute x35, waiting for transfers between devices, swap_now(): return lax.ppermute(v, ('dp', 'tensor'), pairs)  13.3 us
  transfers between devices with their start and end apart: 35, of which 10 were waited for; matrix products, arithmetic and copies ran while one was open for 1% of the time, Pallas kernels for 51%

profile of v4, /device:TPU:0, one launch (start us, length us, event | category | flops | bytes accessed | tf_op | source)
XLA Modules:
  0.0 114.7 jit_solution(745722813510599656)
XLA Ops:
  2.1 3.0 %collective-permute-start.1 = (bf16[528,512]{1,0:T(8,128)(2,1)S(1)}, bf16[528,512]{1,0:T(8,128)(2,1)S(1)}, u32[]{:S(2)}, u32[]{:S(2)}) collective-permute-start(bf16[528,512]{1,0:T(8,128)(2,1)S(1)} %get-tuple-element.155.refs_4_.wa.refs_0_), channel_id=1, source_target_pairs={{0,2},{1,3},{2,0},{3,1},{4,6},{5,7},{6,4},{7,5},{8,10},{9,11},{10,... | collective-permute-start | bytes 1622024 | tf_op jit(solution)/shard_map/ppermute | solution.py:481
  6.1 1.9 %collective-permute-start.9 = (bf16[512,512]{1,0:T(8,128)(2,1)}, bf16[512,512]{1,0:T(8,128)(2,1)}, u32[]{:S(2)}, u32[]{:S(2)}) collective-permute-start(bf16[512,512]{1,0:T(8,128)(2,1)} %refs_8_.3), channel_id=1, source_target_pairs={{0,2},{1,3},{2,0},{3,1},{4,6},{5,7},{6,4},{7,5},{8,10},{9,11},{10,... | collective-permute-start | bytes 1572872 | tf_op jit(solution)/shard_map/ppermute | solution.py:481
  9.4 5.1 %attn_fwd_own.1 = (bf16[1024,256]{1,0:T(8,128)(2,1)S(1)}, bf16[1024,256]{1,0:T(8,128)(2,1)S(1)}, bf16[1024,256]{1,0:T(8,128)(2,1)S(1)}, bf16[1024,256]{1,0:T(8,1...) custom-call(s32[4]{0:T(128)S(1)} %pad_add_fusion.refs_0_.scal, ...), custom_call_target="tpu_custom_call" | custom-call | flops 10000000000 | bytes 100000000 | tf_op jit(solution)/shard_map/attn_fwd_own/pallas_call | solution.py:500
  14.5 3.7 %collective-permute-done.1.refs_4_.bias.refs_2_ = bf16[528,512]{1,0:T(8,128)(2,1)S(1)} collective-permute-done((bf16[528,512]{1,0:T(8,128)(2,1)S(1)}, bf16[528,512]{1,0:T(8,128)(2,1)S(1)}, u32[]{:S(2)}, u32[]{:S(2)}) %collective-permute-start.1) | collective-permute-done | bytes 540704 | tf_op jit(solution)/shard_map/ppermute | solution.py:481
  18.2 2.6 %attn_fwd_y.1 = (bf16[1024,128]{1,0:T(8,128)(2,1)S(1)}, bf16[1024,128]{1,0:T(8,128)(2,1)S(1)}, bf16[1024,128]{1,0:T(8,128)(2,1)S(1)}, bf16[1024,128]{1,0:T(8,128...) custom-call(s32[4]{0:T(128)S(1)} %pad_add_fusion.refs_0_.scal, s32[1,32,2]{2,1,0:T(8,128)S(1)} %copy.35.refs_1_, ...), custom_call_target="tpu_custom_call" | custom-call | flops 10000000000 | bytes 100000000 | tf_op jit(solution)/shard_map/attn_fwd_y/pallas_call | solution.py:500
  21.5 3.5 %attn_fwd_yc.1 = (bf16[1024,128]{1,0:T(8,128)(2,1)S(1)}, bf16[1024,128]{1,0:T(8,128)(2,1)S(1)}, bf16[1024,128]{1,0:T(8,128)(2,1)S(1)}, bf16[1024,128]{1,0:T(8,12...) custom-call(s32[4]{0:T(128)S(1)} %pad_add_fusion.refs_0_.scal, ...), custom_call_target="tpu_custom_call" | custom-call | flops 10000000000 | bytes 100000000 | tf_op jit(solution)/shard_map/attn_fwd_yc/pallas_call | solution.py:500
  25.0 3.9 %mlp_own.1 = (bf16[512,512]{1,0:T(8,128)(2,1)S(1)}, bf16[512,512]{1,0:T(8,128)(2,1)S(1)}, f32[1024,512]{1,0:T(8,128)S(1)}, f32[1024,512]{1,0:T(8,128)S(1)}, f32[8,512]{1,0:T(8,128)S(1)}) custom-call(bf16[1024,512]{1,0:T(8,128)(2,1)S(1)} %get-tuple-element.202.n2, bf16[1024,512]{1,0:T(8,128)(2,1)S(1)} %copy-done.1, ...), custom_call_target="tpu_custom_call" | custom-call | flops 10000000000 | bytes 100000000 | tf_op jit(solution)/shard_map/mlp_own/pallas_call | solution.py:500
  29.6 3.9 %mlp_c.1 = (bf16[512,512]{1,0:T(8,128)(2,1)S(1)}, bf16[512,512]{1,0:T(8,128)(2,1)S(1)}, f32[1024,512]{1,0:T(8,128)S(1)}, f32[1024,512]{1,0:T(8,128)S(1)}, f32[8,...) custom-call(bf16[1024,512]{1,0:T(8,128)(2,1)S(1)} %get-tuple-element.202.n2, bf16[1024,512]{1,0:T(8,128)(2,1)S(1)} %copy-done.1, ...), custom_call_target="tpu_custom_call" | custom-call | flops 10000000000 | bytes 100000000 | tf_op jit(solution)/shard_map/mlp_c/pallas_call | solution.py:500
  36.3 1.7 %mlp_up_y.1 = (bf16[1024,512]{1,0:T(8,128)(2,1)S(1)}, f32[1024,512]{1,0:T(8,128)S(1)}, bf16[512,512]{1,0:T(8,128)(2,1)S(1)}) custom-call(bf16[1024,512]{1,0:T(8,128)(2,1)S(1)} %get-tuple-element.202.n2, bf16[1024,512]{1,0:T(8,128)(2,1)S(1)} %copy-done.1, bf16[528,512]{1,0:T(8,128)(2,1)S(1)} %collective-permute-done.1.refs_4_.bias.refs_2_, ...), custom_call_target="tpu_custom_call" | custom-call | flops 10000000000 | bytes 100000000 | tf_op jit(solution)/shard_map/mlp_up_y/pallas_call | solution.py:500
  38.9 2.1 %collective-permute-start.13 = (bf16[512,512]{1,0:T(8,128)(2,1)S(1)}, bf16[512,512]{1,0:T(8,128)(2,1)S(1)}, u32[]{:S(2)}, u32[]{:S(2)}) collective-permute-start(bf16[512,512]{1,0:T(8,128)(2,1)S(1)} %get-tuple-element.193), channel_id=1, source_target_pairs={{0,2},{1,3},{2,0},{3,1},{4,6},{5,7},{6,4},{7,5},{8,10},{9,11},{10,... | collective-permute-start | bytes 1572872 | tf_op jit(solution)/shard_map/ppermute | solution.py:481
  41.0 3.5 %mlp_down_y.1 = (bf16[512,512]{1,0:T(8,128)(2,1)S(1)}, f32[1024,512]{1,0:T(8,128)S(1)}, f32[1024,512]{1,0:T(8,128)S(1)}, f32[8,512]{1,0:T(8,128)S(1)}) custom-call(bf16[1024,512]{1,0:T(8,128)(2,1)S(1)} %get-tuple-element.202.n2, bf16[1024,512]{1,0:T(8,128)(2,1)S(1)} %copy-done.1, bf16[1024,512]{1,0:T(8,128)(2,1)S(1)} %get-tuple-element.195.act, ...), custom_call_target="tpu_custom_call" | custom-call | flops 10000000000 | bytes 100000000 | tf_op jit(solution)/shard_map/mlp_down_y/pallas_call | solution.py:500
  44.5 2.5 %mlp_down_yc.1 = (bf16[512,512]{1,0:T(8,128)(2,1)S(1)}, f32[1024,512]{1,0:T(8,128)S(1)}, f32[1024,512]{1,0:T(8,128)S(1)}, f32[8,512]{1,0:T(8,128)S(1)}) custom-call(bf16[1024,512]{1,0:T(8,128)(2,1)S(1)} %get-tuple-element.202.n2, bf16[1024,512]{1,0:T(8,128)(2,1)S(1)} %copy-done.1, bf16[1024,512]{1,0:T(8,128)(2,1)S(1)} %get-tuple-element.203.act, ...), custom_call_target="tpu_custom_call" | custom-call | flops 10000000000 | bytes 100000000 | tf_op jit(solution)/shard_map/mlp_down_yc/pallas_call | solution.py:500
  47.6 3.3 %ln2_bwd.1 = (f32[1024,512]{1,0:T(8,128)S(1)}, bf16[1024,512]{1,0:T(8,128)(2,1)S(1)}, bf16[1024,512]{1,0:T(8,128)(2,1)S(1)}, f32[8,512]{1,0:T(8,128)S(1)}) custom-call(f32[1024,512]{1,0:T(8,128)S(1)} %get-tuple-element.208.hid, f32[1024,512]{1,0:T(8,128)S(1)} %get-tuple-element.209.dn2, bf16[1024,512]{1,0:T(8,128)(2,1)S(1)} %copy-done.2, ...), custom_call_target="tpu_custom_call" | custom-call | flops 10000000000 | bytes 100000000 | tf_op jit(solution)/shard_map/ln2_bwd/pallas_call | solution.py:500
  53.9 1.8 %collective-permute-start.16 = (bf16[256,512]{1,0:T(8,128)(2,1)S(1)}, bf16[256,512]{1,0:T(8,128)(2,1)S(1)}, u32[]{:S(2)}, u32[]{:S(2)}) collective-permute-start(bf16[256,512]{1,0:T(8,128)(2,1)S(1)} %get-tuple-element.217), channel_id=1, source_target_pairs={{0,4},{1,5},{2,6},{3,7},{4,0},{5,1},{6,2},{7,3},{8,12},{9,13},{10,... | collective-permute-start | bytes 786440 | tf_op jit(solution)/shard_map/ppermute | solution.py:481
  55.7 3.2 %attn_core_bwd.1 = (bf16[1024,512]{1,0:T(8,128)(2,1)S(1)}, bf16[1024,512]{1,0:T(8,128)(2,1)S(1)}, bf16[1024,512]{1,0:T(8,128)(2,1)S(1)}) custom-call(bf16[1024,256]{1,0:T(8,128)(2,1)S(1)} %get-tuple-element.156.refs_0_, bf16[1024,256]{1,0:T(8,128)(2,1)S(1)} %get-tuple-element.157.refs_1_, bf16[1024,256]{1,0:T(8,128)(2,1)S(1)} %get-tuple-element.158.refs_2_, ...), custom_call_target="tpu_custom_call" | custom-call | flops 1000000000 | bytes 100000000 | tf_op jit(solution)/shard_map/attn_core_bwd/pallas_call | solution.py:500
  58.9 2.4 %attn_dx.1 = (f32[1024,512]{1,0:T(8,128)S(1)}, f32[8,512]{1,0:T(8,128)S(1)}) custom-call(bf16[1024,512]{1,0:T(8,128)(2,1)S(1)} %copy-done, bf16[1024,512]{1,0:T(8,128)(2,1)S(1)} %get-tuple-element.238.dq, bf16[1024,512]{1,0:T(8,128)(2,1)S(1)} %get-tuple-element.229.dk, bf16[1024,512]{1,0:T(8,128)(2,1)S(1)} %get-tuple-element.230.dv, ...), custom_call_target="tpu_custom_call" | custom-call | flops 1000000000 | bytes 100000000 | tf_op jit(solution)/shard_map/attn_dx/pallas_call | solution.py:500
  62.7 2.9 %collective-permute-done.14.refs_2_ = bf16[512,512]{1,0:T(8,128)(2,1)S(1)} collective-permute-done((bf16[512,512]{1,0:T(8,128)(2,1)S(1)}, bf16[512,512]{1,0:T(8,128)(2,1)S(1)}, u32[]{:S(2)}, u32[]{:S(2)}) %collective-permute-start.14) | collective-permute-done | bytes 524320 | tf_op jit(solution)/shard_map/ppermute | solution.py:481
  76.9 2.6 %collective-permute-start.22 = (bf16[128,512]{1,0:T(8,128)(2,1)S(1)}, bf16[128,512]{1,0:T(8,128)(2,1)S(1)}, u32[]{:S(2)}, u32[]{:S(2)}) collective-permute-start(bf16[128,512]{1,0:T(8,128)(2,1)S(1)} %add_all_d.1.refs_1_), channel_id=1, source_target_pairs={{0,16},{1,17},{2,18},{3,19},{4,20},{5,21},{6,22},{7,23},{8,24},{9,... | collective-permute-start | bytes 393224 | tf_op jit(solution)/shard_map/ppermute | solution.py:481
  83.4 2.6 %collective-permute-start.26 = (bf16[128,512]{1,0:T(8,128)(2,1)S(1)}, bf16[128,512]{1,0:T(8,128)(2,1)S(1)}, u32[]{:S(2)}, u32[]{:S(2)}) collective-permute-start(bf16[128,512]{1,0:T(8,128)(2,1)S(1)} %add_all_u.1.refs_1_), channel_id=1, source_target_pairs={{0,16},{1,17},{2,18},{3,19},{4,20},{5,21},{6,22},{7,23},{8,24},{9,... | collective-permute-start | bytes 393224 | tf_op jit(solution)/shard_map/ppermute | solution.py:481
  89.4 3.0 %collective-permute-done.25.other = bf16[128,512]{1,0:T(8,128)(2,1)S(1)} collective-permute-done((bf16[128,512]{1,0:T(8,128)(2,1)S(1)}, bf16[128,512]{1,0:T(8,128)(2,1)S(1)}, u32[]{:S(2)}, u32[]{:S(2)}) %collective-permute-start.25) | collective-permute-done | bytes 131104 | tf_op jit(solution)/shard_map/ppermute | solution.py:481
  92.9 2.9 %collective-permute-start.29 = (bf16[256,512]{1,0:T(8,128)(2,1)S(1)}, bf16[256,512]{1,0:T(8,128)(2,1)S(1)}, u32[]{:S(2)}, u32[]{:S(2)}) collective-permute-start(bf16[256,512]{1,0:T(8,128)(2,1)S(1)} %join_d.1.refs_1_), channel_id=1, source_target_pairs={{0,4},{1,5},{2,6},{3,7},{4,0},{5,1},{6,2},{7,3},{8,12},{9,13},{10,... | collective-permute-start | bytes 786440 | tf_op jit(solution)/shard_map/ppermute | solution.py:481
  98.4 2.6 %rows_out.1 = (bf16[1024,512]{1,0:T(8,128)(2,1)}, bf16[1024,512]{1,0:T(8,128)(2,1)}) custom-call(bf16[1024,512]{1,0:T(8,128)(2,1)S(1)} %copy-done, f32[1024,512]{1,0:T(8,128)S(1)} %get-tuple-element.271.dh, f32[1024,512]{1,0:T(8,128)S(1)} %get-tuple-element.272.dn1, f32[1024,512]{1,0:T(8,128)S(1)} %get-tuple-element.208.hid, ...), custom_call_target="tpu_custom_call" | custom-call | flops 1000000000 | bytes 100000000 | tf_op jit(solution)/shard_map/rows_out/pallas_call | solution.py:500
  103.2 1.7 %final_down.1 = f32[512,512]{1,0:T(8,128)} custom-call(s32[4]{0:T(128)S(1)} %pad_add_fusion.refs_0_.scal, bf16[256,512]{1,0:T(8,128)(2,1)S(1)} %join_d.1.refs_1_, bf16[256,512]{1,0:T(8,128)(2,1)S(1)} %collective-permute-done.29.refs_2_), custom_call_target="tpu_custom_call" | custom-call | flops 10000000000 | bytes 100000000 | tf_op jit(solution)/shard_map/final_down/pallas_call | solution.py:500
  107.8 1.7 %collective-permute-start.32 = (bf16[128,512]{1,0:T(8,128)(2,1)S(1)}, bf16[128,512]{1,0:T(8,128)(2,1)S(1)}, u32[]{:S(2)}, u32[]{:S(2)}) collective-permute-start(bf16[128,512]{1,0:T(8,128)(2,1)S(1)} %get-tuple-element.282.refs_1_), channel_id=1, source_target_pairs={{0,8},{1,9},{2,10},{3,11},{4,12},{5,13},{6,14},{7,15},{8,0},{9,1},... | collective-permute-start | bytes 393224 | tf_op jit(solution)/shard_map/ppermute | solution.py:481
  (96 shorter events, 45.3 us)
Async XLA Ops:
  2.1 16.1 %collective-permute-start.1 = (bf16[528,512]{1,0:T(8,128)(2,1)S(1)}, bf16[528,512]{1,0:T(8,128)(2,1)S(1)}, u32[]{:S(2)}, u32[]{:S(2)}) collective-permute-start(bf16[528,512]{1,0:T(8,128)(2,1)S(1)} %get-tuple-element.155.refs_4_.wa.refs_0_), channel_id=1, source_target_pairs={{0,2},{1,3},{2,0},{3,1},{4,6},{5,7},{6,4},{7,5},{8,10},{9,11},{10,... | collective-permute-start | bytes 1622024 | tf_op jit(solution)/shard_map/ppermute | solution.py:481
  5.9 23.7 %collective-permute-start.5 = (bf16[512,512]{1,0:T(8,128)(2,1)}, bf16[512,512]{1,0:T(8,128)(2,1)}, u32[]{:S(2)}, u32[]{:S(2)}) collective-permute-start(bf16[512,512]{1,0:T(8,128)(2,1)} %refs_7_.3), channel_id=1, source_target_pairs={{0,2},{1,3},{2,0},{3,1},{4,6},{5,7},{6,4},{7,5},{8,10},{9,11},{10,... | collective-permute-start | bytes 1572872 | tf_op jit(solution)/shard_map/ppermute | solution.py:481
  6.1 34.9 %collective-permute-start.9 = (bf16[512,512]{1,0:T(8,128)(2,1)}, bf16[512,512]{1,0:T(8,128)(2,1)}, u32[]{:S(2)}, u32[]{:S(2)}) collective-permute-start(bf16[512,512]{1,0:T(8,128)(2,1)} %refs_8_.3), channel_id=1, source_target_pairs={{0,2},{1,3},{2,0},{3,1},{4,6},{5,7},{6,4},{7,5},{8,10},{9,11},{10,... | collective-permute-start | bytes 1572872 | tf_op jit(solution)/shard_map/ppermute | solution.py:481
  20.8 8.7 %collective-permute-start.3 = (bf16[512,512]{1,0:T(8,128)(2,1)}, bf16[512,512]{1,0:T(8,128)(2,1)S(1)}, u32[]{:S(2)}, u32[]{:S(2)}) collective-permute-start(bf16[512,512]{1,0:T(8,128)(2,1)} %refs_7_.3), channel_id=1, source_target_pairs={{0,1},{1,0},{2,3},{3,2},{4,5},{5,4},{6,7},{7,6},{8,9},{9,8},{10,11... | collective-permute-start | bytes 1572872 | tf_op jit(solution)/shard_map/ppermute | solution.py:481
  21.4 8.2 %collective-permute-start.4 = (bf16[512,512]{1,0:T(8,128)(2,1)}, bf16[512,512]{1,0:T(8,128)(2,1)S(1)}, u32[]{:S(2)}, u32[]{:S(2)}) collective-permute-start(bf16[512,512]{1,0:T(8,128)(2,1)} %refs_8_.3), channel_id=1, source_target_pairs={{0,1},{1,0},{2,3},{3,2},{4,5},{5,4},{6,7},{7,6},{8,9},{9,8},{10,11... | collective-permute-start | bytes 1572872 | tf_op jit(solution)/shard_map/ppermute | solution.py:481
  34.1 16.8 %collective-permute-start.11 = (bf16[512,512]{1,0:T(8,128)(2,1)S(1)}, bf16[512,512]{1,0:T(8,128)(2,1)S(1)}, u32[]{:S(2)}, u32[]{:S(2)}) collective-permute-start(bf16[512,512]{1,0:T(8,128)(2,1)S(1)} %get-tuple-element.212), channel_id=1, source_target_pairs={{0,1},{1,0},{2,3},{3,2},{4,5},{5,4},{6,7},{7,6},{8,9},{9,8},{10,11... | collective-permute-start | bytes 1572872 | tf_op jit(solution)/shard_map/ppermute | solution.py:481
  38.9 14.4 %collective-permute-start.13 = (bf16[512,512]{1,0:T(8,128)(2,1)S(1)}, bf16[512,512]{1,0:T(8,128)(2,1)S(1)}, u32[]{:S(2)}, u32[]{:S(2)}) collective-permute-start(bf16[512,512]{1,0:T(8,128)(2,1)S(1)} %get-tuple-element.193), channel_id=1, source_target_pairs={{0,2},{1,3},{2,0},{3,1},{4,6},{5,7},{6,4},{7,5},{8,10},{9,11},{10,... | collective-permute-start | bytes 1572872 | tf_op jit(solution)/shard_map/ppermute | solution.py:481
  51.7 13.9 %collective-permute-start.14 = (bf16[512,512]{1,0:T(8,128)(2,1)S(1)}, bf16[512,512]{1,0:T(8,128)(2,1)S(1)}, u32[]{:S(2)}, u32[]{:S(2)}) collective-permute-start(bf16[512,512]{1,0:T(8,128)(2,1)S(1)} %get-tuple-element.215), channel_id=1, source_target_pairs={{0,2},{1,3},{2,0},{3,1},{4,6},{5,7},{6,4},{7,5},{8,10},{9,11},{10,... | collective-permute-start | bytes 1572872 | tf_op jit(solution)/shard_map/ppermute | solution.py:481
  53.9 15.2 %collective-permute-start.16 = (bf16[256,512]{1,0:T(8,128)(2,1)S(1)}, bf16[256,512]{1,0:T(8,128)(2,1)S(1)}, u32[]{:S(2)}, u32[]{:S(2)}) collective-permute-start(bf16[256,512]{1,0:T(8,128)(2,1)S(1)} %get-tuple-element.217), channel_id=1, source_target_pairs={{0,4},{1,5},{2,6},{3,7},{4,0},{5,1},{6,2},{7,3},{8,12},{9,13},{10,... | collective-permute-start | bytes 786440 | tf_op jit(solution)/shard_map/ppermute | solution.py:481
  62.6 8.8 %collective-permute-start.15 = (bf16[1056,512]{1,0:T(8,128)(2,1)S(1)}, bf16[1056,512]{1,0:T(8,128)(2,1)S(1)}, u32[]{:S(2)}, u32[]{:S(2)}) collective-permute-start(bf16[1056,512]{1,0:T(8,128)(2,1)S(1)} %attn_dw_sent.1), channel_id=1, source_target_pairs={{0,1},{1,0},{2,3},{3,2},{4,5},{5,4},{6,7},{7,6},{8,9},{9,8},{10,11... | collective-permute-start | bytes 3244040 | tf_op jit(solution)/shard_map/ppermute | solution.py:481
  66.3 7.8 %collective-permute-start.17 = (bf16[256,512]{1,0:T(8,128)(2,1)S(1)}, bf16[256,512]{1,0:T(8,128)(2,1)S(1)}, u32[]{:S(2)}, u32[]{:S(2)}) collective-permute-start(bf16[256,512]{1,0:T(8,128)(2,1)S(1)} %get-tuple-element.237), channel_id=1, source_target_pairs={{0,4},{1,5},{2,6},{3,7},{4,0},{5,1},{6,2},{7,3},{8,12},{9,13},{10,... | collective-permute-start | bytes 786440 | tf_op jit(solution)/shard_map/ppermute | solution.py:481
  69.8 6.5 %collective-permute-start.18 = (bf16[128,512]{1,0:T(8,128)(2,1)S(1)}, bf16[128,512]{1,0:T(8,128)(2,1)S(1)}, u32[]{:S(2)}, u32[]{:S(2)}) collective-permute-start(bf16[128,512]{1,0:T(8,128)(2,1)S(1)} %get-tuple-element.243), channel_id=1, source_target_pairs={{0,8},{1,9},{2,10},{3,11},{4,12},{5,13},{6,14},{7,15},{8,0},{9,1},... | collective-permute-start | bytes 393224 | tf_op jit(solution)/shard_map/ppermute | solution.py:481
  72.1 8.1 %collective-permute-start.19 = (bf16[272,512]{1,0:T(8,128)(2,1)S(1)}, bf16[272,512]{1,0:T(8,128)(2,1)S(1)}, u32[]{:S(2)}, u32[]{:S(2)}) collective-permute-start(bf16[272,512]{1,0:T(8,128)(2,1)S(1)} %get-tuple-element.249), channel_id=1, source_target_pairs={{0,2},{1,3},{2,0},{3,1},{4,6},{5,7},{6,4},{7,5},{8,10},{9,11},{10,... | collective-permute-start | bytes 835592 | tf_op jit(solution)/shard_map/ppermute | solution.py:481
  73.5 6.6 %collective-permute-start.20 = (bf16[256,512]{1,0:T(8,128)(2,1)S(1)}, bf16[256,512]{1,0:T(8,128)(2,1)S(1)}, u32[]{:S(2)}, u32[]{:S(2)}) collective-permute-start(bf16[256,512]{1,0:T(8,128)(2,1)S(1)} %get-tuple-element.251), channel_id=1, source_target_pairs={{0,4},{1,5},{2,6},{3,7},{4,0},{5,1},{6,2},{7,3},{8,12},{9,13},{10,... | collective-permute-start | bytes 786440 | tf_op jit(solution)/shard_map/ppermute | solution.py:481
  74.8 8.1 %collective-permute-start.21 = (bf16[128,512]{1,0:T(8,128)(2,1)S(1)}, bf16[128,512]{1,0:T(8,128)(2,1)S(1)}, u32[]{:S(2)}, u32[]{:S(2)}) collective-permute-start(bf16[128,512]{1,0:T(8,128)(2,1)S(1)} %get-tuple-element.253), channel_id=1, source_target_pairs={{0,8},{1,9},{2,10},{3,11},{4,12},{5,13},{6,14},{7,15},{8,0},{9,1},... | collective-permute-start | bytes 393224 | tf_op jit(solution)/shard_map/ppermute | solution.py:481
  76.9 9.1 %collective-permute-start.22 = (bf16[128,512]{1,0:T(8,128)(2,1)S(1)}, bf16[128,512]{1,0:T(8,128)(2,1)S(1)}, u32[]{:S(2)}, u32[]{:S(2)}) collective-permute-start(bf16[128,512]{1,0:T(8,128)(2,1)S(1)} %add_all_d.1.refs_1_), channel_id=1, source_target_pairs={{0,16},{1,17},{2,18},{3,19},{4,20},{5,21},{6,22},{7,23},{8,24},{9,... | collective-permute-start | bytes 393224 | tf_op jit(solution)/shard_map/ppermute | solution.py:481
  80.8 6.9 %collective-permute-start.24 = (bf16[128,512]{1,0:T(8,128)(2,1)S(1)}, bf16[128,512]{1,0:T(8,128)(2,1)S(1)}, u32[]{:S(2)}, u32[]{:S(2)}) collective-permute-start(bf16[128,512]{1,0:T(8,128)(2,1)S(1)} %get-tuple-element.259), channel_id=1, source_target_pairs={{0,2},{1,3},{2,0},{3,1},{4,6},{5,7},{6,4},{7,5},{8,10},{9,11},{10,... | collective-permute-start | bytes 393224 | tf_op jit(solution)/shard_map/ppermute | solution.py:481
  83.4 12.4 %collective-permute-start.26 = (bf16[128,512]{1,0:T(8,128)(2,1)S(1)}, bf16[128,512]{1,0:T(8,128)(2,1)S(1)}, u32[]{:S(2)}, u32[]{:S(2)}) collective-permute-start(bf16[128,512]{1,0:T(8,128)(2,1)S(1)} %add_all_u.1.refs_1_), channel_id=1, source_target_pairs={{0,16},{1,17},{2,18},{3,19},{4,20},{5,21},{6,22},{7,23},{8,24},{9,... | collective-permute-start | bytes 393224 | tf_op jit(solution)/shard_map/ppermute | solution.py:481
  88.4 8.0 %collective-permute-start.27 = (bf16[144,512]{1,0:T(8,128)(2,1)S(1)}, bf16[144,512]{1,0:T(8,128)(2,1)S(1)}, u32[]{:S(2)}, u32[]{:S(2)}) collective-permute-start(bf16[144,512]{1,0:T(8,128)(2,1)S(1)} %get-tuple-element.266), channel_id=1, source_target_pairs={{0,8},{1,9},{2,10},{3,11},{4,12},{5,13},{6,14},{7,15},{8,0},{9,1},... | collective-permute-start | bytes 442376 | tf_op jit(solution)/shard_map/ppermute | solution.py:481
  92.9 10.3 %collective-permute-start.29 = (bf16[256,512]{1,0:T(8,128)(2,1)S(1)}, bf16[256,512]{1,0:T(8,128)(2,1)S(1)}, u32[]{:S(2)}, u32[]{:S(2)}) collective-permute-start(bf16[256,512]{1,0:T(8,128)(2,1)S(1)} %join_d.1.refs_1_), channel_id=1, source_target_pairs={{0,4},{1,5},{2,6},{3,7},{4,0},{5,1},{6,2},{7,3},{8,12},{9,13},{10,... | collective-permute-start | bytes 786440 | tf_op jit(solution)/shard_map/ppermute | solution.py:481
  97.0 7.9 %collective-permute-start.30 = (bf16[144,512]{1,0:T(8,128)(2,1)S(1)}, bf16[144,512]{1,0:T(8,128)(2,1)S(1)}, u32[]{:S(2)}, u32[]{:S(2)}) collective-permute-start(bf16[144,512]{1,0:T(8,128)(2,1)S(1)} %add_all_a.1.refs_1_), channel_id=1, source_target_pairs={{0,16},{1,17},{2,18},{3,19},{4,20},{5,21},{6,22},{7,23},{8,24},{9,... | collective-permute-start | bytes 442376 | tf_op jit(solution)/shard_map/ppermute | solution.py:481
  101.9 8.3 %collective-permute-start.31 = (bf16[256,512]{1,0:T(8,128)(2,1)S(1)}, bf16[256,512]{1,0:T(8,128)(2,1)S(1)}, u32[]{:S(2)}, u32[]{:S(2)}) collective-permute-start(bf16[256,512]{1,0:T(8,128)(2,1)S(1)} %join_u.1.refs_1_), channel_id=1, source_target_pairs={{0,4},{1,5},{2,6},{3,7},{4,0},{5,1},{6,2},{7,3},{8,12},{9,13},{10,... | collective-permute-start | bytes 786440 | tf_op jit(solution)/shard_map/ppermute | solution.py:481
  106.0 6.0 %collective-permute-start.34 = (bf16[128,512]{1,0:T(8,128)(2,1)S(1)}, bf16[128,512]{1,0:T(8,128)(2,1)S(1)}, u32[]{:S(2)}, u32[]{:S(2)}) collective-permute-start(bf16[128,512]{1,0:T(8,128)(2,1)S(1)} %get-tuple-element.282.refs_1_), channel_id=1, source_target_pairs={{0,12},{1,13},{2,14},{3,15},{4,8},{5,9},{6,10},{7,11},{8,4},{9,5},... | collective-permute-start | bytes 393224 | tf_op jit(solution)/shard_map/ppermute | solution.py:481
  106.7 6.4 %collective-permute-start.33 = (bf16[128,512]{1,0:T(8,128)(2,1)S(1)}, bf16[128,512]{1,0:T(8,128)(2,1)S(1)}, u32[]{:S(2)}, u32[]{:S(2)}) collective-permute-start(bf16[128,512]{1,0:T(8,128)(2,1)S(1)} %get-tuple-element.282.refs_1_), channel_id=1, source_target_pairs={{0,4},{1,5},{2,6},{3,7},{4,0},{5,1},{6,2},{7,3},{8,12},{9,13},{10,... | collective-permute-start | bytes 393224 | tf_op jit(solution)/shard_map/ppermute | solution.py:481
  (15 other events, 58.3 us)

commit v5 on v4

--- a/solution.py
+++ b/solution.py
@@ -452,6 +452,15 @@
         outs[3][...] = outs[4][...].T
 
 
+def attn_final_kernel(scal, *refs):
+    sums, outs = refs[4], refs[5:]
+    final_kernel("attn", scal, *refs[0:4], *outs[0:4], outs[-1])
+    outs[4][...] = sums[0:1, 0:128].reshape(128)
+    outs[5][...] = sums[0:1, 256:384].reshape(128)
+    for i in range(7):
+        outs[6 + i][...] = sums[i + 1 : i + 2, :].reshape(D)
+
+
 def layer(
     n_dp, n_t, x, lengths, ln1_gain, ln1_bias, w_query, b_query, w_key, w_value, b_value, w_out, b_out,
     ln2_gain, ln2_bias, w_up, b_up, w_down, b_down, cot,
@@ -699,10 +708,14 @@
     mine_a, sums = next(z_a)
     all_a = gather(mine_a)
     (grad_w_up,) = finish("up", [sds((D, D), F32)], all_u)
-    gwq, gwk, gwv, gwo = finish("attn", [sds((D, 128), F32)] * 3 + [sds((128, D), F32)], all_a)
+    vec, short = sds((D,), F32), sds((128,), F32)
+    gwq, gwk, gwv, gwo, gbq, gbv, *vectors = call(
+        attn_final_kernel, "final_attn", [sds((D, 128), F32)] * 3 + [sds((128, D), F32)] + [short] * 2 + [vec] * 7,
+        [scal, *all_a, sums], [pltpu.VMEM((D, 128), F32)],
+    )
+    ln1_g, ln1_b, b_o, ln2_g, ln2_b, b_d, b_u = vectors
     return (
-        block_out, grad_in, sums[1], sums[2], gwq, sums[0, 0:128], gwk, gwv, sums[0, 256:384], gwo, sums[3],
-        sums[4], sums[5], grad_w_up, sums[7], grad_w_down, sums[6],
+        block_out, grad_in, ln1_g, ln1_b, gwq, gbq, gwk, gwv, gbv, gwo, b_o, ln2_g, ln2_b, grad_w_up, b_u, grad_w_down, b_d,
     )
 
 

time: 115 us -> 115 us (level)
  transfers between devices with their start and end apart: 35 -> 35, of which waited for: 10 -> 10; matrix products, arithmetic and copies ran while one was open for 1% -> 0% of each run, Pallas kernels for 51% -> 51%
where the time goes in v5:
time: 115 us; the launch traced here: 114 us
  Pallas kernels  61 us (53%)
  starting transfers between devices  36.9 us (32%)
  waiting for transfers between devices  13.9 us (12%)
  local copies, waits for them, and re-layouts  1.33 us (1%)
  between operations  1.17 us (1%)
    pallas_call x38, Pallas kernels, call(): pl.pallas_call(kernel, out_shape=out_shape, in_specs=specs, out_specs=[VM...  61 us
    ppermute x35, starting transfers between devices, swap_now(): return lax.ppermute(v, ('dp', 'tensor'), pairs)  36.9 us
    ppermute x35, waiting for transfers between devices, swap_now(): return lax.ppermute(v, ('dp', 'tensor'), pairs)  13.9 us
  transfers between devices with their start and end apart: 35, of which 10 were waited for; matrix products, arithmetic and copies ran while one was open for 0% of the time, Pallas kernels for 51%

profile of v5, /device:TPU:0, one launch (start us, length us, event | category | flops | bytes accessed | tf_op | source)
XLA Modules:
  0.0 114.4 jit_solution(5931474383111128036)
XLA Ops:
  2.1 3.0 %collective-permute-start.1 = (bf16[528,512]{1,0:T(8,128)(2,1)S(1)}, bf16[528,512]{1,0:T(8,128)(2,1)S(1)}, u32[]{:S(2)}, u32[]{:S(2)}) collective-permute-start(bf16[528,512]{1,0:T(8,128)(2,1)S(1)} %get-tuple-element.164.refs_4_.wa.refs_0_), channel_id=1, source_target_pairs={{0,2},{1,3},{2,0},{3,1},{4,6},{5,7},{6,4},{7,5},{8,10},{9,11},{10,... | collective-permute-start | bytes 1622024 | tf_op jit(solution)/shard_map/ppermute | solution.py:490
  6.1 1.9 %collective-permute-start.9 = (bf16[512,512]{1,0:T(8,128)(2,1)}, bf16[512,512]{1,0:T(8,128)(2,1)}, u32[]{:S(2)}, u32[]{:S(2)}) collective-permute-start(bf16[512,512]{1,0:T(8,128)(2,1)} %refs_8_.3), channel_id=1, source_target_pairs={{0,2},{1,3},{2,0},{3,1},{4,6},{5,7},{6,4},{7,5},{8,10},{9,11},{10,... | collective-permute-start | bytes 1572872 | tf_op jit(solution)/shard_map/ppermute | solution.py:490
  9.4 5.1 %attn_fwd_own.1 = (bf16[1024,256]{1,0:T(8,128)(2,1)S(1)}, bf16[1024,256]{1,0:T(8,128)(2,1)S(1)}, bf16[1024,256]{1,0:T(8,128)(2,1)S(1)}, bf16[1024,256]{1,0:T(8,1...) custom-call(s32[4]{0:T(128)S(1)} %pad_add_fusion.refs_0_.scal, ...), custom_call_target="tpu_custom_call" | custom-call | flops 10000000000 | bytes 100000000 | tf_op jit(solution)/shard_map/attn_fwd_own/pallas_call | solution.py:509
  14.5 3.7 %collective-permute-done.1.refs_4_.bias.refs_2_ = bf16[528,512]{1,0:T(8,128)(2,1)S(1)} collective-permute-done((bf16[528,512]{1,0:T(8,128)(2,1)S(1)}, bf16[528,512]{1,0:T(8,128)(2,1)S(1)}, u32[]{:S(2)}, u32[]{:S(2)}) %collective-permute-start.1) | collective-permute-done | bytes 540704 | tf_op jit(solution)/shard_map/ppermute | solution.py:490
  18.2 2.6 %attn_fwd_y.1 = (bf16[1024,128]{1,0:T(8,128)(2,1)S(1)}, bf16[1024,128]{1,0:T(8,128)(2,1)S(1)}, bf16[1024,128]{1,0:T(8,128)(2,1)S(1)}, bf16[1024,128]{1,0:T(8,128...) custom-call(s32[4]{0:T(128)S(1)} %pad_add_fusion.refs_0_.scal, s32[1,32,2]{2,1,0:T(8,128)S(1)} %copy.35.refs_1_, ...), custom_call_target="tpu_custom_call" | custom-call | flops 10000000000 | bytes 100000000 | tf_op jit(solution)/shard_map/attn_fwd_y/pallas_call | solution.py:509
  21.5 3.5 %attn_fwd_yc.1 = (bf16[1024,128]{1,0:T(8,128)(2,1)S(1)}, bf16[1024,128]{1,0:T(8,128)(2,1)S(1)}, bf16[1024,128]{1,0:T(8,128)(2,1)S(1)}, bf16[1024,128]{1,0:T(8,12...) custom-call(s32[4]{0:T(128)S(1)} %pad_add_fusion.refs_0_.scal, ...), custom_call_target="tpu_custom_call" | custom-call | flops 10000000000 | bytes 100000000 | tf_op jit(solution)/shard_map/attn_fwd_yc/pallas_call | solution.py:509
  25.0 3.9 %mlp_own.1 = (bf16[512,512]{1,0:T(8,128)(2,1)S(1)}, bf16[512,512]{1,0:T(8,128)(2,1)S(1)}, f32[1024,512]{1,0:T(8,128)S(1)}, f32[1024,512]{1,0:T(8,128)S(1)}, f32[8,512]{1,0:T(8,128)S(1)}) custom-call(bf16[1024,512]{1,0:T(8,128)(2,1)S(1)} %get-tuple-element.211.n2, bf16[1024,512]{1,0:T(8,128)(2,1)S(1)} %copy-done.1, ...), custom_call_target="tpu_custom_call" | custom-call | flops 10000000000 | bytes 100000000 | tf_op jit(solution)/shard_map/mlp_own/pallas_call | solution.py:509
  29.6 3.9 %mlp_c.1 = (bf16[512,512]{1,0:T(8,128)(2,1)S(1)}, bf16[512,512]{1,0:T(8,128)(2,1)S(1)}, f32[1024,512]{1,0:T(8,128)S(1)}, f32[1024,512]{1,0:T(8,128)S(1)}, f32[8,...) custom-call(bf16[1024,512]{1,0:T(8,128)(2,1)S(1)} %get-tuple-element.211.n2, bf16[1024,512]{1,0:T(8,128)(2,1)S(1)} %copy-done.1, ...), custom_call_target="tpu_custom_call" | custom-call | flops 10000000000 | bytes 100000000 | tf_op jit(solution)/shard_map/mlp_c/pallas_call | solution.py:509
  36.3 1.7 %mlp_up_y.1 = (bf16[1024,512]{1,0:T(8,128)(2,1)S(1)}, f32[1024,512]{1,0:T(8,128)S(1)}, bf16[512,512]{1,0:T(8,128)(2,1)S(1)}) custom-call(bf16[1024,512]{1,0:T(8,128)(2,1)S(1)} %get-tuple-element.211.n2, bf16[1024,512]{1,0:T(8,128)(2,1)S(1)} %copy-done.1, bf16[528,512]{1,0:T(8,128)(2,1)S(1)} %collective-permute-done.1.refs_4_.bias.refs_2_, ...), custom_call_target="tpu_custom_call" | custom-call | flops 10000000000 | bytes 100000000 | tf_op jit(solution)/shard_map/mlp_up_y/pallas_call | solution.py:509
  38.9 2.1 %collective-permute-start.13 = (bf16[512,512]{1,0:T(8,128)(2,1)S(1)}, bf16[512,512]{1,0:T(8,128)(2,1)S(1)}, u32[]{:S(2)}, u32[]{:S(2)}) collective-permute-start(bf16[512,512]{1,0:T(8,128)(2,1)S(1)} %get-tuple-element.202), channel_id=1, source_target_pairs={{0,2},{1,3},{2,0},{3,1},{4,6},{5,7},{6,4},{7,5},{8,10},{9,11},{10,... | collective-permute-start | bytes 1572872 | tf_op jit(solution)/shard_map/ppermute | solution.py:490
  41.0 3.5 %mlp_down_y.1 = (bf16[512,512]{1,0:T(8,128)(2,1)S(1)}, f32[1024,512]{1,0:T(8,128)S(1)}, f32[1024,512]{1,0:T(8,128)S(1)}, f32[8,512]{1,0:T(8,128)S(1)}) custom-call(bf16[1024,512]{1,0:T(8,128)(2,1)S(1)} %get-tuple-element.211.n2, bf16[1024,512]{1,0:T(8,128)(2,1)S(1)} %copy-done.1, bf16[1024,512]{1,0:T(8,128)(2,1)S(1)} %get-tuple-element.204.act, ...), custom_call_target="tpu_custom_call" | custom-call | flops 10000000000 | bytes 100000000 | tf_op jit(solution)/shard_map/mlp_down_y/pallas_call | solution.py:509
  44.5 2.5 %mlp_down_yc.1 = (bf16[512,512]{1,0:T(8,128)(2,1)S(1)}, f32[1024,512]{1,0:T(8,128)S(1)}, f32[1024,512]{1,0:T(8,128)S(1)}, f32[8,512]{1,0:T(8,128)S(1)}) custom-call(bf16[1024,512]{1,0:T(8,128)(2,1)S(1)} %get-tuple-element.211.n2, bf16[1024,512]{1,0:T(8,128)(2,1)S(1)} %copy-done.1, bf16[1024,512]{1,0:T(8,128)(2,1)S(1)} %get-tuple-element.212.act, ...), custom_call_target="tpu_custom_call" | custom-call | flops 10000000000 | bytes 100000000 | tf_op jit(solution)/shard_map/mlp_down_yc/pallas_call | solution.py:509
  47.6 3.3 %ln2_bwd.1 = (f32[1024,512]{1,0:T(8,128)S(1)}, bf16[1024,512]{1,0:T(8,128)(2,1)S(1)}, bf16[1024,512]{1,0:T(8,128)(2,1)S(1)}, f32[8,512]{1,0:T(8,128)S(1)}) custom-call(f32[1024,512]{1,0:T(8,128)S(1)} %get-tuple-element.217.hid, f32[1024,512]{1,0:T(8,128)S(1)} %get-tuple-element.218.dn2, bf16[1024,512]{1,0:T(8,128)(2,1)S(1)} %copy-done.2, ...), custom_call_target="tpu_custom_call" | custom-call | flops 10000000000 | bytes 100000000 | tf_op jit(solution)/shard_map/ln2_bwd/pallas_call | solution.py:509
  53.9 1.8 %collective-permute-start.16 = (bf16[256,512]{1,0:T(8,128)(2,1)S(1)}, bf16[256,512]{1,0:T(8,128)(2,1)S(1)}, u32[]{:S(2)}, u32[]{:S(2)}) collective-permute-start(bf16[256,512]{1,0:T(8,128)(2,1)S(1)} %get-tuple-element.226), channel_id=1, source_target_pairs={{0,4},{1,5},{2,6},{3,7},{4,0},{5,1},{6,2},{7,3},{8,12},{9,13},{10,... | collective-permute-start | bytes 786440 | tf_op jit(solution)/shard_map/ppermute | solution.py:490
  55.7 3.2 %attn_core_bwd.1 = (bf16[1024,512]{1,0:T(8,128)(2,1)S(1)}, bf16[1024,512]{1,0:T(8,128)(2,1)S(1)}, bf16[1024,512]{1,0:T(8,128)(2,1)S(1)}) custom-call(bf16[1024,256]{1,0:T(8,128)(2,1)S(1)} %get-tuple-element.165.refs_0_, bf16[1024,256]{1,0:T(8,128)(2,1)S(1)} %get-tuple-element.166.refs_1_, bf16[1024,256]{1,0:T(8,128)(2,1)S(1)} %get-tuple-element.167.refs_2_, ...), custom_call_target="tpu_custom_call" | custom-call | flops 1000000000 | bytes 100000000 | tf_op jit(solution)/shard_map/attn_core_bwd/pallas_call | solution.py:509
  58.9 2.4 %attn_dx.1 = (f32[1024,512]{1,0:T(8,128)S(1)}, f32[8,512]{1,0:T(8,128)S(1)}) custom-call(bf16[1024,512]{1,0:T(8,128)(2,1)S(1)} %copy-done, bf16[1024,512]{1,0:T(8,128)(2,1)S(1)} %get-tuple-element.247.dq, bf16[1024,512]{1,0:T(8,128)(2,1)S(1)} %get-tuple-element.238.dk, bf16[1024,512]{1,0:T(8,128)(2,1)S(1)} %get-tuple-element.239.dv, ...), custom_call_target="tpu_custom_call" | custom-call | flops 1000000000 | bytes 100000000 | tf_op jit(solution)/shard_map/attn_dx/pallas_call | solution.py:509
  62.7 2.9 %collective-permute-done.14.refs_2_ = bf16[512,512]{1,0:T(8,128)(2,1)S(1)} collective-permute-done((bf16[512,512]{1,0:T(8,128)(2,1)S(1)}, bf16[512,512]{1,0:T(8,128)(2,1)S(1)}, u32[]{:S(2)}, u32[]{:S(2)}) %collective-permute-start.14) | collective-permute-done | bytes 524320 | tf_op jit(solution)/shard_map/ppermute | solution.py:490
  76.9 2.7 %collective-permute-start.22 = (bf16[128,512]{1,0:T(8,128)(2,1)S(1)}, bf16[128,512]{1,0:T(8,128)(2,1)S(1)}, u32[]{:S(2)}, u32[]{:S(2)}) collective-permute-start(bf16[128,512]{1,0:T(8,128)(2,1)S(1)} %add_all_d.1.refs_1_), channel_id=1, source_target_pairs={{0,16},{1,17},{2,18},{3,19},{4,20},{5,21},{6,22},{7,23},{8,24},{9,... | collective-permute-start | bytes 393224 | tf_op jit(solution)/shard_map/ppermute | solution.py:490
  83.4 2.6 %collective-permute-start.26 = (bf16[128,512]{1,0:T(8,128)(2,1)S(1)}, bf16[128,512]{1,0:T(8,128)(2,1)S(1)}, u32[]{:S(2)}, u32[]{:S(2)}) collective-permute-start(bf16[128,512]{1,0:T(8,128)(2,1)S(1)} %add_all_u.1.refs_1_), channel_id=1, source_target_pairs={{0,16},{1,17},{2,18},{3,19},{4,20},{5,21},{6,22},{7,23},{8,24},{9,... | collective-permute-start | bytes 393224 | tf_op jit(solution)/shard_map/ppermute | solution.py:490
  89.4 3.0 %collective-permute-done.25.other = bf16[128,512]{1,0:T(8,128)(2,1)S(1)} collective-permute-done((bf16[128,512]{1,0:T(8,128)(2,1)S(1)}, bf16[128,512]{1,0:T(8,128)(2,1)S(1)}, u32[]{:S(2)}, u32[]{:S(2)}) %collective-permute-start.25) | collective-permute-done | bytes 131104 | tf_op jit(solution)/shard_map/ppermute | solution.py:490
  92.9 2.9 %collective-permute-start.29 = (bf16[256,512]{1,0:T(8,128)(2,1)S(1)}, bf16[256,512]{1,0:T(8,128)(2,1)S(1)}, u32[]{:S(2)}, u32[]{:S(2)}) collective-permute-start(bf16[256,512]{1,0:T(8,128)(2,1)S(1)} %join_d.1.refs_1_), channel_id=1, source_target_pairs={{0,4},{1,5},{2,6},{3,7},{4,0},{5,1},{6,2},{7,3},{8,12},{9,13},{10,... | collective-permute-start | bytes 786440 | tf_op jit(solution)/shard_map/ppermute | solution.py:490
  98.4 2.6 %rows_out.1 = (bf16[1024,512]{1,0:T(8,128)(2,1)}, bf16[1024,512]{1,0:T(8,128)(2,1)}) custom-call(bf16[1024,512]{1,0:T(8,128)(2,1)S(1)} %copy-done, f32[1024,512]{1,0:T(8,128)S(1)} %get-tuple-element.280.dh, f32[1024,512]{1,0:T(8,128)S(1)} %get-tuple-element.281.dn1, f32[1024,512]{1,0:T(8,128)S(1)} %get-tuple-element.217.hid, ...), custom_call_target="tpu_custom_call" | custom-call | flops 1000000000 | bytes 100000000 | tf_op jit(solution)/shard_map/rows_out/pallas_call | solution.py:509
  103.2 1.7 %final_down.1 = f32[512,512]{1,0:T(8,128)} custom-call(s32[4]{0:T(128)S(1)} %pad_add_fusion.refs_0_.scal, bf16[256,512]{1,0:T(8,128)(2,1)S(1)} %join_d.1.refs_1_, bf16[256,512]{1,0:T(8,128)(2,1)S(1)} %collective-permute-done.29.refs_2_), custom_call_target="tpu_custom_call" | custom-call | flops 10000000000 | bytes 100000000 | tf_op jit(solution)/shard_map/final_down/pallas_call | solution.py:509
  107.3 1.7 %collective-permute-start.32 = (bf16[128,512]{1,0:T(8,128)(2,1)S(1)}, bf16[128,512]{1,0:T(8,128)(2,1)S(1)}, u32[]{:S(2)}, u32[]{:S(2)}) collective-permute-start(bf16[128,512]{1,0:T(8,128)(2,1)S(1)} %get-tuple-element.291.refs_0_), channel_id=1, source_target_pairs={{0,8},{1,9},{2,10},{3,11},{4,12},{5,13},{6,14},{7,15},{8,0},{9,1},... | collective-permute-start | bytes 393224 | tf_op jit(solution)/shard_map/ppermute | solution.py:490
  (94 shorter events, 44.9 us)
Async XLA Ops:
  2.1 16.1 %collective-permute-start.1 = (bf16[528,512]{1,0:T(8,128)(2,1)S(1)}, bf16[528,512]{1,0:T(8,128)(2,1)S(1)}, u32[]{:S(2)}, u32[]{:S(2)}) collective-permute-start(bf16[528,512]{1,0:T(8,128)(2,1)S(1)} %get-tuple-element.164.refs_4_.wa.refs_0_), channel_id=1, source_target_pairs={{0,2},{1,3},{2,0},{3,1},{4,6},{5,7},{6,4},{7,5},{8,10},{9,11},{10,... | collective-permute-start | bytes 1622024 | tf_op jit(solution)/shard_map/ppermute | solution.py:490
  5.9 23.7 %collective-permute-start.5 = (bf16[512,512]{1,0:T(8,128)(2,1)}, bf16[512,512]{1,0:T(8,128)(2,1)}, u32[]{:S(2)}, u32[]{:S(2)}) collective-permute-start(bf16[512,512]{1,0:T(8,128)(2,1)} %refs_7_.3), channel_id=1, source_target_pairs={{0,2},{1,3},{2,0},{3,1},{4,6},{5,7},{6,4},{7,5},{8,10},{9,11},{10,... | collective-permute-start | bytes 1572872 | tf_op jit(solution)/shard_map/ppermute | solution.py:490
  6.1 34.9 %collective-permute-start.9 = (bf16[512,512]{1,0:T(8,128)(2,1)}, bf16[512,512]{1,0:T(8,128)(2,1)}, u32[]{:S(2)}, u32[]{:S(2)}) collective-permute-start(bf16[512,512]{1,0:T(8,128)(2,1)} %refs_8_.3), channel_id=1, source_target_pairs={{0,2},{1,3},{2,0},{3,1},{4,6},{5,7},{6,4},{7,5},{8,10},{9,11},{10,... | collective-permute-start | bytes 1572872 | tf_op jit(solution)/shard_map/ppermute | solution.py:490
  20.8 8.7 %collective-permute-start.3 = (bf16[512,512]{1,0:T(8,128)(2,1)}, bf16[512,512]{1,0:T(8,128)(2,1)S(1)}, u32[]{:S(2)}, u32[]{:S(2)}) collective-permute-start(bf16[512,512]{1,0:T(8,128)(2,1)} %refs_7_.3), channel_id=1, source_target_pairs={{0,1},{1,0},{2,3},{3,2},{4,5},{5,4},{6,7},{7,6},{8,9},{9,8},{10,11... | collective-permute-start | bytes 1572872 | tf_op jit(solution)/shard_map/ppermute | solution.py:490
  21.4 8.2 %collective-permute-start.4 = (bf16[512,512]{1,0:T(8,128)(2,1)}, bf16[512,512]{1,0:T(8,128)(2,1)S(1)}, u32[]{:S(2)}, u32[]{:S(2)}) collective-permute-start(bf16[512,512]{1,0:T(8,128)(2,1)} %refs_8_.3), channel_id=1, source_target_pairs={{0,1},{1,0},{2,3},{3,2},{4,5},{5,4},{6,7},{7,6},{8,9},{9,8},{10,11... | collective-permute-start | bytes 1572872 | tf_op jit(solution)/shard_map/ppermute | solution.py:490
  34.1 16.8 %collective-permute-start.11 = (bf16[512,512]{1,0:T(8,128)(2,1)S(1)}, bf16[512,512]{1,0:T(8,128)(2,1)S(1)}, u32[]{:S(2)}, u32[]{:S(2)}) collective-permute-start(bf16[512,512]{1,0:T(8,128)(2,1)S(1)} %get-tuple-element.221), channel_id=1, source_target_pairs={{0,1},{1,0},{2,3},{3,2},{4,5},{5,4},{6,7},{7,6},{8,9},{9,8},{10,11... | collective-permute-start | bytes 1572872 | tf_op jit(solution)/shard_map/ppermute | solution.py:490
  38.9 14.4 %collective-permute-start.13 = (bf16[512,512]{1,0:T(8,128)(2,1)S(1)}, bf16[512,512]{1,0:T(8,128)(2,1)S(1)}, u32[]{:S(2)}, u32[]{:S(2)}) collective-permute-start(bf16[512,512]{1,0:T(8,128)(2,1)S(1)} %get-tuple-element.202), channel_id=1, source_target_pairs={{0,2},{1,3},{2,0},{3,1},{4,6},{5,7},{6,4},{7,5},{8,10},{9,11},{10,... | collective-permute-start | bytes 1572872 | tf_op jit(solution)/shard_map/ppermute | solution.py:490
  51.7 13.9 %collective-permute-start.14 = (bf16[512,512]{1,0:T(8,128)(2,1)S(1)}, bf16[512,512]{1,0:T(8,128)(2,1)S(1)}, u32[]{:S(2)}, u32[]{:S(2)}) collective-permute-start(bf16[512,512]{1,0:T(8,128)(2,1)S(1)} %get-tuple-element.224), channel_id=1, source_target_pairs={{0,2},{1,3},{2,0},{3,1},{4,6},{5,7},{6,4},{7,5},{8,10},{9,11},{10,... | collective-permute-start | bytes 1572872 | tf_op jit(solution)/shard_map/ppermute | solution.py:490
  53.9 15.2 %collective-permute-start.16 = (bf16[256,512]{1,0:T(8,128)(2,1)S(1)}, bf16[256,512]{1,0:T(8,128)(2,1)S(1)}, u32[]{:S(2)}, u32[]{:S(2)}) collective-permute-start(bf16[256,512]{1,0:T(8,128)(2,1)S(1)} %get-tuple-element.226), channel_id=1, source_target_pairs={{0,4},{1,5},{2,6},{3,7},{4,0},{5,1},{6,2},{7,3},{8,12},{9,13},{10,... | collective-permute-start | bytes 786440 | tf_op jit(solution)/shard_map/ppermute | solution.py:490
  62.6 8.8 %collective-permute-start.15 = (bf16[1056,512]{1,0:T(8,128)(2,1)S(1)}, bf16[1056,512]{1,0:T(8,128)(2,1)S(1)}, u32[]{:S(2)}, u32[]{:S(2)}) collective-permute-start(bf16[1056,512]{1,0:T(8,128)(2,1)S(1)} %attn_dw_sent.1), channel_id=1, source_target_pairs={{0,1},{1,0},{2,3},{3,2},{4,5},{5,4},{6,7},{7,6},{8,9},{9,8},{10,11... | collective-permute-start | bytes 3244040 | tf_op jit(solution)/shard_map/ppermute | solution.py:490
  66.3 7.9 %collective-permute-start.17 = (bf16[256,512]{1,0:T(8,128)(2,1)S(1)}, bf16[256,512]{1,0:T(8,128)(2,1)S(1)}, u32[]{:S(2)}, u32[]{:S(2)}) collective-permute-start(bf16[256,512]{1,0:T(8,128)(2,1)S(1)} %get-tuple-element.246), channel_id=1, source_target_pairs={{0,4},{1,5},{2,6},{3,7},{4,0},{5,1},{6,2},{7,3},{8,12},{9,13},{10,... | collective-permute-start | bytes 786440 | tf_op jit(solution)/shard_map/ppermute | solution.py:490
  69.8 6.5 %collective-permute-start.18 = (bf16[128,512]{1,0:T(8,128)(2,1)S(1)}, bf16[128,512]{1,0:T(8,128)(2,1)S(1)}, u32[]{:S(2)}, u32[]{:S(2)}) collective-permute-start(bf16[128,512]{1,0:T(8,128)(2,1)S(1)} %get-tuple-element.252), channel_id=1, source_target_pairs={{0,8},{1,9},{2,10},{3,11},{4,12},{5,13},{6,14},{7,15},{8,0},{9,1},... | collective-permute-start | bytes 393224 | tf_op jit(solution)/shard_map/ppermute | solution.py:490
  72.1 8.1 %collective-permute-start.19 = (bf16[272,512]{1,0:T(8,128)(2,1)S(1)}, bf16[272,512]{1,0:T(8,128)(2,1)S(1)}, u32[]{:S(2)}, u32[]{:S(2)}) collective-permute-start(bf16[272,512]{1,0:T(8,128)(2,1)S(1)} %get-tuple-element.258), channel_id=1, source_target_pairs={{0,2},{1,3},{2,0},{3,1},{4,6},{5,7},{6,4},{7,5},{8,10},{9,11},{10,... | collective-permute-start | bytes 835592 | tf_op jit(solution)/shard_map/ppermute | solution.py:490
  73.5 6.6 %collective-permute-start.20 = (bf16[256,512]{1,0:T(8,128)(2,1)S(1)}, bf16[256,512]{1,0:T(8,128)(2,1)S(1)}, u32[]{:S(2)}, u32[]{:S(2)}) collective-permute-start(bf16[256,512]{1,0:T(8,128)(2,1)S(1)} %get-tuple-element.260), channel_id=1, source_target_pairs={{0,4},{1,5},{2,6},{3,7},{4,0},{5,1},{6,2},{7,3},{8,12},{9,13},{10,... | collective-permute-start | bytes 786440 | tf_op jit(solution)/shard_map/ppermute | solution.py:490
  74.8 8.1 %collective-permute-start.21 = (bf16[128,512]{1,0:T(8,128)(2,1)S(1)}, bf16[128,512]{1,0:T(8,128)(2,1)S(1)}, u32[]{:S(2)}, u32[]{:S(2)}) collective-permute-start(bf16[128,512]{1,0:T(8,128)(2,1)S(1)} %get-tuple-element.262), channel_id=1, source_target_pairs={{0,8},{1,9},{2,10},{3,11},{4,12},{5,13},{6,14},{7,15},{8,0},{9,1},... | collective-permute-start | bytes 393224 | tf_op jit(solution)/shard_map/ppermute | solution.py:490
  76.9 9.1 %collective-permute-start.22 = (bf16[128,512]{1,0:T(8,128)(2,1)S(1)}, bf16[128,512]{1,0:T(8,128)(2,1)S(1)}, u32[]{:S(2)}, u32[]{:S(2)}) collective-permute-start(bf16[128,512]{1,0:T(8,128)(2,1)S(1)} %add_all_d.1.refs_1_), channel_id=1, source_target_pairs={{0,16},{1,17},{2,18},{3,19},{4,20},{5,21},{6,22},{7,23},{8,24},{9,... | collective-permute-start | bytes 393224 | tf_op jit(solution)/shard_map/ppermute | solution.py:490
  80.8 7.0 %collective-permute-start.24 = (bf16[128,512]{1,0:T(8,128)(2,1)S(1)}, bf16[128,512]{1,0:T(8,128)(2,1)S(1)}, u32[]{:S(2)}, u32[]{:S(2)}) collective-permute-start(bf16[128,512]{1,0:T(8,128)(2,1)S(1)} %get-tuple-element.268), channel_id=1, source_target_pairs={{0,2},{1,3},{2,0},{3,1},{4,6},{5,7},{6,4},{7,5},{8,10},{9,11},{10,... | collective-permute-start | bytes 393224 | tf_op jit(solution)/shard_map/ppermute | solution.py:490
  83.4 12.3 %collective-permute-start.26 = (bf16[128,512]{1,0:T(8,128)(2,1)S(1)}, bf16[128,512]{1,0:T(8,128)(2,1)S(1)}, u32[]{:S(2)}, u32[]{:S(2)}) collective-permute-start(bf16[128,512]{1,0:T(8,128)(2,1)S(1)} %add_all_u.1.refs_1_), channel_id=1, source_target_pairs={{0,16},{1,17},{2,18},{3,19},{4,20},{5,21},{6,22},{7,23},{8,24},{9,... | collective-permute-start | bytes 393224 | tf_op jit(solution)/shard_map/ppermute | solution.py:490
  88.4 8.0 %collective-permute-start.27 = (bf16[144,512]{1,0:T(8,128)(2,1)S(1)}, bf16[144,512]{1,0:T(8,128)(2,1)S(1)}, u32[]{:S(2)}, u32[]{:S(2)}) collective-permute-start(bf16[144,512]{1,0:T(8,128)(2,1)S(1)} %get-tuple-element.275), channel_id=1, source_target_pairs={{0,8},{1,9},{2,10},{3,11},{4,12},{5,13},{6,14},{7,15},{8,0},{9,1},... | collective-permute-start | bytes 442376 | tf_op jit(solution)/shard_map/ppermute | solution.py:490
  92.9 10.3 %collective-permute-start.29 = (bf16[256,512]{1,0:T(8,128)(2,1)S(1)}, bf16[256,512]{1,0:T(8,128)(2,1)S(1)}, u32[]{:S(2)}, u32[]{:S(2)}) collective-permute-start(bf16[256,512]{1,0:T(8,128)(2,1)S(1)} %join_d.1.refs_1_), channel_id=1, source_target_pairs={{0,4},{1,5},{2,6},{3,7},{4,0},{5,1},{6,2},{7,3},{8,12},{9,13},{10,... | collective-permute-start | bytes 786440 | tf_op jit(solution)/shard_map/ppermute | solution.py:490
  97.0 7.9 %collective-permute-start.30 = (bf16[144,512]{1,0:T(8,128)(2,1)S(1)}, bf16[144,512]{1,0:T(8,128)(2,1)S(1)}, u32[]{:S(2)}, u32[]{:S(2)}) collective-permute-start(bf16[144,512]{1,0:T(8,128)(2,1)S(1)} %add_all_a.1.refs_1_), channel_id=1, source_target_pairs={{0,16},{1,17},{2,18},{3,19},{4,20},{5,21},{6,22},{7,23},{8,24},{9,... | collective-permute-start | bytes 442376 | tf_op jit(solution)/shard_map/ppermute | solution.py:490
  101.9 7.8 %collective-permute-start.31 = (bf16[256,512]{1,0:T(8,128)(2,1)S(1)}, bf16[256,512]{1,0:T(8,128)(2,1)S(1)}, u32[]{:S(2)}, u32[]{:S(2)}) collective-permute-start(bf16[256,512]{1,0:T(8,128)(2,1)S(1)} %join_u.1.refs_1_), channel_id=1, source_target_pairs={{0,4},{1,5},{2,6},{3,7},{4,0},{5,1},{6,2},{7,3},{8,12},{9,13},{10,... | collective-permute-start | bytes 786440 | tf_op jit(solution)/shard_map/ppermute | solution.py:490
  105.5 6.0 %collective-permute-start.34 = (bf16[128,512]{1,0:T(8,128)(2,1)S(1)}, bf16[128,512]{1,0:T(8,128)(2,1)S(1)}, u32[]{:S(2)}, u32[]{:S(2)}) collective-permute-start(bf16[128,512]{1,0:T(8,128)(2,1)S(1)} %get-tuple-element.291.refs_0_), channel_id=1, source_target_pairs={{0,12},{1,13},{2,14},{3,15},{4,8},{5,9},{6,10},{7,11},{8,4},{9,5},... | collective-permute-start | bytes 393224 | tf_op jit(solution)/shard_map/ppermute | solution.py:490
  106.2 6.4 %collective-permute-start.33 = (bf16[128,512]{1,0:T(8,128)(2,1)S(1)}, bf16[128,512]{1,0:T(8,128)(2,1)S(1)}, u32[]{:S(2)}, u32[]{:S(2)}) collective-permute-start(bf16[128,512]{1,0:T(8,128)(2,1)S(1)} %get-tuple-element.291.refs_0_), channel_id=1, source_target_pairs={{0,4},{1,5},{2,6},{3,7},{4,0},{5,1},{6,2},{7,3},{8,12},{9,13},{10,... | collective-permute-start | bytes 393224 | tf_op jit(solution)/shard_map/ppermute | solution.py:490
  (15 other events, 58.3 us)
